TPU v7x, 256 devices: a whole 4x4x8 slice. The times are simulated.
256 devices in a mesh: context: 32 (over y, x, core), head: 8 (over z).
Axes of the slice: x: 4, y: 4, z: 8, core: 2. Of those that a mesh axis runs over, the one named last changes fastest.
Arguments:
- queries: bfloat16 [4096, 64, 128], P('context', 'head'), may hold values from -200 to 200
- keys: bfloat16 [4096, 8, 128], P('context', 'head'), may hold values from -6 to 6
- c_proj: bfloat16 [4096, 64, 128], P('context', 'head'), may hold values from -0.3125 to 0.3125
- b_proj: bfloat16 [4096, 8, 128], P('context', 'head'), may hold values from -0.3125 to 0.3125
- log_decay: float32 [4096, 64], P('context', 'head'), may hold values from -0.6 to 0, as said below
Outputs:
- distill_loss: float32 [], replicated
- grad_c: float32 [4096, 64, 128], P('context', 'head')
- grad_b: float32 [4096, 8, 128], P('context', 'head')
Inputs may be any that keep to these rules, and one draw needn't show every extreme that they name: `log_decay`: negative.
All inputs are finite; a program needn't handle non-finite values.
Results may differ from a plain program's by a relative error of at most 0.00076.
Values may be sent and summed in bfloat16 or wider, within the bound.
No kernel may reach another device: no remote copies, remote signals or barrier semaphores. Data moves between devices by JAX's collectives and lax.ppermute only.
A program may use at most 128 MiB of HBM per device.

v0:
```python
import math

import jax
import jax.numpy as jnp
from jax import lax
from jax.sharding import PartitionSpec as P


def prefix(value, axis, combine, identity):
    peers, here = (lax.axis_size(axis), lax.axis_index(axis))
    everything = lax.all_gather(value, axis)
    start = jnp.broadcast_to(jnp.asarray(identity, value.dtype), value.shape)

    def turn(k, before):
        reached = k < here
        new = combine(before, everything[k])
        return jnp.where(reached, new, before)

    return lax.fori_loop(0, peers, turn, start)


def shards(queries, keys, c_proj, b_proj, log_decay):
    rows_dev, heads_local, head_size = queries.shape
    groups_local = keys.shape[1]
    per_group = heads_local // groups_local
    ctx_devices = lax.axis_size("context")
    seq_len = rows_dev * ctx_devices
    first_row = lax.axis_index("context") * rows_dev
    block_len = min(seq_len, max(rows_dev, 512))
    scale_factor = 1.0 / math.sqrt(head_size)
    local_cum = jnp.cumsum(log_decay, axis=0)
    offset = prefix(
        jnp.sum(log_decay, axis=0),
        "context",
        lambda earlier, later: earlier + later,
        jnp.zeros((heads_local,), jnp.float32),
    )
    row_cum = local_cum + offset[None, :]
    key_cum = lax.all_gather(row_cum, "context", axis=0, tiled=True)
    all_keys, all_b = (
        lax.all_gather(keys, "context", axis=0, tiled=True),
        lax.all_gather(b_proj, "context", axis=0, tiled=True),
    )
    query_four = queries.reshape(rows_dev, groups_local, per_group, head_size)
    c_four = c_proj.reshape(rows_dev, groups_local, per_group, head_size)
    row_cum_four = row_cum.reshape(rows_dev, groups_local, per_group).transpose(1, 2, 0)[..., None]
    key_cum_three = key_cum.reshape(seq_len, groups_local, per_group).transpose(1, 2, 0)
    row_pos = first_row + jnp.arange(rows_dev, dtype=jnp.int32)
    needed = (first_row + rows_dev + block_len - 1) // block_len

    def block_scores(block_start):
        key_block = lax.dynamic_slice_in_dim(all_keys, block_start, block_len, 0)
        scores = (
            jnp.einsum("tghd,sgd->ghts", query_four, key_block, preferred_element_type=jnp.float32)
            * scale_factor
        )
        key_pos = block_start + jnp.arange(block_len, dtype=jnp.int32)
        causal = row_pos[:, None] >= key_pos[None, :]
        return (jnp.where(causal, scores, -jnp.inf), causal)

    def stats_step(block_index, running):
        peak_old, total_old = running
        masked, causal = block_scores(block_index * block_len)
        peak_new = jnp.maximum(peak_old, jnp.max(masked, axis=3))
        exponent = jnp.exp(masked - peak_new[..., None])
        total_new = total_old * jnp.exp(peak_old - peak_new) + jnp.sum(exponent, axis=3)
        return (peak_new, total_new)

    stat_shape = (groups_local, per_group, rows_dev)
    row_peak, row_total = lax.fori_loop(
        0,
        needed,
        stats_step,
        (jnp.full(stat_shape, -jnp.inf, jnp.float32), jnp.zeros(stat_shape, jnp.float32)),
    )

    def grad_step(block_index, running):
        loss_part, grad_part, key_terms = running
        block_start = block_index * block_len
        masked, causal = block_scores(block_start)
        teacher = (
            jnp.where(causal, jnp.exp(masked - row_peak[..., None]), 0.0) / row_total[..., None]
        )
        b_block = lax.dynamic_slice_in_dim(all_b, block_start, block_len, 0)
        block_cum = lax.dynamic_slice_in_dim(key_cum_three, block_start, block_len, 2)[
            :, :, None, :
        ]
        decays = jnp.exp(jnp.where(causal, row_cum_four - block_cum, -jnp.inf))
        student = (
            jnp.einsum("tghd,sgd->ghts", c_four, b_block, preferred_element_type=jnp.float32)
            * decays
        )
        mismatch = student - teacher
        weighted = (2.0 * mismatch * decays).astype(jnp.bfloat16)
        grad_part = grad_part + jnp.einsum(
            "ghts,sgd->tghd", weighted, b_block, preferred_element_type=jnp.float32
        )
        loss_part = loss_part + jnp.sum(mismatch * mismatch)
        block_terms = jnp.einsum(
            "ghts,tghd->sgd", weighted, c_four, preferred_element_type=jnp.float32
        )
        key_terms = lax.dynamic_update_slice_in_dim(key_terms, block_terms, block_start, 0)
        return (loss_part, grad_part, key_terms)

    terms_start = jnp.zeros((seq_len, groups_local, head_size), jnp.float32)
    loss_part, grad_part, key_terms = lax.fori_loop(
        0,
        needed,
        grad_step,
        (
            jnp.zeros((), jnp.float32),
            jnp.zeros((rows_dev, groups_local, per_group, head_size), jnp.float32),
            terms_start,
        ),
    )
    grad_c = grad_part.reshape(rows_dev, heads_local, head_size)
    grad_b = lax.psum_scatter(key_terms, "context", scatter_dimension=0, tiled=True)
    heads_total = heads_local * lax.axis_size("head")
    distill_loss = lax.psum(loss_part, ("context", "head")) / (heads_total * seq_len)
    return (distill_loss, grad_c, grad_b)


def solution(mesh):
    in_specs = (
        P("context", "head", None),
        P("context", "head", None),
        P("context", "head", None),
        P("context", "head", None),
        P("context", "head"),
    )
    out_specs = (P(), P("context", "head", None), P("context", "head", None))
    return jax.shard_map(shards, mesh=mesh, in_specs=in_specs, out_specs=out_specs, check_vma=False)
```

profile of v0, /device:TPU:1, one launch (start us, length us, event | category | flops | bytes accessed | tf_op | source)
XLA Modules:
  0.0 294.5 jit_solution(9389664560101105908)
XLA Ops:
  7.2 0.0 all-gather.6.cloned.1.call-start
  7.2 0.7 all-gather.6.cloned.1.call-update
  7.9 0.0 all-gather.4.cloned.1.call-start
  7.9 0.7 all-gather.4.cloned.1.call-update
  8.6 0.0 reduce-scatter.2.cloned.1.call-start
  8.7 0.8 copy.20
  9.5 0.8 reduce_sum.29
  10.3 1.3 dynamic-slice
  12.2 0.2 dynamic-update-slice
  12.5 65.3 %all-reduce = f32[256]{0:T(256)S(1)} all-reduce(f32[256]{0:T(256)S(1)} %dynamic-update-slice), channel_id=2, replica_groups=mesh['context'=32,'head'=8] {'context'}, use_global_device_ids=true, to_apply=%add | all-reduce | flops 256 | bytes 2048
  77.8 0.1 reshape.118
  77.9 1.3 while.44
  79.2 0.2 reduce_window_sum.13
  79.4 27.1 %all_gather.18 = f32[4096,8]{1,0:T(8,128)S(1)} all-gather(f32[128,8]{1,0:T(8,128)S(1)} %broadcast_add_fusion), channel_id=1, replica_groups=mesh['context'=32,'head'=8] {'context'}, dimensions={0}, use_global_device_ids=true | all-gather | bytes 135168 | tf_op jit(solution)/shard_map/all_gather | solution.py:39
  106.6 0.6 copy.23
  107.1 0.1 copy_bitcast_fusion
  107.3 2.0 while.42
  107.4 0.1 broadcast_compare_fusion.4
  107.5 1.4 fusion.44
  108.9 0.4 exponential_reduce_fusion.2
  109.4 3.2 %all-gather.4.cloned.1.call-done = bf16[4096,1,128]{2,0,1:T(8,128)(2,1)} async-done(((bf16[128,1,128]{2,0,1:T(8,128)(2,1)}), bf16[4096,1,128]{2,0,1:T(8,128)(2,1)}) %all-gather.4.cloned.1.call-update) | async-done | bytes 1048592 | tf_op jit(solution)/shard_map/all_gather | solution.py:42
  112.6 0.1 broadcast_in_dim.45
  112.8 9.5 %while.43 = (s32[]{:T(128)}, f32[]{:T(128)}, f32[128,1,8,128]{0,3,2,1:T(8,128)S(1)}, f32[4096,1,128]{2,0,1:T(8,128)S(1)}, s32[]{:T(128)}, /*index=5*/bf16[4096,1...) while((s32[]{:T(128)}, f32[]{:T(128)}, ...), condition=%wide.region_10.11_spmd.clone, body=%wide.region_8.10_spmd.clone.sunk | while | flops 548078208 | bytes 21734684 | solution.py:106
  112.8 0.1 broadcast_compare_fusion.5
  113.0 1.3 fusion.51
  114.3 4.0 %multiply_reduce_fusion.2 = (f32[]{:T(128)}, f32[1,8,128,512]{2,3,1,0:T(8,128)}) fusion(f32[8,128]{1,0:T(8,128)S(1)} %bitcast.162, f32[8,128]{1,0:T(8,128)S(1)} %bitcast.161, bf16[128,1,8,128]{3,0,2,1:T(8,128)(2,1)S(1)} %get-tuple-element.611, bf16[4096,1,128]{2,0,1:T(8,128)(2,1)} %get-tuple-element.610, s32[]{:T(128)S(6)} %select_n.110, ...), kind=kOutput, calls=%fused_computation.23.clone.1 | convolution fusion | flops 139984896 | bytes 4681736 | tf_op jit(solution)/shard_map/while/body/tghd,sgd->ghts/dot_general | solution.py:54
  118.9 2.5 fusion.52
  121.5 0.8 fusion.53
  122.3 1.3 copy-done
  123.7 156.6 %psum.7 = f32[]{:T(128)} all-reduce(f32[]{:T(128)} %get-tuple-element.199), channel_id=1, replica_groups=mesh['context'=32,'head'=8] {'context','head'}, use_global_device_ids=true, to_apply=%region_11.12 | all-reduce | flops 1 | bytes 8 | tf_op jit(solution)/shard_map/psum | solution.py:119
  280.3 1.0 copy.24
  281.9 4.9 %reduce-scatter.2.cloned.1.call-done = f32[128,1,128]{2,1,0:T(1,128)} async-done(((f32[4096,1,128]{2,1,0:T(1,128)}), f32[128,1,128]{2,1,0:T(1,128)}) %reduce-scatter.2.cloned.1.call-update) | async-done | bytes 65552 | tf_op jit(solution)/shard_map/reduce_scatter | solution.py:117
  (57 shorter events, 0.8 us)
Async XLA Ops:
  7.2 100.1 %all-gather.6.cloned.1.call-start = ((), (), s32[]{:S(2)}) async-start(), calls=%async_computation.2 | async-start | bytes 1081344 | tf_op jit(solution)/shard_map/all_gather | solution.py:41
  7.9 104.7 %all-gather.4.cloned.1.call-start = ((), (), s32[]{:S(2)}) async-start(), calls=%async_computation.1 | async-start | bytes 1081344 | tf_op jit(solution)/shard_map/all_gather | solution.py:42
  8.6 278.2 %reduce-scatter.2.cloned.1.call-start = ((), (), s32[]{:S(2)}) async-start(), calls=%async_computation.3 | async-start | bytes 2162688 | tf_op jit(solution)/shard_map/reduce_scatter | solution.py:117
  79.4 27.7 %copy-start.1 = (bf16[128,8,128]{2,1,0:T(8,128)(2,1)S(1)}, bf16[128,8,128]{2,1,0:T(8,128)(2,1)}, u32[]{:S(2)}) copy-start(bf16[128,8,128]{2,1,0:T(8,128)(2,1)} %param.11) | copy-start | bytes 786436
  79.4 27.7 %copy-start.2 = (bf16[128,8,128]{2,1,0:T(8,128)(2,1)S(1)}, bf16[128,8,128]{2,1,0:T(8,128)(2,1)}, u32[]{:S(2)}) copy-start(bf16[128,8,128]{2,1,0:T(8,128)(2,1)} %param.13) | copy-start | bytes 786436
  118.9 2.6 copy-start.3
  122.3 1.4 copy-start
Sparse Core Ops, SparseCore 0:
  10.6 52.0 all-gather.5
  65.2 47.3 all-gather.3
  123.8 162.9 reduce-scatter.1
where the time goes:
time: 296 us; the launch traced here: 294 us
  blocking collectives  249 us (84%)
  between operations  16.3 us (6%)
  matrix products  10 us (3%)
  waiting for transfers between devices  9.56 us (3%)
  local copies, waits for them, and re-layouts  5.66 us (2%)
    psum x1, blocking collectives, shards(): lax.psum(loss_part, ('context', 'head')) / (heads_total * seq_len)  157 us
    unnamed x1, blocking collectives  65.3 us
    all_gather x1, blocking collectives, shards(): key_cum = lax.all_gather(row_cum, 'context', axis=0, tiled=True)  27.1 us
  transfers between devices with their start and end apart: 3, of which 2 were waited for; matrix products, arithmetic and copies ran while one was open for 3% of the time, Pallas kernels for 0%

commit v1 on v0

v1 whole, which is shorter than its diff:
```python
import functools
import math

import jax
import jax.numpy as jnp
from jax import lax
from jax.experimental import pallas as pl
from jax.experimental.pallas import tpu as pltpu
from jax.sharding import PartitionSpec as P

NEG = -1e30
LOG2E = math.log2(math.e)
VMEM = 56 * 1024 * 1024


def dot(a, b):
    return jnp.dot(a, b, preferred_element_type=jnp.float32)


def dot_nt(a, b):
    return lax.dot_general(a, b, (((1,), (1,)), ((), ())), preferred_element_type=jnp.float32)


def pieces(x):
    high = x.astype(jnp.bfloat16)
    rest = x - high.astype(jnp.float32)
    mid = rest.astype(jnp.bfloat16)
    return high, mid, (rest - mid.astype(jnp.float32)).astype(jnp.bfloat16)


def block_kernel(keys, b_rows, log_decay, out, decay_rows):
    fill = jnp.zeros((128, 128 - log_decay.shape[1]), jnp.float32)
    wide = jnp.concatenate([log_decay[...], fill], axis=1)
    for i, part in enumerate(pieces(wide)):
        decay_rows[i] = part
    high, mid, low = pieces(wide.T[0:8])
    down = jnp.concatenate([high, mid, low, jnp.zeros((8, 128), jnp.bfloat16)], axis=0)
    for k in range(out.shape[0]):
        out[k, 0:128] = keys[...]
        out[k, 128:256] = b_rows[...]
        out[k, 256:288] = down


def final_kernel(back, grad_b, lost):
    total = back[0]
    for k in range(1, back.shape[0]):
        total = total + back[k]
    grad_b[...] = 2.0 * total[0:128].T
    for k in range(lost.shape[0]):
        lost[k] = total[128:136]


def pair_of(got, p, first):
    return jnp.concatenate([got[2 * p, first : first + 128], got[2 * p + 1, first : first + 128]], axis=0)


def position(core, row):
    return (row + core * 128) % 256


def causal_mask(place, p, rows):
    chip, core = place[0], place[1]
    row = position(core, lax.broadcasted_iota(jnp.int32, (rows, 256), 0)) + chip * 256
    lane = lax.broadcasted_iota(jnp.int32, (rows, 256), 1)
    key = (2 * p + lane // 128) * 256 + core * 128 + lane % 128
    return row >= key


def stats_kernel(heads, scale2, place, got, own_q, other_q, out, peak, total):
    chip = place[0]
    rows = 2 * own_q.shape[1]
    peak[...] = jnp.full_like(peak, NEG)
    total[...] = jnp.zeros_like(total)

    def step(p, masked):
        keys = pair_of(got, p, 0)
        causal = causal_mask(place, p, rows) if masked else None
        for h in range(heads):
            s = dot_nt(jnp.concatenate([own_q[h], other_q[h]], axis=0), keys)
            if masked:
                s = jnp.where(causal, s, NEG)
            a, b = s[:, :128], s[:, 128:]
            old = peak[h]
            new = jnp.maximum(old, jnp.maximum(a, b))
            total[h] = (
                total[h] * jnp.exp2((old - new) * scale2)
                + jnp.exp2((a - new) * scale2)
                + jnp.exp2((b - new) * scale2)
            )
            peak[h] = new

    full = chip // 2

    @pl.loop(0, full)
    def _(p):
        step(p, False)

    step(full, True)
    lane = lax.broadcasted_iota(jnp.int32, (rows, 128), 1)
    result = jnp.zeros((rows, 128), jnp.float32)
    for h in range(heads):
        top = jnp.max(peak[h], axis=1, keepdims=True)
        summed = jnp.sum(total[h] * jnp.exp2((peak[h] - top) * scale2), axis=1, keepdims=True)
        result = jnp.where(lane == h, top, result)
        result = jnp.where(lane == heads + h, summed, result)
    out[:rows] = result
    blocks = got.shape[0]
    ones = jnp.ones((128, 128), jnp.bfloat16)
    for k in range(blocks):
        sums = dot(got[k, 256:288], ones)
        sums = sums[0:8] + sums[8:16] + sums[16:24]
        out[rows + 8 * k : rows + 8 * k + 8] = sums


def grad_kernel(heads, scale2, place, got, own_q, other_q, own_c, other_c, own_t, other_t, own_s, other_s, own_d, other_d,
                own_grad, other_grad, grad_b, loss, peak, inverse, fade, key_fade):
    chip, core = place[0], place[1]
    rows = 2 * own_q.shape[1]
    half = own_q.shape[1]
    blocks = got.shape[0]
    mine = own_s[:rows]
    theirs = jnp.concatenate([other_s[half:rows], other_s[:half]], axis=0)
    for h in range(heads):
        a, b = mine[:, h : h + 1], theirs[:, h : h + 1]
        top = jnp.maximum(a, b)
        summed = mine[:, heads + h : heads + h + 1] * jnp.exp2((a - top) * scale2) + theirs[
            :, heads + h : heads + h + 1
        ] * jnp.exp2((b - top) * scale2)
        peak[h] = jnp.broadcast_to(top, (rows, 128))
        inverse[h] = jnp.broadcast_to(1.0 / summed, (rows, 128))
    u = lax.broadcasted_iota(jnp.int32, (rows, rows), 0)
    v = lax.broadcasted_iota(jnp.int32, (rows, rows), 1)
    lower = jnp.where(position(core, u) >= position(core, v), 1.0, 0.0).astype(jnp.bfloat16)
    log_rows = jnp.zeros((rows, 128), jnp.float32)
    for i in range(3):
        log_rows = log_rows + dot(lower, jnp.concatenate([own_d[i], other_d[i]], axis=0))
    log_rows = log_rows * LOG2E
    for h in range(heads):
        fade[h] = jnp.broadcast_to(log_rows[:, h : h + 1], (rows, 128))
    u = lax.broadcasted_iota(jnp.int32, (128, 128), 0)
    v = lax.broadcasted_iota(jnp.int32, (128, 128), 1)
    after = jnp.where(u > v, 1.0, 0.0).astype(jnp.bfloat16)
    upto = jnp.where(u <= v, 1.0, 0.0).astype(jnp.bfloat16)
    behind = jnp.zeros((8, 128), jnp.float32)
    for k in range(blocks - 1, -1, -1):
        own_sum, other_sum = (x[rows + 8 * k : rows + 8 * k + 8] for x in (own_s, other_s))
        tail = dot(got[k, 256:288], after)
        tail = tail[0:8] + tail[8:16] + tail[16:24]
        tail = tail + jnp.where(core == 0, other_sum, 0.0) + behind
        head = dot(got[k, 256:288], upto)
        head = head[0:8] + head[8:16] + head[16:24]
        head = head + jnp.where(core == 0, 0.0, other_sum)
        key_fade[k] = jnp.where(chip > k, tail, -head) * LOG2E
        behind = behind + jnp.where(chip > k, own_sum + other_sum, 0.0)

    own_grad[...] = jnp.zeros_like(own_grad)
    other_grad[...] = jnp.zeros_like(other_grad)
    loss[...] = jnp.zeros_like(loss)

    def step(p, masked):
        keys, b_keys = pair_of(got, p, 0), pair_of(got, p, 128)
        causal = causal_mask(place, p, rows) if masked else None
        total_b = jnp.zeros((128, 256), jnp.float32)
        lost = jnp.zeros((8, 128), jnp.float32)
        for h in range(heads):
            s = dot_nt(jnp.concatenate([own_q[h], other_q[h]], axis=0), keys)
            inner = dot_nt(jnp.concatenate([own_c[h], other_c[h]], axis=0), b_keys)
            top = jnp.concatenate([peak[h], peak[h]], axis=1)
            inv = jnp.concatenate([inverse[h], inverse[h]], axis=1)
            teacher = jnp.exp2((s - top) * scale2) * inv
            row_log = jnp.concatenate([fade[h], fade[h]], axis=1)
            key_log = jnp.concatenate([key_fade[2 * p, h : h + 1], key_fade[2 * p + 1, h : h + 1]], axis=1)
            if masked:
                decay = jnp.exp2(jnp.where(causal, row_log + key_log, NEG))
                teacher = jnp.where(causal, teacher, 0.0)
            else:
                decay = jnp.exp2(row_log + key_log)
            mismatch = inner * decay - teacher
            square = mismatch * mismatch
            lost = lost + jnp.sum(square.reshape(rows // 8, 8, 256), axis=0)[:, :128]
            lost = lost + jnp.sum(square.reshape(rows // 8, 8, 256), axis=0)[:, 128:]
            weighted = (mismatch * decay).astype(jnp.bfloat16)
            part = dot(weighted, b_keys)
            own_grad[h] += part[:half]
            other_grad[h] += part[half:]
            total_b = total_b + dot(jnp.concatenate([own_t[h], other_t[h]], axis=1), weighted)
        loss[...] += lost
        grad_b[2 * p] = total_b[:, :128]
        grad_b[2 * p + 1] = total_b[:, 128:]

    full = chip // 2

    @pl.loop(0, full)
    def _(p):
        step(p, False)

    step(full, True)

    @pl.loop(full + 1, blocks // 2)
    def _(p):
        grad_b[2 * p] = jnp.zeros((128, 128), jnp.float32)
        grad_b[2 * p + 1] = jnp.zeros((128, 128), jnp.float32)


def shards(queries, keys, c_proj, b_proj, log_decay):
    rows_dev, heads, size = queries.shape
    peers = lax.axis_size("context")
    chips = peers // 2
    rows = 2 * rows_dev
    here = lax.axis_index("context")
    core = here % 2
    place = jnp.stack([here // 2, core]).astype(jnp.int32)
    scale2 = LOG2E / math.sqrt(size)
    plane = [[2 * k + c for k in range(chips)] for c in range(2)]
    swap = [(i, i ^ 1) for i in range(peers)]

    f32 = functools.partial(jax.ShapeDtypeStruct, dtype=jnp.float32)
    bf16 = functools.partial(jax.ShapeDtypeStruct, dtype=jnp.bfloat16)
    smem = pl.BlockSpec(memory_space=pltpu.SMEM)
    vmem = pl.BlockSpec(memory_space=pltpu.VMEM)
    params = pltpu.CompilerParams(vmem_limit_bytes=VMEM)
    work = heads * rows * chips * 128

    block, own_d = pl.pallas_call(
        block_kernel,
        out_shape=(bf16((chips, 288, 128)), bf16((3, rows_dev, 128))),
        in_specs=[vmem] * 3,
        out_specs=(vmem,) * 2,
        compiler_params=params,
        name="block",
    )(keys[:, 0], b_proj[:, 0], log_decay)
    got = lax.all_to_all(block, "context", 0, 0, axis_index_groups=plane)

    own_q, own_c, own_t = queries.transpose(1, 0, 2), c_proj.transpose(1, 0, 2), c_proj.transpose(1, 2, 0)
    other_q, other_c, other_t, other_d = (lax.ppermute(x, "context", swap) for x in (own_q, own_c, own_t, own_d))

    own_s = pl.pallas_call(
        functools.partial(stats_kernel, heads, scale2),
        out_shape=f32((rows + 8 * chips, 128)),
        in_specs=[smem] + [vmem] * 3,
        out_specs=vmem,
        scratch_shapes=[pltpu.VMEM((heads, rows, 128), jnp.float32)] * 2,
        compiler_params=params,
        cost_estimate=pl.CostEstimate(flops=2 * work * size, bytes_accessed=2 << 20, transcendentals=work),
        name="stats",
    )(place, got, own_q, other_q)
    other_s = lax.ppermute(own_s, "context", swap)

    own_grad, other_grad, grad_b, loss = pl.pallas_call(
        functools.partial(grad_kernel, heads, scale2),
        out_shape=(f32((heads, rows_dev, size)),) * 2 + (f32((chips, size, 128)), f32((8, 128))),
        in_specs=[smem] + [vmem] * 11,
        out_specs=(vmem,) * 4,
        scratch_shapes=[pltpu.VMEM((heads, rows, 128), jnp.float32)] * 3 + [pltpu.VMEM((chips, 8, 128), jnp.float32)],
        compiler_params=params,
        cost_estimate=pl.CostEstimate(flops=8 * work * size, bytes_accessed=6 << 20, transcendentals=2 * work),
        name="grads",
    )(place, got, own_q, other_q, own_c, other_c, own_t, other_t, own_s, other_s, own_d, other_d)

    lost = jnp.broadcast_to(jnp.sum(loss), (chips, 8, 128))
    sent = jnp.concatenate([grad_b, lost], axis=1)
    back = lax.all_to_all(sent, "context", 0, 0, axis_index_groups=plane)
    grad_c = (2.0 * (own_grad + lax.ppermute(other_grad, "context", swap))).transpose(1, 0, 2)
    z_size = lax.axis_size("head")
    mine, lost = pl.pallas_call(
        final_kernel,
        out_shape=(f32((rows_dev, size)), f32((2 * z_size, 8, 128))),
        in_specs=[vmem],
        out_specs=(vmem,) * 2,
        compiler_params=params,
        name="final",
    )(back)

    columns = [[(2 * k + c) * z_size + z for c in range(2) for z in range(z_size)] for k in range(chips)]
    lost = lax.all_to_all(lost, ("context", "head"), 0, 0, axis_index_groups=columns)
    distill_loss = jnp.sum(lost[:, 0, 0]) / (heads * z_size * peers * rows_dev)
    return distill_loss, grad_c, mine[:, None, :]


def solution(mesh):
    in_specs = (
        P("context", "head", None),
        P("context", "head", None),
        P("context", "head", None),
        P("context", "head", None),
        P("context", "head"),
    )
    out_specs = (P(), P("context", "head", None), P("context", "head", None))
    return jax.shard_map(shards, mesh=mesh, in_specs=in_specs, out_specs=out_specs, check_vma=False)
```

time: 296 us -> 111 us (0.38)
  blocking collectives: 249 us -> 0 us
  starting transfers between devices: 0.11 us -> 43.9 us
  waiting for transfers between devices: 9.56 us -> 38.6 us
  between operations: 16.3 us -> 2.55 us
  Pallas kernels: 0 us -> 13.7 us
  matrix products: 10 us -> 0 us
  local copies, waits for them, and re-layouts: 5.66 us -> 9.39 us
    psum x1 -> x0, blocking collectives: 157 us -> none  [shards(): lax.psum(loss_part, ('context', 'head')) / (heads_total * seq_len)]
    unnamed x1 -> x0, blocking collectives: 65.3 us -> none
    all_to_all x0 -> x3, starting transfers between devices: none -> 38.6 us  [the longest x1 20.4 us: shards(): back = lax.all_to_all(sent, 'context', 0, 0, axis_index_groups=plane)]
    all_to_all x0 -> x3, waiting for transfers between devices: none -> 37.3 us  [the longest x1 16.7 us: shards(): back = lax.all_to_all(sent, 'context', 0, 0, axis_index_groups=plane)]
    all_gather x1 -> x0, blocking collectives: 27.1 us -> none  [shards(): key_cum = lax.all_gather(row_cum, 'context', axis=0, tiled=True)]
    pallas_call x0 -> x4, Pallas kernels: none -> 13.7 us  [the longest x1 6.33 us: shards(): pl.pallas_call(functools.partial(grad_kernel, heads, scale2), out_shape=(...]
    dot_general x5 -> x0, matrix products: 10 us -> none  [the longest x2 5.33 us: block_scores(): jnp.einsum('tghd,sgd->ghts', query_four, key_block, preferred_element_typ...]
    ppermute x0 -> x6, starting transfers between devices: none -> 5.26 us  [the longest x1 2.79 us: shards(): other_s = lax.ppermute(own_s, 'context', swap)]
  transfers between devices with their start and end apart: 3 -> 9, of which waited for: 2 -> 4; matrix products, arithmetic and copies ran while one was open for 3% -> 2% of each run, Pallas kernels for 0% -> 5%
where the time goes in v1:
time: 111 us
  starting transfers between devices  43.9 us (40%)
  waiting for transfers between devices  38.6 us (35%)
  Pallas kernels  13.7 us (12%)
  local copies, waits for them, and re-layouts  9.39 us (8%)
  other arithmetic  2.56 us (2%)
  between operations  2.55 us (2%)
    all_to_all x1, starting transfers between devices, shards(): back = lax.all_to_all(sent, 'context', 0, 0, axis_index_groups=plane)  20.4 us
    all_to_all x1, waiting for transfers between devices, shards(): back = lax.all_to_all(sent, 'context', 0, 0, axis_index_groups=plane)  16.7 us
    all_to_all x1, waiting for transfers between devices, shards(): got = lax.all_to_all(block, 'context', 0, 0, axis_index_groups=plane)  14.7 us
    all_to_all x1, starting transfers between devices, shards(): lax.all_to_all(lost, ('context', 'head'), 0, 0, axis_index_groups=columns)  10.6 us
    all_to_all x1, starting transfers between devices, shards(): got = lax.all_to_all(block, 'context', 0, 0, axis_index_groups=plane)  7.72 us
    unnamed x35, local copies, waits for them, and re-layouts  6.42 us
    pallas_call x1, Pallas kernels, shards(): pl.pallas_call(functools.partial(grad_kernel, heads, scale2), out_shape=(...  6.33 us
    all_to_all x1, waiting for transfers between devices, shards(): lax.all_to_all(lost, ('context', 'head'), 0, 0, axis_index_groups=columns)  5.98 us
  transfers between devices with their start and end apart: 9, of which 4 were waited for; matrix products, arithmetic and copies ran while one was open for 2% of the time, Pallas kernels for 5%

profile of v1, /device:TPU:1, one launch (start us, length us, event | category | flops | bytes accessed | tf_op | source)
XLA Modules:
  0.0 110.7 jit_solution(10366125430889947051)
XLA Ops:
  0.6 1.4 %copy.8.log_decay = f32[128,8]{1,0:T(8,128)} copy(f32[128,8]{0,1:T(8,128)} %param.9) | data formatting | bytes 8192 | tf_op args[4]
  2.0 2.1 %block.1 = (bf16[16,288,128]{2,1,0:T(8,128)(2,1)}, bf16[3,128,128]{2,1,0:T(8,128)(2,1)}) custom-call(bf16[128,128]{1,0:T(8,128)(2,1)} %bitcast.23, bf16[128,128]{1,0:T(8,128)(2,1)} %bitcast.24, f32[128,8]{1,0:T(8,128)} %copy.8.log_decay), custom_call_target="tpu_custom_call" | custom-call | tf_op jit(solution)/shard_map/block/pallas_call | solution.py:224
  4.1 7.7 %all-to-all-start = ((bf16[16,288,128]{2,1,0:T(8,128)(2,1)}), bf16[16,288,128]{2,1,0:T(8,128)(2,1)S(1)}, u32[]{:S(2)}, u32[]{:S(2)}) async-start(bf16[16,288,128]{2,1,0:T(8,128)(2,1)} %get-tuple-element.11), calls=%async_computation | async-start | bytes 2359296 | tf_op jit(solution)/shard_map/all_to_all | solution.py:232
  11.9 1.0 collective-permute-start
  13.0 0.1 collective-permute-start.1
  13.1 0.2 copy.11
  13.4 0.6 collective-permute-start.2
  13.9 0.6 pad_add_fusion.place
  14.5 14.7 %all-to-all-done.got = bf16[16,288,128]{2,1,0:T(8,128)(2,1)S(1)} async-done(((bf16[16,288,128]{2,1,0:T(8,128)(2,1)}), bf16[16,288,128]{2,1,0:T(8,128)(2,1)S(1)}, u32[]{:S(2)}, u32[]{:S(2)}) %all-to-all-start) | async-done | bytes 1179680 | tf_op jit(solution)/shard_map/all_to_all | solution.py:232
  29.2 1.0 copy-done.1
  30.3 3.3 %stats.1.own_s = f32[384,128]{1,0:T(8,128)} custom-call(s32[2]{0:T(128)} %pad_add_fusion.place, bf16[16,288,128]{2,1,0:T(8,128)(2,1)} %copy-done.1, bf16[8,128,128]{2,1,0:T(8,128)(2,1)} %bitcast.17, bf16[8,128,128]{2,1,0:T(8,128)(2,1)} %copy-done.9), custom_call_target="tpu_custom_call" | custom-call | flops 1073741824 | bytes 2097152 | tf_op jit(solution)/shard_map/stats/pallas_call | solution.py:237
  33.6 2.8 %collective-permute-start.3 = (f32[384,128]{1,0:T(8,128)}, f32[384,128]{1,0:T(8,128)S(1)}, u32[]{:S(2)}, u32[]{:S(2)}) collective-permute-start(f32[384,128]{1,0:T(8,128)} %stats.1.own_s), channel_id=1, source_target_pairs={{0,8},{8,0},{16,24},{24,16},{32,40},{40,32},{48,56},{56,48},{64,72... | collective-permute-start | bytes 589832 | tf_op jit(solution)/shard_map/ppermute | solution.py:247
  36.4 0.1 collective-permute-start.4
  36.5 1.2 %collective-permute-done.4.other_d = bf16[3,128,128]{2,1,0:T(8,128)(2,1)S(1)} collective-permute-done((bf16[3,128,128]{2,1,0:T(8,128)(2,1)S(1)}, bf16[3,128,128]{2,1,0:T(8,128)(2,1)S(1)}, u32[]{:S(2)}, u32[]{:S(2)}) %collective-permute-start.4) | collective-permute-done | bytes 98336 | tf_op jit(solution)/shard_map/ppermute | solution.py:235
  37.8 0.6 copy-done.14
  38.4 0.1 copy-done.10
  38.5 0.1 copy-done.11
  38.6 0.7 copy-done.12
  39.3 6.3 %grads.1 = (f32[8,128,128]{2,1,0:T(8,128)}, f32[8,128,128]{2,1,0:T(8,128)}, f32[16,128,128]{2,1,0:T(8,128)}, f32[8,128]{1,0:T(8,128)}) custom-call(s32[2]{0:T(128)} %pad_add_fusion.place, bf16[16,288,128]{2,1,0:T(8,128)(2,1)} %copy-done.1, bf16[8,128,128]{2,1,0:T(8,128)(2,1)} %bitcast.18, bf16[8,128,128]{2,1,0:T(8,128)(2,1)} %copy-done.9, ...), custom_call_target="tpu_custom_call" | custom-call | flops 4294967296 | bytes 6291456 | tf_op jit(solution)/shard_map/grads/pallas_call | solution.py:249
  45.6 1.3 %reduce_sum.18 = f32[]{:T(128)} reduce(f32[8,128]{1,0:T(8,128)} %get-tuple-element.14, f32[]{:T(128)} %constant.34.clone.1), dimensions={0,1}, to_apply=%region_0.1 | reduce | flops 1023 | bytes 4104 | tf_op jit(solution)/shard_map/reduce_sum | solution.py:260
  46.9 3.0 %concatenate.3 = f32[16,136,128]{2,1,0:T(8,128)} pad(f32[16,128,128]{2,1,0:T(8,128)} %get-tuple-element.13, f32[]{:T(128)} %reduce_sum.18), padding=0_0x0_8x0_0 | pad | bytes 2162692 | tf_op jit(solution)/shard_map/concatenate | solution.py:261
  49.9 20.4 %all-to-all-start.1 = ((f32[16,136,128]{2,1,0:T(8,128)}), f32[16,136,128]{2,1,0:T(8,128)S(1)}, u32[]{:S(2)}, u32[]{:S(2)}) async-start(f32[16,136,128]{2,1,0:T(8,128)} %concatenate.3), calls=%async_computation.1 | async-start | bytes 2228224 | tf_op jit(solution)/shard_map/all_to_all | solution.py:262
  70.2 0.0 copy-start.3
  70.3 0.6 collective-permute-start.5
  70.9 16.7 %all-to-all-done.1.back = f32[16,136,128]{2,1,0:T(8,128)S(1)} async-done(((f32[16,136,128]{2,1,0:T(8,128)}), f32[16,136,128]{2,1,0:T(8,128)S(1)}, u32[]{:S(2)}, u32[]{:S(2)}) %all-to-all-start.1) | async-done | bytes 1114144 | tf_op jit(solution)/shard_map/all_to_all | solution.py:262
  87.6 1.0 copy-done
  88.6 2.0 %final.1 = (f32[128,128]{1,0:T(8,128)}, f32[16,8,128]{2,1,0:T(8,128)}) custom-call(f32[16,136,128]{2,1,0:T(8,128)} %copy-done), custom_call_target="tpu_custom_call" | custom-call | tf_op jit(solution)/shard_map/final/pallas_call | solution.py:265
  90.6 10.6 %all-to-all-start.2 = ((f32[16,8,128]{2,1,0:T(8,128)}), f32[16,8,128]{2,1,0:T(8,128)S(1)}, u32[]{:S(2)}, u32[]{:S(2)}) async-start(f32[16,8,128]{2,1,0:T(8,128)} %get-tuple-element.15), calls=%async_computation.2 | async-start | bytes 131072 | tf_op jit(solution)/shard_map/all_to_all | solution.py:275
  101.2 0.1 multiply_bitcast_fusion
  101.2 1.1 copy.12
  102.3 6.0 %all-to-all-done.2 = f32[16,8,128]{2,1,0:T(8,128)S(1)} async-done(((f32[16,8,128]{2,1,0:T(8,128)}), f32[16,8,128]{2,1,0:T(8,128)S(1)}, u32[]{:S(2)}, u32[]{:S(2)}) %all-to-all-start.2) | async-done | bytes 65568 | tf_op jit(solution)/shard_map/all_to_all | solution.py:275
  108.3 0.6 slice_reduce_fusion
  (30 shorter events, 0.1 us)
Async XLA Ops:
  4.1 7.7 %copy-start.4 = (bf16[128,8,128]{2,1,0:T(8,128)(2,1)S(1)}, bf16[128,8,128]{2,1,0:T(8,128)(2,1)}, u32[]{:S(2)}) copy-start(bf16[128,8,128]{2,1,0:T(8,128)(2,1)} %param.5) | copy-start | bytes 786436
  4.1 8.8 %copy-start.2 = (bf16[128,8,128]{2,1,0:T(8,128)(2,1)S(1)}, bf16[128,8,128]{2,1,0:T(8,128)(2,1)}, u32[]{:S(2)}) copy-start(bf16[128,8,128]{2,1,0:T(8,128)(2,1)} %param.7) | copy-start | bytes 786436
  4.1 25.1 %all-to-all-start = ((bf16[16,288,128]{2,1,0:T(8,128)(2,1)}), bf16[16,288,128]{2,1,0:T(8,128)(2,1)S(1)}, u32[]{:S(2)}, u32[]{:S(2)}) async-start(bf16[16,288,128]{2,1,0:T(8,128)(2,1)} %get-tuple-element.11), calls=%async_computation | async-start | bytes 2359296 | tf_op jit(solution)/shard_map/all_to_all | solution.py:232
  11.9 17.3 %copy-start.5 = (bf16[128,8,128]{2,0,1:T(8,128)(2,1)}, bf16[128,8,128]{2,0,1:T(8,128)(2,1)S(1)}, u32[]{:S(2)}) copy-start(bf16[128,8,128]{2,0,1:T(8,128)(2,1)S(1)} %copy.17) | copy-start | bytes 786436
  11.9 2.6 %collective-permute-start = (bf16[8,128,128]{2,1,0:T(8,128)(2,1)S(1)}, bf16[8,128,128]{2,1,0:T(8,128)(2,1)S(1)}, u32[]{:S(2)}, u32[]{:S(2)}) collective-permute-start(bf16[8,128,128]{2,1,0:T(8,128)(2,1)S(1)} %bitcast.16), channel_id=1, source_target_pairs={{0,8},{8,0},{16,24},{24,16},{32,40},{40,32},{48,56},{56,48},{64,72... | collective-permute-start | bytes 786440 | tf_op jit(solution)/shard_map/ppermute | solution.py:235
  13.0 20.6 %copy-start.6 = (bf16[128,8,128]{2,0,1:T(8,128)(2,1)}, bf16[128,8,128]{2,0,1:T(8,128)(2,1)S(1)}, u32[]{:S(2)}) copy-start(bf16[128,8,128]{2,0,1:T(8,128)(2,1)S(1)} %copy.16) | copy-start | bytes 786436
  13.0 24.7 %collective-permute-start.1 = (bf16[8,128,128]{2,1,0:T(8,128)(2,1)S(1)}, bf16[8,128,128]{2,1,0:T(8,128)(2,1)S(1)}, u32[]{:S(2)}, u32[]{:S(2)}) collective-permute-start(bf16[8,128,128]{2,1,0:T(8,128)(2,1)S(1)} %bitcast.19), channel_id=1, source_target_pairs={{0,8},{8,0},{16,24},{24,16},{32,40},{40,32},{48,56},{56,48},{64,72... | collective-permute-start | bytes 786440 | tf_op jit(solution)/shard_map/ppermute | solution.py:235
  13.3 20.3 %copy-start.7 = (bf16[128,8,128]{0,2,1:T(8,128)(2,1)}, bf16[128,8,128]{0,2,1:T(8,128)(2,1)S(1)}, u32[]{:S(2)}) copy-start(bf16[128,8,128]{0,2,1:T(8,128)(2,1)S(1)} %copy.11) | copy-start | bytes 786436
  13.4 24.4 %collective-permute-start.2 = (bf16[8,128,128]{2,1,0:T(8,128)(2,1)S(1)}, bf16[8,128,128]{2,1,0:T(8,128)(2,1)S(1)}, u32[]{:S(2)}, u32[]{:S(2)}) collective-permute-start(bf16[8,128,128]{2,1,0:T(8,128)(2,1)S(1)} %bitcast.21), channel_id=1, source_target_pairs={{0,8},{8,0},{16,24},{24,16},{32,40},{40,32},{48,56},{56,48},{64,72... | collective-permute-start | bytes 786440 | tf_op jit(solution)/shard_map/ppermute | solution.py:235
  14.5 21.9 %copy-start.13 = (bf16[3,128,128]{2,1,0:T(8,128)(2,1)S(1)}, bf16[3,128,128]{2,1,0:T(8,128)(2,1)}, u32[]{:S(2)}) copy-start(bf16[3,128,128]{2,1,0:T(8,128)(2,1)} %get-tuple-element.12.own_d) | copy-start | bytes 294916
  14.5 14.7 %copy-start.9 = (bf16[8,128,128]{2,1,0:T(8,128)(2,1)}, bf16[8,128,128]{2,1,0:T(8,128)(2,1)S(1)}, u32[]{:S(2)}) copy-start(bf16[8,128,128]{2,1,0:T(8,128)(2,1)S(1)} %collective-permute-done.other_q) | copy-start | bytes 786436
  29.2 1.0 copy-start.1
  33.6 4.1 %collective-permute-start.3 = (f32[384,128]{1,0:T(8,128)}, f32[384,128]{1,0:T(8,128)S(1)}, u32[]{:S(2)}, u32[]{:S(2)}) collective-permute-start(f32[384,128]{1,0:T(8,128)} %stats.1.own_s), channel_id=1, source_target_pairs={{0,8},{8,0},{16,24},{24,16},{32,40},{40,32},{48,56},{56,48},{64,72... | collective-permute-start | bytes 589832 | tf_op jit(solution)/shard_map/ppermute | solution.py:247
  36.4 1.3 %collective-permute-start.4 = (bf16[3,128,128]{2,1,0:T(8,128)(2,1)S(1)}, bf16[3,128,128]{2,1,0:T(8,128)(2,1)S(1)}, u32[]{:S(2)}, u32[]{:S(2)}) collective-permute-start(bf16[3,128,128]{2,1,0:T(8,128)(2,1)S(1)} %copy-done.13), channel_id=1, source_target_pairs={{0,8},{8,0},{16,24},{24,16},{32,40},{40,32},{48,56},{56,48},{64,72... | collective-permute-start | bytes 294920 | tf_op jit(solution)/shard_map/ppermute | solution.py:235
  37.7 0.7 copy-start.14
  37.7 0.7 copy-start.10
  37.7 0.8 copy-start.11
  38.6 0.7 copy-start.12
  49.9 20.4 %copy-start.8 = (f32[8,128,128]{2,1,0:T(8,128)S(1)}, f32[8,128,128]{2,1,0:T(8,128)}, u32[]{:S(2)}) copy-start(f32[8,128,128]{2,1,0:T(8,128)} %get-tuple-element.17) | copy-start | bytes 1572868
  49.9 37.7 %all-to-all-start.1 = ((f32[16,136,128]{2,1,0:T(8,128)}), f32[16,136,128]{2,1,0:T(8,128)S(1)}, u32[]{:S(2)}, u32[]{:S(2)}) async-start(f32[16,136,128]{2,1,0:T(8,128)} %concatenate.3), calls=%async_computation.1 | async-start | bytes 2228224 | tf_op jit(solution)/shard_map/all_to_all | solution.py:262
  70.2 30.9 %copy-start.3 = (f32[8,128,128]{2,1,0:T(8,128)S(1)}, f32[8,128,128]{2,1,0:T(8,128)}, u32[]{:S(2)}) copy-start(f32[8,128,128]{2,1,0:T(8,128)} %get-tuple-element.16) | copy-start | bytes 1572868
  70.3 30.9 %collective-permute-start.5 = (f32[8,128,128]{2,1,0:T(8,128)S(1)}, f32[8,128,128]{2,1,0:T(8,128)S(1)}, u32[]{:S(2)}, u32[]{:S(2)}) collective-permute-start(f32[8,128,128]{2,1,0:T(8,128)S(1)} %copy-done.8), channel_id=1, source_target_pairs={{0,8},{8,0},{16,24},{24,16},{32,40},{40,32},{48,56},{56,48},{64,72... | collective-permute-start | bytes 1572872 | tf_op jit(solution)/shard_map/ppermute | solution.py:263
  87.6 1.0 copy-start
  90.6 17.7 %all-to-all-start.2 = ((f32[16,8,128]{2,1,0:T(8,128)}), f32[16,8,128]{2,1,0:T(8,128)S(1)}, u32[]{:S(2)}, u32[]{:S(2)}) async-start(f32[16,8,128]{2,1,0:T(8,128)} %get-tuple-element.15), calls=%async_computation.2 | async-start | bytes 131072 | tf_op jit(solution)/shard_map/all_to_all | solution.py:275

commit v2 on v1

v2 whole, which is shorter than its diff:
```python
import functools
import math

import jax
import jax.numpy as jnp
from jax import lax
from jax.experimental import pallas as pl
from jax.experimental.pallas import tpu as pltpu
from jax.sharding import PartitionSpec as P

NEG = -1e30
LOG2E = math.log2(math.e)
TINY = 1e-30
SMALL, STATS, GRADS = 8 << 20, 24 << 20, 32 << 20


def dot(a, b):
    return jnp.dot(a, b, preferred_element_type=jnp.float32)


def dot_nt(a, b):
    return lax.dot_general(a, b, (((1,), (1,)), ((), ())), preferred_element_type=jnp.float32)


def pieces(x):
    high = x.astype(jnp.bfloat16)
    rest = x - high.astype(jnp.float32)
    mid = rest.astype(jnp.bfloat16)
    return high, mid, (rest - mid.astype(jnp.float32)).astype(jnp.bfloat16)


def exponent(x):
    return jnp.floor(jnp.log2(jnp.maximum(x, TINY)))


def position(core, row):
    return (row + core * 128) % 256


def block_kernel(keys, b_rows, log_decay, out):
    high, mid, low = pieces(log_decay[...])
    down = jnp.concatenate([high, mid, low, jnp.zeros((8, 128), jnp.bfloat16)], axis=0)
    key_cols, b_cols = keys[...].T, b_rows[...].T
    for k in range(out.shape[0]):
        out[k, 0:128] = key_cols
        out[k, 128:256] = b_cols
        out[k, 256:288] = down


def stats_kernel(heads, scale2, place, got, own_q, other_q, log_decay, out):
    chip, core = place[0], place[1]
    blocks = got.shape[0]
    half = own_q.shape[1]
    rows = 2 * half
    row = lax.broadcasted_iota(jnp.int32, (rows, 128), 0)
    lane = lax.broadcasted_iota(jnp.int32, (rows, 128), 1)
    gap = position(core, row) - lane - core * 128 + chip * 256
    keys = jnp.concatenate([got[k, 0:128] for k in range(blocks)], axis=1)
    result = jnp.zeros((rows, 128), jnp.float32)
    for h in range(heads):
        s = dot(jnp.concatenate([own_q[h], other_q[h]], axis=0), keys)
        parts = [jnp.where(gap >= 256 * k, s[:, 128 * k : 128 * k + 128], NEG) for k in range(blocks)]
        top = jnp.max(functools.reduce(jnp.maximum, parts), axis=1, keepdims=True)
        summed = jnp.sum(sum(jnp.exp2((x - top) * scale2) for x in parts), axis=1, keepdims=True)
        result = jnp.where(lane == h, top, result)
        result = jnp.where(lane == heads + h, summed, result)
    out[:rows] = result
    ones = jnp.ones((128, 128), jnp.bfloat16)
    for k in range(blocks):
        sums = dot(got[k, 256:288], ones)
        out[rows + 8 * k : rows + 8 * k + 8] = sums[0:8] + sums[8:16] + sums[16:24]
    wide = jnp.concatenate([log_decay[...], jnp.zeros((128 - heads, 128), jnp.float32)], axis=0)
    out[rows + 8 * blocks :] = wide.T


def grad_kernel(heads, scale2, group, place, got, own_q, other_q, own_c, other_c, own_t, other_t, own_s, other_s,
                own_grad, other_grad, sent, peak, fade, log_fade, key_fade, key_log, weighted, loss):
    chip, core = place[0], place[1]
    half = own_s.shape[0] // 4
    rows = 2 * half
    blocks = got.shape[0]
    tiles = 2 * heads
    width = group * 128
    mine = own_s[:rows]
    theirs = jnp.concatenate([other_s[half:rows], other_s[:half]], axis=0)
    u = lax.broadcasted_iota(jnp.int32, (rows, rows), 0)
    v = lax.broadcasted_iota(jnp.int32, (rows, rows), 1)
    lower = jnp.where(position(core, u) >= position(core, v), 1.0, 0.0).astype(jnp.bfloat16)
    log_rows = jnp.zeros((rows, 128), jnp.float32)
    for part in pieces(jnp.concatenate([own_s[rows + 8 * blocks :], other_s[rows + 8 * blocks :]], axis=0)):
        log_rows = log_rows + dot(lower, part)
    log_rows = log_rows * LOG2E
    for h in range(heads):
        a, b = mine[:, h : h + 1], theirs[:, h : h + 1]
        top = jnp.maximum(a, b)
        summed = mine[:, heads + h : heads + h + 1] * jnp.exp2((a - top) * scale2) + theirs[
            :, heads + h : heads + h + 1
        ] * jnp.exp2((b - top) * scale2)
        level = jnp.broadcast_to(top * scale2 + jnp.log2(summed), (rows, 128))
        row_log = jnp.broadcast_to(log_rows[:, h : h + 1], (rows, 128))
        row_fade = jnp.exp2(row_log)
        for t, first in ((h, 0), (heads + h, half)):
            peak[t] = level[first : first + half]
            log_fade[t] = row_log[first : first + half]
            fade[t] = row_fade[first : first + half]
    u = lax.broadcasted_iota(jnp.int32, (128, 128), 0)
    v = lax.broadcasted_iota(jnp.int32, (128, 128), 1)
    after = jnp.where(u > v, 1.0, 0.0).astype(jnp.bfloat16)
    upto = jnp.where(u <= v, 1.0, 0.0).astype(jnp.bfloat16)
    behind = jnp.zeros((8, 128), jnp.float32)
    for k in range(blocks - 1, -1, -1):
        own_sum, other_sum = (x[rows + 8 * k : rows + 8 * k + 8] for x in (own_s, other_s))
        tail = dot(got[k, 256:288], after)
        tail = tail[0:8] + tail[8:16] + tail[16:24]
        tail = tail + jnp.where(core == 0, other_sum, 0.0) + behind
        head = dot(got[k, 256:288], upto)
        head = head[0:8] + head[8:16] + head[16:24]
        head = head + jnp.where(core == 0, 0.0, other_sum)
        logs = jnp.where(chip > k, tail, -head) * LOG2E
        key_log[k] = logs
        key_fade[k] = jnp.exp2(jnp.minimum(logs, 0.0))
        behind = behind + jnp.where(chip > k, own_sum + other_sum, 0.0)

    own_grad[...] = jnp.zeros_like(own_grad)
    other_grad[...] = jnp.zeros_like(other_grad)
    loss[...] = jnp.zeros_like(loss)
    row = lax.broadcasted_iota(jnp.int32, (half, 128), 0)
    lane = lax.broadcasted_iota(jnp.int32, (half, 128), 1)
    gaps = [position(core, row + first) - lane - core * 128 for first in (0, half)]

    def step(p, masked):
        keys = jnp.concatenate([got[group * p + i, 0:128] for i in range(group)], axis=1)
        b_cols = jnp.concatenate([got[group * p + i, 128:256] for i in range(group)], axis=1)
        lost = jnp.zeros((8, 128), jnp.float32)
        for side, (q, c) in enumerate(((own_q, own_c), (other_q, other_c))):
            scores = dot(q[...].reshape(heads * half, 128), keys)
            inner = dot(c[...].reshape(heads * half, 128), b_cols)
            for h in range(heads):
                t = side * heads + h
                at = slice(h * half, h * half + half)
                for i in range(group):
                    to = slice(128 * i, 128 * i + 128)
                    k = group * p + i
                    s = scores[at, to] * scale2
                    if masked:
                        causal = gaps[side] >= (k - chip) * 256
                        teacher = jnp.exp2(jnp.where(causal, s - peak[t], NEG))
                        decay = jnp.exp2(jnp.where(causal, log_fade[t] + key_log[k, h : h + 1], NEG))
                    else:
                        teacher = jnp.exp2(s - peak[t])
                        decay = fade[t] * key_fade[k, h : h + 1]
                    mismatch = inner[at, to] * decay - teacher
                    square = mismatch * mismatch
                    lost = lost + jnp.sum(square.reshape(half // 8, 8, 128), axis=0)
                    weighted[t * half : t * half + half, to] = (mismatch * decay).astype(jnp.bfloat16)
        loss[...] += lost
        parts = dot_nt(b_cols, weighted[...])
        own_grad[...] += parts[:, : heads * half]
        other_grad[...] += parts[:, heads * half :]
        parts = dot(own_t[...], weighted[: heads * half]) + dot(other_t[...], weighted[heads * half :])
        for i in range(group):
            sent[group * p + i, 0:128] = parts[:, 128 * i : 128 * i + 128]

    full = chip // group

    @pl.loop(0, full)
    def _(p):
        step(p, False)

    step(full, True)

    @pl.loop(group * (full + 1), blocks)
    def _(k):
        sent[k, 0:128] = jnp.zeros((128, 128), jnp.float32)

    top = functools.reduce(jnp.maximum, [jnp.abs(sent[k, 0:128]) for k in range(blocks)])
    power = exponent(jnp.broadcast_to(jnp.max(top, keepdims=True), (16, 128)))
    total = jnp.broadcast_to(jnp.sum(loss[...], keepdims=True), (16, 128))
    lost_power = exponent(total)
    share = total * jnp.exp2(-lost_power)
    coarse = jnp.floor(share * 1024.0) * (1.0 / 1024.0)
    lane = lax.broadcasted_iota(jnp.int32, (16, 128), 1)
    extra = jnp.where(lane == 0, power, 0.0)
    extra = jnp.where(lane == 1, lost_power, extra)
    extra = jnp.where(lane == 2, coarse, extra)
    extra = jnp.where(lane == 3, (share - coarse) * 1024.0, extra)
    up = jnp.broadcast_to(jnp.exp2(13.0 - power)[0:1], (128, 128))
    for k in range(blocks):
        sent[k, 0:128] = sent[k, 0:128] * up
        sent[k, 128:144] = extra


def final_kernel(back, grad_b, lost):
    blocks = back.shape[0]
    total = jnp.zeros((128, 128), jnp.float32)
    loss = jnp.zeros((1, 128), jnp.float32)
    for k in range(blocks):
        extra = back[k, 128:129]
        power = jnp.broadcast_to(extra[:, 0:1], (1, 128))
        total = total + back[k, 0:128] * jnp.exp2(power - 13.0)
        share = extra[:, 2:3] + extra[:, 3:4] * (1.0 / 1024.0)
        loss = loss + jnp.broadcast_to(share * jnp.exp2(extra[:, 1:2]), (1, 128))
    grad_b[...] = 2.0 * total.T
    for k in range(lost.shape[0]):
        lost[k] = jnp.broadcast_to(loss, (8, 128))


def shards(queries, keys, c_proj, b_proj, log_decay):
    rows_dev, heads, size = queries.shape
    peers = lax.axis_size("context")
    z_size = lax.axis_size("head")
    chips = peers // 2
    rows = 2 * rows_dev
    group = 4
    here = lax.axis_index("context")
    place = jnp.stack([here // 2, here % 2]).astype(jnp.int32)
    scale2 = LOG2E / math.sqrt(size)
    plane = [[2 * k + c for k in range(chips)] for c in range(2)]
    swap = [(i, i ^ 1) for i in range(peers)]

    f32 = functools.partial(jax.ShapeDtypeStruct, dtype=jnp.float32)
    bf16 = functools.partial(jax.ShapeDtypeStruct, dtype=jnp.bfloat16)
    smem = pl.BlockSpec(memory_space=pltpu.SMEM)
    vmem = pl.BlockSpec(memory_space=pltpu.VMEM)
    work = heads * rows * chips * 128

    down = log_decay.T
    block = pl.pallas_call(
        block_kernel,
        out_shape=bf16((chips, 288, 128)),
        in_specs=[vmem] * 3,
        out_specs=vmem,
        compiler_params=pltpu.CompilerParams(vmem_limit_bytes=SMALL),
        name="block",
    )(keys[:, 0], b_proj[:, 0], down)
    got = lax.all_to_all(block, "context", 0, 0, axis_index_groups=plane)

    own_q, own_c = queries.transpose(1, 0, 2), c_proj.transpose(1, 0, 2)
    own_t = c_proj.transpose(2, 1, 0).reshape(size, heads * rows_dev)
    other_q, other_c, other_t = (lax.ppermute(x, "context", swap) for x in (own_q, own_c, own_t))

    own_s = pl.pallas_call(
        functools.partial(stats_kernel, heads, scale2),
        out_shape=f32((rows + 8 * chips + 128, 128)),
        in_specs=[smem] + [vmem] * 4,
        out_specs=vmem,
        compiler_params=pltpu.CompilerParams(vmem_limit_bytes=STATS),
        cost_estimate=pl.CostEstimate(flops=2 * work * size, bytes_accessed=2 << 20, transcendentals=work),
        name="stats",
    )(place, got, own_q, other_q, down)
    other_s = lax.ppermute(own_s, "context", swap)

    own_grad, other_grad, sent = pl.pallas_call(
        functools.partial(grad_kernel, heads, scale2, group),
        out_shape=(f32((size, heads * rows_dev)),) * 2 + (f32((chips, 144, 128)),),
        in_specs=[smem] + [vmem] * 9,
        out_specs=(vmem,) * 3,
        scratch_shapes=[pltpu.VMEM((2 * heads, rows_dev, 128), jnp.float32)] * 3
        + [pltpu.VMEM((chips, 8, 128), jnp.float32)] * 2
        + [pltpu.VMEM((heads * rows, group * 128), jnp.bfloat16), pltpu.VMEM((8, 128), jnp.float32)],
        compiler_params=pltpu.CompilerParams(vmem_limit_bytes=GRADS),
        cost_estimate=pl.CostEstimate(flops=8 * work * size, bytes_accessed=6 << 20, transcendentals=2 * work),
        name="grads",
    )(place, got, own_q, other_q, own_c, other_c, own_t, other_t, own_s, other_s)

    back = lax.all_to_all(sent.astype(jnp.float16), "context", 0, 0, axis_index_groups=plane)
    grad_c = 2.0 * (own_grad + lax.ppermute(other_grad, "context", swap))
    grad_c = grad_c.reshape(size, heads, rows_dev).transpose(2, 1, 0)
    mine, lost = pl.pallas_call(
        final_kernel,
        out_shape=(f32((rows_dev, size)), f32((2 * z_size, 8, 128))),
        in_specs=[vmem],
        out_specs=(vmem,) * 2,
        compiler_params=pltpu.CompilerParams(vmem_limit_bytes=SMALL),
        name="final",
    )(back.astype(jnp.float32))

    columns = [[(2 * k + c) * z_size + z for c in range(2) for z in range(z_size)] for k in range(chips)]
    lost = lax.all_to_all(lost, ("context", "head"), 0, 0, axis_index_groups=columns)
    distill_loss = jnp.sum(lost[:, 0, 0]) / (heads * z_size * peers * rows_dev)
    return distill_loss, grad_c, mine[:, None, :]


def solution(mesh):
    in_specs = (
        P("context", "head", None),
        P("context", "head", None),
        P("context", "head", None),
        P("context", "head", None),
        P("context", "head"),
    )
    out_specs = (P(), P("context", "head", None), P("context", "head", None))
    return jax.shard_map(shards, mesh=mesh, in_specs=in_specs, out_specs=out_specs, check_vma=False)
```

time: 111 us -> 88.2 us (0.79)
  starting transfers between devices: 43.9 us -> 33 us
  waiting for transfers between devices: 38.6 us -> 32.2 us
  local copies, waits for them, and re-layouts: 9.39 us -> 5.35 us
    all_to_all x1, starting transfers between devices: 20.4 us -> 9.7 us  [shards(): lax.all_to_all(sent.astype(jnp.float16), 'context', 0, 0, axis_index_grou...]
    all_to_all x1, waiting for transfers between devices: 16.7 us -> 10.7 us  [shards(): lax.all_to_all(sent.astype(jnp.float16), 'context', 0, 0, axis_index_grou...]
    concatenate x1 -> x0, local copies, waits for them, and re-layouts: 2.98 us -> none  [shards(): sent = jnp.concatenate([grad_b, lost], axis=1)]
    unnamed x35 -> x20, local copies, waits for them, and re-layouts: 6.42 us -> 4.07 us
    pallas_call x1, Pallas kernels: 3.35 us -> 5.6 us  [shards(): pl.pallas_call(functools.partial(stats_kernel, heads, scale2), out_shape=...]
    pallas_call x2, Pallas kernels: 8.4 us -> 6.27 us  [the longest x1 5.03 us: shards(): pl.pallas_call(functools.partial(grad_kernel, heads, scale2, group), out_...]
    reduce_sum x1 -> x0, other arithmetic: 1.29 us -> none  [shards(): lost = jnp.broadcast_to(jnp.sum(loss), (chips, 8, 128))]
    ppermute x4 -> x3, waiting for transfers between devices: 1.21 us -> 0.07 us  [shards(): lax.ppermute(x, 'context', swap)]
  transfers between devices with their start and end apart: 9 -> 8, of which waited for: 4 -> 5; matrix products, arithmetic and copies ran while one was open for 2% -> 2% of each run, Pallas kernels for 5% -> 7%
where the time goes in v2:
time: 88.2 us; the launch traced here: 87.6 us
  starting transfers between devices  33 us (37%)
  waiting for transfers between devices  32.2 us (37%)
  Pallas kernels  12.8 us (15%)
  local copies, waits for them, and re-layouts  5.35 us (6%)
  between operations  2.52 us (3%)
  other arithmetic  1.74 us (2%)
    all_to_all x1, waiting for transfers between devices, shards(): got = lax.all_to_all(block, 'context', 0, 0, axis_index_groups=plane)  15.1 us
    all_to_all x1, waiting for transfers between devices, shards(): lax.all_to_all(sent.astype(jnp.float16), 'context', 0, 0, axis_index_grou...  10.7 us
    all_to_all x1, starting transfers between devices, shards(): lax.all_to_all(lost, ('context', 'head'), 0, 0, axis_index_groups=columns)  10.3 us
    all_to_all x1, starting transfers between devices, shards(): lax.all_to_all(sent.astype(jnp.float16), 'context', 0, 0, axis_index_grou...  9.7 us
    all_to_all x1, starting transfers between devices, shards(): got = lax.all_to_all(block, 'context', 0, 0, axis_index_groups=plane)  7.72 us
    all_to_all x1, waiting for transfers between devices, shards(): lax.all_to_all(lost, ('context', 'head'), 0, 0, axis_index_groups=columns)  5.95 us
    pallas_call x1, Pallas kernels, shards(): pl.pallas_call(functools.partial(stats_kernel, heads, scale2), out_shape=...  5.6 us
    pallas_call x1, Pallas kernels, shards(): pl.pallas_call(functools.partial(grad_kernel, heads, scale2, group), out_...  5.03 us
  transfers between devices with their start and end apart: 8, of which 5 were waited for; matrix products, arithmetic and copies ran while one was open for 2% of the time, Pallas kernels for 7%

profile of v2, /device:TPU:1, one launch (start us, length us, event | category | flops | bytes accessed | tf_op | source)
XLA Modules:
  0.0 87.6 jit_solution(17387166507831516056)
XLA Ops:
  0.6 0.7 copy-done
  1.4 0.8 copy-done.1
  2.1 0.7 copy-done.2
  2.8 1.2 %block.1 = bf16[16,288,128]{2,1,0:T(8,128)(2,1)} custom-call(bf16[128,128]{1,0:T(8,128)(2,1)S(1)} %bitcast.30, bf16[128,128]{1,0:T(8,128)(2,1)S(1)} %bitcast.31, f32[8,128]{1,0:T(8,128)S(1)} %bitcast.32), custom_call_target="tpu_custom_call" | custom-call | tf_op jit(solution)/shard_map/block/pallas_call | solution.py:228
  4.1 7.7 %all-to-all-start = ((bf16[16,288,128]{2,1,0:T(8,128)(2,1)}), bf16[16,288,128]{2,1,0:T(8,128)(2,1)S(1)}, u32[]{:S(2)}, u32[]{:S(2)}) async-start(bf16[16,288,128]{2,1,0:T(8,128)(2,1)} %block.1), calls=%async_computation | async-start | bytes 2359296 | tf_op jit(solution)/shard_map/all_to_all | solution.py:236
  11.8 0.0 copy-start.3
  11.9 1.0 %collective-permute-start = (bf16[8,128,128]{2,1,0:T(8,128)(2,1)S(1)}, bf16[8,128,128]{2,1,0:T(8,128)(2,1)S(1)}, u32[]{:S(2)}, u32[]{:S(2)}) collective-permute-start(bf16[8,128,128]{2,1,0:T(8,128)(2,1)S(1)} %bitcast.23), channel_id=1, source_target_pairs={{0,8},{8,0},{16,24},{24,16},{32,40},{40,32},{48,56},{56,48},{64,72... | collective-permute-start | bytes 786440 | tf_op jit(solution)/shard_map/ppermute | solution.py:240
  13.0 0.1 collective-permute-start.1
  13.1 0.2 copy.10
  13.4 0.6 collective-permute-start.2
  13.9 0.1 pad_add_fusion.place
  14.0 0.1 collective-permute-done.other_q
  14.1 15.1 %all-to-all-done.got = bf16[16,288,128]{2,1,0:T(8,128)(2,1)S(1)} async-done(((bf16[16,288,128]{2,1,0:T(8,128)(2,1)}), bf16[16,288,128]{2,1,0:T(8,128)(2,1)S(1)}, u32[]{:S(2)}, u32[]{:S(2)}) %all-to-all-start) | async-done | bytes 1179680 | tf_op jit(solution)/shard_map/all_to_all | solution.py:236
  29.2 5.6 %stats.1.own_s = f32[512,128]{1,0:T(8,128)S(1)} custom-call(s32[2]{0:T(128)S(1)} %pad_add_fusion.place, bf16[16,288,128]{2,1,0:T(8,128)(2,1)S(1)} %all-to-all-done.got, bf16[8,128,128]{2,1,0:T(8,128)(2,1)S(1)} %bitcast.24, bf16[8,128,128]{2,1,0:T(8,128)(2,1)S(1)} %collective-permute-done.other_q, f32[8,128]{1,0:T(8,128)S(1)} %bitcast.33), custom_call_target="tpu_custom_call" | custom-call | flops 1073741824 | bytes 2097152 | tf_op jit(solution)/shard_map/stats/pallas_call | solution.py:242
  34.8 2.9 %collective-permute-start.3 = (f32[512,128]{1,0:T(8,128)S(1)}, f32[512,128]{1,0:T(8,128)S(1)}, u32[]{:S(2)}, u32[]{:S(2)}) collective-permute-start(f32[512,128]{1,0:T(8,128)S(1)} %stats.1.own_s), channel_id=1, source_target_pairs={{0,8},{8,0},{16,24},{24,16},{32,40},{40,32},{48,56},{56,48},{64,72... | collective-permute-start | bytes 786440 | tf_op jit(solution)/shard_map/ppermute | solution.py:251
  37.7 0.0 collective-permute-done.1.other_c
  37.7 0.7 copy-done.4
  38.4 0.5 collective-permute-done.3.other_s
  38.8 0.9 %copy-done.5 = bf16[128,1024]{1,0:T(8,128)(2,1)S(1)} copy-done((bf16[128,1024]{1,0:T(8,128)(2,1)S(1)}, bf16[128,1024]{1,0:T(8,128)(2,1)}, u32[]{:S(2)}) %copy-start.5) | copy-done | bytes 262168
  39.8 5.0 %grads.1 = (f32[128,1024]{1,0:T(8,128)S(1)}, f32[128,1024]{1,0:T(8,128)S(1)}, f32[16,144,128]{2,1,0:T(8,128)S(1)}) custom-call(s32[2]{0:T(128)S(1)} %pad_add_fusion.place, bf16[16,288,128]{2,1,0:T(8,128)(2,1)S(1)} %all-to-all-done.got, bf16[8,128,128]{2,1,0:T(8,128)(2,1)S(1)} %bitcast.25, bf16[8,128,128]{2,1,0:T(8,128)(2,1)S(1)} %collective-permute-done.other_q, ...), custom_call_target="tpu_custom_call" | custom-call | flops 4294967296 | bytes 6291456 | tf_op jit(solution)/shard_map/grads/pallas_call | solution.py:253
  44.8 0.9 %convert_element_type.6 = f16[16,144,128]{2,1,0:T(8,128)(2,1)} convert(f32[16,144,128]{2,1,0:T(8,128)S(1)} %get-tuple-element.8) | non-fusion elementwise | flops 294912 | bytes 1769472 | tf_op jit(solution)/shard_map/convert_element_type | solution.py:266
  45.7 9.7 %all-to-all-start.1 = ((f16[16,144,128]{2,1,0:T(8,128)(2,1)}), f16[16,144,128]{2,1,0:T(8,128)(2,1)S(1)}, u32[]{:S(2)}, u32[]{:S(2)}) async-start(f16[16,144,128]{2,1,0:T(8,128)(2,1)} %convert_element_type.6), calls=%async_computation.1 | async-start | bytes 1179648 | tf_op jit(solution)/shard_map/all_to_all | solution.py:266
  55.4 0.7 collective-permute-start.4
  56.2 10.7 %all-to-all-done.1 = f16[16,144,128]{2,1,0:T(8,128)(2,1)S(1)} async-done(((f16[16,144,128]{2,1,0:T(8,128)(2,1)}), f16[16,144,128]{2,1,0:T(8,128)(2,1)S(1)}, u32[]{:S(2)}, u32[]{:S(2)}) %all-to-all-start.1) | async-done | bytes 589856 | tf_op jit(solution)/shard_map/all_to_all | solution.py:266
  66.8 0.1 convert_element_type.7.back
  66.9 0.9 final.1
  67.8 10.3 %all-to-all-start.2 = ((f32[16,8,128]{2,1,0:T(8,128)}), f32[16,8,128]{2,1,0:T(8,128)S(1)}, u32[]{:S(2)}, u32[]{:S(2)}) async-start(f32[16,8,128]{2,1,0:T(8,128)} %get-tuple-element.9), calls=%async_computation.2 | async-start | bytes 131072 | tf_op jit(solution)/shard_map/all_to_all | solution.py:279
  78.1 0.1 multiply_bitcast_fusion
  78.1 0.1 copy.14
  78.2 1.0 %copy.11 = f32[128,8,128]{0,1,2:T(8,128)} copy(f32[128,8,128]{2,1,0:T(8,128)S(1)} %bitcast.34) | data formatting | bytes 1048576 | tf_op jit(solution)/shard_map/reshape | solution.py:268
  79.3 5.9 %all-to-all-done.2 = f32[16,8,128]{2,1,0:T(8,128)S(1)} async-done(((f32[16,8,128]{2,1,0:T(8,128)}), f32[16,8,128]{2,1,0:T(8,128)S(1)}, u32[]{:S(2)}, u32[]{:S(2)}) %all-to-all-start.2) | async-done | bytes 65568 | tf_op jit(solution)/shard_map/all_to_all | solution.py:279
  85.2 0.6 slice_reduce_fusion
  (15 shorter events, 0.1 us)
Async XLA Ops:
  0.6 0.8 copy-start
  1.4 0.8 copy-start.1
  2.1 0.7 copy-start.2
  4.1 7.7 %copy-start.7 = (bf16[128,8,128]{2,1,0:T(8,128)(2,1)S(1)}, bf16[128,8,128]{2,1,0:T(8,128)(2,1)}, u32[]{:S(2)}) copy-start(bf16[128,8,128]{2,1,0:T(8,128)(2,1)} %param.5) | copy-start | bytes 786436
  4.1 8.8 %copy-start.6 = (bf16[128,8,128]{2,1,0:T(8,128)(2,1)S(1)}, bf16[128,8,128]{2,1,0:T(8,128)(2,1)}, u32[]{:S(2)}) copy-start(bf16[128,8,128]{2,1,0:T(8,128)(2,1)} %param.7) | copy-start | bytes 786436
  4.1 25.1 %all-to-all-start = ((bf16[16,288,128]{2,1,0:T(8,128)(2,1)}), bf16[16,288,128]{2,1,0:T(8,128)(2,1)S(1)}, u32[]{:S(2)}, u32[]{:S(2)}) async-start(bf16[16,288,128]{2,1,0:T(8,128)(2,1)} %block.1), calls=%async_computation | async-start | bytes 2359296 | tf_op jit(solution)/shard_map/all_to_all | solution.py:236
  11.8 17.4 %copy-start.3 = (f32[128,8]{0,1:T(8,128)S(1)}, f32[128,8]{0,1:T(8,128)}, u32[]{:S(2)}) copy-start(f32[128,8]{0,1:T(8,128)} %param.9) | copy-start | bytes 12292
  11.9 2.2 %collective-permute-start = (bf16[8,128,128]{2,1,0:T(8,128)(2,1)S(1)}, bf16[8,128,128]{2,1,0:T(8,128)(2,1)S(1)}, u32[]{:S(2)}, u32[]{:S(2)}) collective-permute-start(bf16[8,128,128]{2,1,0:T(8,128)(2,1)S(1)} %bitcast.23), channel_id=1, source_target_pairs={{0,8},{8,0},{16,24},{24,16},{32,40},{40,32},{48,56},{56,48},{64,72... | collective-permute-start | bytes 786440 | tf_op jit(solution)/shard_map/ppermute | solution.py:240
  13.0 24.7 %collective-permute-start.1 = (bf16[8,128,128]{2,1,0:T(8,128)(2,1)S(1)}, bf16[8,128,128]{2,1,0:T(8,128)(2,1)S(1)}, u32[]{:S(2)}, u32[]{:S(2)}) collective-permute-start(bf16[8,128,128]{2,1,0:T(8,128)(2,1)S(1)} %bitcast.26), channel_id=1, source_target_pairs={{0,8},{8,0},{16,24},{24,16},{32,40},{40,32},{48,56},{56,48},{64,72... | collective-permute-start | bytes 786440 | tf_op jit(solution)/shard_map/ppermute | solution.py:240
  13.4 24.3 %collective-permute-start.2 = (bf16[128,1024]{1,0:T(8,128)(2,1)S(1)}, bf16[128,1024]{1,0:T(8,128)(2,1)S(1)}, u32[]{:S(2)}, u32[]{:S(2)}) collective-permute-start(bf16[128,1024]{1,0:T(8,128)(2,1)S(1)} %bitcast.28), channel_id=1, source_target_pairs={{0,8},{8,0},{16,24},{24,16},{32,40},{40,32},{48,56},{56,48},{64,72... | collective-permute-start | bytes 786440 | tf_op jit(solution)/shard_map/ppermute | solution.py:240
  34.8 4.0 %collective-permute-start.3 = (f32[512,128]{1,0:T(8,128)S(1)}, f32[512,128]{1,0:T(8,128)S(1)}, u32[]{:S(2)}, u32[]{:S(2)}) collective-permute-start(f32[512,128]{1,0:T(8,128)S(1)} %stats.1.own_s), channel_id=1, source_target_pairs={{0,8},{8,0},{16,24},{24,16},{32,40},{40,32},{48,56},{56,48},{64,72... | collective-permute-start | bytes 786440 | tf_op jit(solution)/shard_map/ppermute | solution.py:251
  37.7 0.7 copy-start.4
  38.8 0.9 %copy-start.5 = (bf16[128,1024]{1,0:T(8,128)(2,1)S(1)}, bf16[128,1024]{1,0:T(8,128)(2,1)}, u32[]{:S(2)}) copy-start(bf16[128,1024]{1,0:T(8,128)(2,1)} %copy-done.4) | copy-start | bytes 786436
  45.7 21.1 %all-to-all-start.1 = ((f16[16,144,128]{2,1,0:T(8,128)(2,1)}), f16[16,144,128]{2,1,0:T(8,128)(2,1)S(1)}, u32[]{:S(2)}, u32[]{:S(2)}) async-start(f16[16,144,128]{2,1,0:T(8,128)(2,1)} %convert_element_type.6), calls=%async_computation.1 | async-start | bytes 1179648 | tf_op jit(solution)/shard_map/all_to_all | solution.py:266
  55.4 22.6 %collective-permute-start.4 = (f32[128,1024]{1,0:T(8,128)S(1)}, f32[128,1024]{1,0:T(8,128)S(1)}, u32[]{:S(2)}, u32[]{:S(2)}) collective-permute-start(f32[128,1024]{1,0:T(8,128)S(1)} %get-tuple-element.11), channel_id=1, source_target_pairs={{0,8},{8,0},{16,24},{24,16},{32,40},{40,32},{48,56},{56,48},{64,72... | collective-permute-start | bytes 1572872 | tf_op jit(solution)/shard_map/ppermute | solution.py:267
  67.8 17.4 %all-to-all-start.2 = ((f32[16,8,128]{2,1,0:T(8,128)}), f32[16,8,128]{2,1,0:T(8,128)S(1)}, u32[]{:S(2)}, u32[]{:S(2)}) async-start(f32[16,8,128]{2,1,0:T(8,128)} %get-tuple-element.9), calls=%async_computation.2 | async-start | bytes 131072 | tf_op jit(solution)/shard_map/all_to_all | solution.py:279

commit v3 on v2

v3 whole, which is shorter than its diff:
```python
import functools
import math

import jax
import jax.numpy as jnp
from jax import lax
from jax.experimental import pallas as pl
from jax.experimental.pallas import tpu as pltpu
from jax.sharding import PartitionSpec as P

NEG = -1e30
LOG2E = math.log2(math.e)
TINY = 1e-30
FULL, SMALL, STATS, GRADS = 60 << 20, 8 << 20, 16 << 20, 20 << 20


def dot(a, b):
    return jnp.dot(a, b, preferred_element_type=jnp.float32)


def dot_nt(a, b):
    return lax.dot_general(a, b, (((1,), (1,)), ((), ())), preferred_element_type=jnp.float32)


def pieces(x):
    high = x.astype(jnp.bfloat16)
    rest = x - high.astype(jnp.float32)
    mid = rest.astype(jnp.bfloat16)
    return high, mid, (rest - mid.astype(jnp.float32)).astype(jnp.bfloat16)


def exponent(x):
    return jnp.floor(jnp.log2(jnp.maximum(x, TINY)))


def position(core, row):
    return (row + core * 128) % 256


def block_kernel(keys, b_rows, log_decay, out):
    high, mid, low = pieces(log_decay[...])
    down = jnp.concatenate([high, mid, low, jnp.zeros((8, 128), jnp.bfloat16)], axis=0)
    key_cols, b_cols = keys[...].T, b_rows[...].T
    for k in range(out.shape[0]):
        out[k, 0:128] = key_cols
        out[k, 128:256] = b_cols
        out[k, 256:288] = down


def stats_kernel(heads, scale2, group, place, got, own_q, other_q, log_decay, out, scores):
    chip, core = place[0], place[1]
    blocks = got.shape[0]
    half = own_q.shape[1]
    rows = 2 * half
    row = lax.broadcasted_iota(jnp.int32, (rows, 128), 0)
    lane = lax.broadcasted_iota(jnp.int32, (rows, 128), 1)
    gap = position(core, row) - lane - core * 128 + chip * 256
    keys = jnp.concatenate([got[k, 0:128] for k in range(blocks)], axis=1)
    result = jnp.zeros((rows, 128), jnp.float32)
    width = 128 * group
    for h in range(heads):
        s = dot(jnp.concatenate([own_q[h], other_q[h]], axis=0), keys) * scale2
        for p in range(blocks // group):
            scores[p, h * half : h * half + half] = s[:half, width * p : width * p + width]
            scores[p, (heads + h) * half : (heads + h) * half + half] = s[half:, width * p : width * p + width]
        parts = [jnp.where(gap >= 256 * k, s[:, 128 * k : 128 * k + 128], NEG) for k in range(blocks)]
        top = jnp.max(functools.reduce(jnp.maximum, parts), axis=1, keepdims=True)
        summed = jnp.sum(sum(jnp.exp2(x - top) for x in parts), axis=1, keepdims=True)
        result = jnp.where(lane == h, top, result)
        result = jnp.where(lane == heads + h, summed, result)
    out[:rows] = result
    ones = jnp.ones((128, 128), jnp.bfloat16)
    for k in range(blocks):
        sums = dot(got[k, 256:288], ones)
        out[rows + 8 * k : rows + 8 * k + 8] = sums[0:8] + sums[8:16] + sums[16:24]
    wide = jnp.concatenate([log_decay[...], jnp.zeros((128 - heads, 128), jnp.float32)], axis=0)
    out[rows + 8 * blocks :] = wide.T


def mismatch_kernel(heads, group, place, got, scores, own_c, other_c, own_s, other_s, weighted, loss,
                    peak, fade, log_fade, key_fade, key_log, total):
    chip, core = place[0], place[1]
    half = own_s.shape[0] // 4
    rows = 2 * half
    blocks = got.shape[0]
    mine = own_s[:rows]
    theirs = jnp.concatenate([other_s[half:rows], other_s[:half]], axis=0)
    u = lax.broadcasted_iota(jnp.int32, (rows, rows), 0)
    v = lax.broadcasted_iota(jnp.int32, (rows, rows), 1)
    lower = jnp.where(position(core, u) >= position(core, v), 1.0, 0.0).astype(jnp.bfloat16)
    log_rows = jnp.zeros((rows, 128), jnp.float32)
    for part in pieces(jnp.concatenate([own_s[rows + 8 * blocks :], other_s[rows + 8 * blocks :]], axis=0)):
        log_rows = log_rows + dot(lower, part)
    log_rows = log_rows * LOG2E
    for h in range(heads):
        a, b = mine[:, h : h + 1], theirs[:, h : h + 1]
        top = jnp.maximum(a, b)
        summed = mine[:, heads + h : heads + h + 1] * jnp.exp2(a - top) + theirs[
            :, heads + h : heads + h + 1
        ] * jnp.exp2(b - top)
        level = jnp.broadcast_to(top + jnp.log2(summed), (rows, 128))
        row_log = jnp.broadcast_to(log_rows[:, h : h + 1], (rows, 128))
        row_fade = jnp.exp2(row_log)
        for t, first in ((h, 0), (heads + h, half)):
            peak[t] = level[first : first + half]
            log_fade[t] = row_log[first : first + half]
            fade[t] = row_fade[first : first + half]
    u = lax.broadcasted_iota(jnp.int32, (128, 128), 0)
    v = lax.broadcasted_iota(jnp.int32, (128, 128), 1)
    after = jnp.where(u > v, 1.0, 0.0).astype(jnp.bfloat16)
    upto = jnp.where(u <= v, 1.0, 0.0).astype(jnp.bfloat16)
    behind = jnp.zeros((8, 128), jnp.float32)
    for k in range(blocks - 1, -1, -1):
        own_sum, other_sum = (x[rows + 8 * k : rows + 8 * k + 8] for x in (own_s, other_s))
        tail = dot(got[k, 256:288], after)
        tail = tail[0:8] + tail[8:16] + tail[16:24]
        tail = tail + jnp.where(core == 0, other_sum, 0.0) + behind
        head = dot(got[k, 256:288], upto)
        head = head[0:8] + head[8:16] + head[16:24]
        head = head + jnp.where(core == 0, 0.0, other_sum)
        logs = jnp.where(chip > k, tail, -head) * LOG2E
        key_log[k] = logs
        key_fade[k] = jnp.exp2(jnp.minimum(logs, 0.0))
        behind = behind + jnp.where(chip > k, own_sum + other_sum, 0.0)

    total[...] = jnp.zeros_like(total)
    row = lax.broadcasted_iota(jnp.int32, (half, 128), 0)
    lane = lax.broadcasted_iota(jnp.int32, (half, 128), 1)
    gaps = [position(core, row + first) - lane - core * 128 for first in (0, half)]

    def wide(x):
        return jnp.concatenate([x] * group, axis=1)

    def step(p, masked):
        places = [group * p + i for i in range(group)]
        b_cols = jnp.concatenate([got[k, 128:256] for k in places], axis=1)
        lost = jnp.zeros((8, 128), jnp.float32)
        for side, c in enumerate((own_c, other_c)):
            inner = dot(c[...].reshape(heads * half, 128), b_cols)
            if masked:
                causal = jnp.concatenate([gaps[side] >= (k - chip) * 256 for k in places], axis=1)
            for h in range(heads):
                t = side * heads + h
                at = slice(t * half, t * half + half)
                from_peak = scores[p, at] - wide(peak[t])
                if masked:
                    logs = wide(log_fade[t]) + jnp.concatenate([key_log[k, h : h + 1] for k in places], axis=1)
                    teacher = jnp.exp2(jnp.where(causal, from_peak, NEG))
                    decay = jnp.exp2(jnp.where(causal, logs, NEG))
                else:
                    teacher = jnp.exp2(from_peak)
                    decay = wide(fade[t]) * jnp.concatenate([key_fade[k, h : h + 1] for k in places], axis=1)
                mismatch = inner[h * half : h * half + half] * decay - teacher
                square = jnp.sum((mismatch * mismatch).reshape(half // 8, 8, 128 * group), axis=0)
                for i in range(group):
                    lost = lost + square[:, 128 * i : 128 * i + 128]
                weighted[p, at] = (mismatch * decay).astype(jnp.bfloat16)
        total[...] += lost

    full = chip // group

    @pl.loop(0, full)
    def _(p):
        step(p, False)

    step(full, True)
    lost = jnp.broadcast_to(jnp.sum(total[...], keepdims=True), (8, 128))
    for k in range(loss.shape[0]):
        loss[k] = lost


def grad_kernel(group, place, got, weighted, own_t, other_t, own_grad, other_grad, sent, power):
    blocks = got.shape[0]
    side = own_t.shape[1]
    full = place[0] // group
    own_grad[...] = jnp.zeros_like(own_grad)
    other_grad[...] = jnp.zeros_like(other_grad)

    @pl.loop(0, full + 1)
    def _(p):
        b_cols = jnp.concatenate([got[group * p + i, 128:256] for i in range(group)], axis=1)
        parts = dot_nt(b_cols, weighted[p])
        own_grad[...] += parts[:, :side]
        other_grad[...] += parts[:, side:]
        parts = dot(own_t[...], weighted[p, :side]) + dot(other_t[...], weighted[p, side:])
        for i in range(group):
            sent[group * p + i] = parts[:, 128 * i : 128 * i + 128]

    @pl.loop(group * (full + 1), blocks)
    def _(k):
        sent[k] = jnp.zeros((128, 128), jnp.float32)

    top = functools.reduce(jnp.maximum, [jnp.abs(sent[k]) for k in range(blocks)])
    level = exponent(jnp.broadcast_to(jnp.max(top, keepdims=True), (128, 128)))
    up = jnp.exp2(13.0 - level)
    for k in range(blocks):
        sent[k] = sent[k] * up
    power[...] = level[0:8]


def extra_kernel(lost, power, extra):
    total = lost[0]
    for k in range(1, lost.shape[0]):
        total = total + lost[k]
    lost_power = exponent(total)
    share = total * jnp.exp2(-lost_power)
    coarse = jnp.floor(share * 1024.0) * (1.0 / 1024.0)
    lane = lax.broadcasted_iota(jnp.int32, (8, 128), 1)
    row = jnp.where(lane == 0, power[...], 0.0)
    row = jnp.where(lane == 1, lost_power, row)
    row = jnp.where(lane == 2, coarse, row)
    row = jnp.where(lane == 3, (share - coarse) * 1024.0, row)
    extra[...] = jnp.concatenate([row, row], axis=0)


def final_kernel(count, back, grad_b, mean):
    blocks = back.shape[0]
    total = jnp.zeros((128, 128), jnp.float32)
    loss = jnp.zeros((1, 128), jnp.float32)
    for k in range(blocks):
        extra = back[k, 128:129]
        power = jnp.broadcast_to(extra[:, 0:1], (1, 128))
        total = total + back[k, 0:128] * jnp.exp2(power - 13.0)
        share = extra[:, 2:3] + extra[:, 3:4] * (1.0 / 1024.0)
        loss = loss + jnp.broadcast_to(share * jnp.exp2(extra[:, 1:2]), (1, 128))
    grad_b[...] = 2.0 * total.T
    mean[...] = jnp.broadcast_to(loss * (1.0 / count), (8, 128))


def shards(queries, keys, c_proj, b_proj, log_decay):
    rows_dev, heads, size = queries.shape
    peers = lax.axis_size("context")
    z_size = lax.axis_size("head")
    chips = peers // 2
    rows = 2 * rows_dev
    group = 4
    here = lax.axis_index("context")
    place = jnp.stack([here // 2, here % 2]).astype(jnp.int32)
    scale2 = LOG2E / math.sqrt(size)
    plane = [[2 * k + c for k in range(chips)] for c in range(2)]
    swap = [(i, i ^ 1) for i in range(peers)]

    f32 = functools.partial(jax.ShapeDtypeStruct, dtype=jnp.float32)
    bf16 = functools.partial(jax.ShapeDtypeStruct, dtype=jnp.bfloat16)
    smem = pl.BlockSpec(memory_space=pltpu.SMEM)
    vmem = pl.BlockSpec(memory_space=pltpu.VMEM)
    work = heads * rows * chips * 128

    down = log_decay.T
    block = pl.pallas_call(
        block_kernel,
        out_shape=bf16((chips, 288, 128)),
        in_specs=[vmem] * 3,
        out_specs=vmem,
        compiler_params=pltpu.CompilerParams(vmem_limit_bytes=FULL),
        name="block",
    )(keys[:, 0], b_proj[:, 0], down)
    got = lax.all_to_all(block, "context", 0, 0, axis_index_groups=plane)

    own_q, own_c = queries.transpose(1, 0, 2), c_proj.transpose(1, 0, 2)
    own_t = c_proj.transpose(2, 1, 0).reshape(size, heads * rows_dev)
    other_q, other_c, other_t = (lax.ppermute(x, "context", swap) for x in (own_q, own_c, own_t))

    own_s, scores = pl.pallas_call(
        functools.partial(stats_kernel, heads, scale2, group),
        out_shape=(f32((rows + 8 * chips + 128, 128)), f32((chips // group, heads * rows, 128 * group))),
        in_specs=[smem] + [vmem] * 4,
        out_specs=(vmem,) * 2,
        compiler_params=pltpu.CompilerParams(vmem_limit_bytes=STATS),
        cost_estimate=pl.CostEstimate(flops=2 * work * size, bytes_accessed=2 << 20, transcendentals=work),
        name="stats",
    )(place, got, own_q, other_q, down)
    other_s = lax.ppermute(own_s, "context", swap)

    weighted, lost = pl.pallas_call(
        functools.partial(mismatch_kernel, heads, group),
        out_shape=(bf16((chips // group, heads * rows, 128 * group)), f32((2 * z_size, 8, 128))),
        in_specs=[smem] + [vmem] * 6,
        out_specs=(vmem,) * 2,
        scratch_shapes=[pltpu.VMEM((2 * heads, rows_dev, 128), jnp.float32)] * 3
        + [pltpu.VMEM((chips, 8, 128), jnp.float32)] * 2
        + [pltpu.VMEM((8, 128), jnp.float32)],
        compiler_params=pltpu.CompilerParams(vmem_limit_bytes=GRADS),
        cost_estimate=pl.CostEstimate(flops=2 * work * size, bytes_accessed=4 << 20, transcendentals=2 * work),
        name="mismatch",
    )(place, got, scores, own_c, other_c, own_s, other_s)

    columns = [[(2 * k + c) * z_size + z for c in range(2) for z in range(z_size)] for k in range(chips)]
    lost = lax.all_to_all(lost, ("context", "head"), 0, 0, axis_index_groups=columns)

    own_grad, other_grad, sent, power = pl.pallas_call(
        functools.partial(grad_kernel, group),
        out_shape=(f32((size, heads * rows_dev)),) * 2 + (f32((chips, size, 128)), f32((8, 128))),
        in_specs=[smem] + [vmem] * 4,
        out_specs=(vmem,) * 4,
        compiler_params=pltpu.CompilerParams(vmem_limit_bytes=GRADS),
        cost_estimate=pl.CostEstimate(flops=4 * work * size, bytes_accessed=4 << 20, transcendentals=0),
        name="grads",
    )(place, got, weighted, own_t, other_t)

    extra = pl.pallas_call(
        extra_kernel,
        out_shape=f32((16, 128)),
        in_specs=[vmem] * 2,
        out_specs=vmem,
        compiler_params=pltpu.CompilerParams(vmem_limit_bytes=SMALL),
        name="extra",
    )(lost, power)

    sent = jnp.concatenate([sent, jnp.broadcast_to(extra, (chips, 16, 128))], axis=1)
    back = lax.all_to_all(sent.astype(jnp.float16), "context", 0, 0, axis_index_groups=plane)
    grad_c = 2.0 * (own_grad + lax.ppermute(other_grad, "context", swap))
    grad_c = grad_c.reshape(size, heads, rows_dev).transpose(2, 1, 0)
    mine, mean = pl.pallas_call(
        functools.partial(final_kernel, heads * z_size * peers * rows_dev),
        out_shape=(f32((rows_dev, size)), f32((8, 128))),
        in_specs=[vmem],
        out_specs=(vmem,) * 2,
        compiler_params=pltpu.CompilerParams(vmem_limit_bytes=SMALL),
        name="final",
    )(back.astype(jnp.float32))
    return mean[0, 0], grad_c, mine[:, None, :]


def solution(mesh):
    in_specs = (
        P("context", "head", None),
        P("context", "head", None),
        P("context", "head", None),
        P("context", "head", None),
        P("context", "head"),
    )
    out_specs = (P(), P("context", "head", None), P("context", "head", None))
    return jax.shard_map(shards, mesh=mesh, in_specs=in_specs, out_specs=out_specs, check_vma=False)
```

time: 88.2 us -> 95.3 us (1.080)
  local copies, waits for them, and re-layouts: 5.35 us -> 20.1 us
  starting transfers between devices: 33 us -> 28.8 us
  waiting for transfers between devices: 32.2 us -> 28.4 us
  Pallas kernels: 12.8 us -> 15.1 us
  between operations: 2.52 us -> 0.78 us
    unnamed x20 -> x18, local copies, waits for them, and re-layouts: 4.07 us -> 18.3 us
    all_to_all x1, waiting for transfers between devices: 5.95 us -> 1.43 us  [shards(): lax.all_to_all(lost, ('context', 'head'), 0, 0, axis_index_groups=columns)]
    all_to_all x1, starting transfers between devices: 9.7 us -> 7.98 us  [shards(): lax.all_to_all(sent.astype(jnp.float16), 'context', 0, 0, axis_index_grou...]
    pallas_call x3 -> x5, Pallas kernels: 11.5 us -> 13.1 us  [the longest x1 6 us: shards(): pl.pallas_call(functools.partial(stats_kernel, heads, scale2, group), out...]
    all_to_all x1, starting transfers between devices: 10.3 us -> 8.86 us  [shards(): lax.all_to_all(lost, ('context', 'head'), 0, 0, axis_index_groups=columns)]
    concatenate x0 -> x1, other arithmetic: none -> 0.98 us  [shards(): jnp.concatenate([sent, jnp.broadcast_to(extra, (chips, 16, 128))], axis=1)]
  transfers between devices with their start and end apart: 8 -> 8, of which waited for: 5 -> 5; matrix products, arithmetic and copies ran while one was open for 2% -> 3% of each run, Pallas kernels for 7% -> 13%
where the time goes in v3:
time: 95.3 us; the launch traced here: 94.5 us
  starting transfers between devices  28.8 us (30%)
  waiting for transfers between devices  28.4 us (30%)
  local copies, waits for them, and re-layouts  20.1 us (21%)
  Pallas kernels  15.1 us (16%)
  other arithmetic  1.32 us (1%)
    unnamed x18, local copies, waits for them, and re-layouts  18.3 us
    all_to_all x1, waiting for transfers between devices, shards(): got = lax.all_to_all(block, 'context', 0, 0, axis_index_groups=plane)  15.1 us
    all_to_all x1, waiting for transfers between devices, shards(): lax.all_to_all(sent.astype(jnp.float16), 'context', 0, 0, axis_index_grou...  10.1 us
    all_to_all x1, starting transfers between devices, shards(): lax.all_to_all(lost, ('context', 'head'), 0, 0, axis_index_groups=columns)  8.86 us
    all_to_all x1, starting transfers between devices, shards(): lax.all_to_all(sent.astype(jnp.float16), 'context', 0, 0, axis_index_grou...  7.98 us
    all_to_all x1, starting transfers between devices, shards(): got = lax.all_to_all(block, 'context', 0, 0, axis_index_groups=plane)  7.72 us
    pallas_call x1, Pallas kernels, shards(): pl.pallas_call(functools.partial(stats_kernel, heads, scale2, group), out...  6 us
    pallas_call x1, Pallas kernels, shards(): pl.pallas_call(functools.partial(mismatch_kernel, heads, group), out_shap...  4.18 us
  transfers between devices with their start and end apart: 8, of which 5 were waited for; matrix products, arithmetic and copies ran while one was open for 3% of the time, Pallas kernels for 13%

profile of v3, /device:TPU:1, one launch (start us, length us, event | category | flops | bytes accessed | tf_op | source)
XLA Modules:
  0.0 94.5 jit_solution(9409894675214055081)
XLA Ops:
  0.6 2.0 %block.1 = bf16[16,288,128]{2,1,0:T(8,128)(2,1)} custom-call(bf16[128,128]{1,0:T(8,128)(2,1)} %bitcast.36, bf16[128,128]{1,0:T(8,128)(2,1)} %bitcast.37, f32[8,128]{1,0:T(8,128)} %bitcast.30), custom_call_target="tpu_custom_call" | custom-call | tf_op jit(solution)/shard_map/block/pallas_call | solution.py:250
  2.6 7.7 %all-to-all-start = ((bf16[16,288,128]{2,1,0:T(8,128)(2,1)}), bf16[16,288,128]{2,1,0:T(8,128)(2,1)S(1)}, u32[]{:S(2)}, u32[]{:S(2)}) async-start(bf16[16,288,128]{2,1,0:T(8,128)(2,1)} %block.1), calls=%async_computation | async-start | bytes 2359296 | tf_op jit(solution)/shard_map/all_to_all | solution.py:258
  10.4 1.0 %collective-permute-start = (bf16[8,128,128]{2,1,0:T(8,128)(2,1)S(1)}, bf16[8,128,128]{2,1,0:T(8,128)(2,1)S(1)}, u32[]{:S(2)}, u32[]{:S(2)}) collective-permute-start(bf16[8,128,128]{2,1,0:T(8,128)(2,1)S(1)} %bitcast.28), channel_id=1, source_target_pairs={{0,8},{8,0},{16,24},{24,16},{32,40},{40,32},{48,56},{56,48},{64,72... | collective-permute-start | bytes 786440 | tf_op jit(solution)/shard_map/ppermute | solution.py:262
  11.5 0.1 collective-permute-start.1
  11.6 0.1 pad_add_fusion.place
  11.7 0.9 collective-permute-done.other_q
  12.6 15.1 %all-to-all-done.got = bf16[16,288,128]{2,1,0:T(8,128)(2,1)S(1)} async-done(((bf16[16,288,128]{2,1,0:T(8,128)(2,1)}), bf16[16,288,128]{2,1,0:T(8,128)(2,1)S(1)}, u32[]{:S(2)}, u32[]{:S(2)}) %all-to-all-start) | async-done | bytes 1179680 | tf_op jit(solution)/shard_map/all_to_all | solution.py:258
  27.8 6.0 %stats.1 = (f32[512,128]{1,0:T(8,128)S(1)}, f32[4,2048,512]{2,1,0:T(8,128)S(1)}) custom-call(s32[2]{0:T(128)S(1)} %pad_add_fusion.place, bf16[16,288,128]{2,1,0:T(8,128)(2,1)S(1)} %all-to-all-done.got, bf16[8,128,128]{2,1,0:T(8,128)(2,1)S(1)} %bitcast.29, bf16[8,128,128]{2,1,0:T(8,128)(2,1)S(1)} %collective-permute-done.other_q, f32[8,128]{1,0:T(8,128)S(1)} %bitcast.31), custom_call_target="tpu_custom_call" | custom-call | flops 1073741824 | bytes 2097152 | tf_op jit(solution)/shard_map/stats/pallas_call | solution.py:264
  33.8 5.7 %copy-done = f32[4,2048,512]{2,1,0:T(8,128)} copy-done((f32[4,2048,512]{2,1,0:T(8,128)}, f32[4,2048,512]{2,1,0:T(8,128)S(1)}, u32[]{:S(2)}) %copy-start) | copy-done | bytes 16777240
  39.5 2.8 %collective-permute-start.2 = (f32[512,128]{1,0:T(8,128)S(1)}, f32[512,128]{1,0:T(8,128)S(1)}, u32[]{:S(2)}, u32[]{:S(2)}) collective-permute-start(f32[512,128]{1,0:T(8,128)S(1)} %get-tuple-element.14.own_s), channel_id=1, source_target_pairs={{0,8},{8,0},{16,24},{24,16},{32,40},{40,32},{48,56},{56,48},{64,72... | collective-permute-start | bytes 786440 | tf_op jit(solution)/shard_map/ppermute | solution.py:273
  42.3 0.2 copy.10
  42.6 0.1 collective-permute-start.3
  42.7 0.0 collective-permute-done.1.other_c
  42.7 0.8 collective-permute-done.2.other_s
  43.5 5.8 %copy-done.1 = f32[4,2048,512]{2,1,0:T(8,128)S(1)} copy-done((f32[4,2048,512]{2,1,0:T(8,128)S(1)}, f32[4,2048,512]{2,1,0:T(8,128)}, u32[]{:S(2)}) %copy-start.1) | copy-done | bytes 16777240
  49.2 4.2 %mismatch.1 = (bf16[4,2048,512]{2,1,0:T(8,128)(2,1)S(1)}, f32[16,8,128]{2,1,0:T(8,128)}) custom-call(s32[2]{0:T(128)S(1)} %pad_add_fusion.place, bf16[16,288,128]{2,1,0:T(8,128)(2,1)S(1)} %all-to-all-done.got, f32[4,2048,512]{2,1,0:T(8,128)S(1)} %copy-done.1, bf16[8,128,128]{2,1,0:T(8,128)(2,1)S(1)} %bitcast.25, ...), custom_call_target="tpu_custom_call" | custom-call | flops 1073741824 | bytes 4194304 | tf_op jit(solution)/shard_map/mismatch/pallas_call | solution.py:275
  53.4 3.2 %copy-done.2 = bf16[4,2048,512]{2,1,0:T(8,128)(2,1)} copy-done((bf16[4,2048,512]{2,1,0:T(8,128)(2,1)}, bf16[4,2048,512]{2,1,0:T(8,128)(2,1)S(1)}, u32[]{:S(2)}) %copy-start.2) | copy-done | bytes 8388632
  56.6 8.9 %all-to-all-start.1 = ((f32[16,8,128]{2,1,0:T(8,128)}), f32[16,8,128]{2,1,0:T(8,128)S(1)}, u32[]{:S(2)}, u32[]{:S(2)}) async-start(f32[16,8,128]{2,1,0:T(8,128)} %get-tuple-element.17), calls=%async_computation.1 | async-start | bytes 131072 | tf_op jit(solution)/shard_map/all_to_all | solution.py:289
  65.5 3.4 %copy-done.3 = bf16[4,2048,512]{2,1,0:T(8,128)(2,1)S(1)} copy-done((bf16[4,2048,512]{2,1,0:T(8,128)(2,1)S(1)}, bf16[4,2048,512]{2,1,0:T(8,128)(2,1)}, u32[]{:S(2)}) %copy-start.3) | copy-done | bytes 8388632
  68.9 2.0 %grads.1 = (f32[128,1024]{1,0:T(8,128)S(1)}, f32[128,1024]{1,0:T(8,128)S(1)}, f32[16,128,128]{2,1,0:T(8,128)S(1)}, f32[8,128]{1,0:T(8,128)S(1)}) custom-call(s32[2]{0:T(128)S(1)} %pad_add_fusion.place, bf16[16,288,128]{2,1,0:T(8,128)(2,1)S(1)} %all-to-all-done.got, bf16[4,2048,512]{2,1,0:T(8,128)(2,1)S(1)} %copy-done.3, bf16[128,1024]{1,0:T(8,128)(2,1)S(1)} %bitcast.27, ...), custom_call_target="tpu_custom_call" | custom-call | flops 2147483648 | bytes 4194304 | tf_op jit(solution)/shard_map/grads/pallas_call | solution.py:291
  70.9 0.2 collective-permute-start.4
  71.1 0.1 convert.7
  71.2 1.4 %all-to-all-done.1.lost = f32[16,8,128]{2,1,0:T(8,128)S(1)} async-done(((f32[16,8,128]{2,1,0:T(8,128)}), f32[16,8,128]{2,1,0:T(8,128)S(1)}, u32[]{:S(2)}, u32[]{:S(2)}) %all-to-all-start.1) | async-done | bytes 65568 | tf_op jit(solution)/shard_map/all_to_all | solution.py:289
  72.7 1.0 %pad_maximum_fusion = f16[16,144,128]{2,1,0:T(8,128)(2,1)} fusion(f16[16,16,128]{2,1,0:T(8,128)(2,1)S(1)} %broadcast_in_dim.6, f16[16,128,128]{2,1,0:T(8,128)(2,1)S(1)} %convert.7), kind=kLoop, calls=%fused_computation | loop fusion | flops 294912 | bytes 1179648 | tf_op jit(solution)/shard_map/concatenate | solution.py:310
  73.7 8.0 %all-to-all-start.2 = ((f16[16,144,128]{2,1,0:T(8,128)(2,1)}), f16[16,144,128]{2,1,0:T(8,128)(2,1)S(1)}, u32[]{:S(2)}, u32[]{:S(2)}) async-start(f16[16,144,128]{2,1,0:T(8,128)(2,1)} %pad_maximum_fusion), calls=%async_computation.2 | async-start | bytes 1179648 | tf_op jit(solution)/shard_map/all_to_all | solution.py:311
  81.7 0.1 multiply_bitcast_fusion
  81.8 0.1 copy.14
  81.9 1.0 %copy.11 = f32[128,8,128]{0,1,2:T(8,128)} copy(f32[128,8,128]{2,1,0:T(8,128)S(1)} %bitcast.32) | data formatting | bytes 1048576 | tf_op jit(solution)/shard_map/reshape | solution.py:313
  82.9 10.1 %all-to-all-done.2 = f16[16,144,128]{2,1,0:T(8,128)(2,1)S(1)} async-done(((f16[16,144,128]{2,1,0:T(8,128)(2,1)}), f16[16,144,128]{2,1,0:T(8,128)(2,1)S(1)}, u32[]{:S(2)}, u32[]{:S(2)}) %all-to-all-start.2) | async-done | bytes 589856 | tf_op jit(solution)/shard_map/all_to_all | solution.py:311
  93.1 0.1 convert_element_type.4.back
  93.2 0.9 final.1
  94.0 0.5 slice.3
  (18 shorter events, 0.2 us)
Async XLA Ops:
  2.6 7.7 %copy-start.6 = (bf16[128,8,128]{2,1,0:T(8,128)(2,1)S(1)}, bf16[128,8,128]{2,1,0:T(8,128)(2,1)}, u32[]{:S(2)}) copy-start(bf16[128,8,128]{2,1,0:T(8,128)(2,1)} %param.5) | copy-start | bytes 786436
  2.6 8.8 %copy-start.5 = (bf16[128,8,128]{2,1,0:T(8,128)(2,1)S(1)}, bf16[128,8,128]{2,1,0:T(8,128)(2,1)}, u32[]{:S(2)}) copy-start(bf16[128,8,128]{2,1,0:T(8,128)(2,1)} %param.7) | copy-start | bytes 786436
  2.6 25.1 %copy-start.4 = (f32[128,8]{0,1:T(8,128)S(1)}, f32[128,8]{0,1:T(8,128)}, u32[]{:S(2)}) copy-start(f32[128,8]{0,1:T(8,128)} %param.9) | copy-start | bytes 12292
  2.6 25.1 %all-to-all-start = ((bf16[16,288,128]{2,1,0:T(8,128)(2,1)}), bf16[16,288,128]{2,1,0:T(8,128)(2,1)S(1)}, u32[]{:S(2)}, u32[]{:S(2)}) async-start(bf16[16,288,128]{2,1,0:T(8,128)(2,1)} %block.1), calls=%async_computation | async-start | bytes 2359296 | tf_op jit(solution)/shard_map/all_to_all | solution.py:258
  10.4 2.2 %collective-permute-start = (bf16[8,128,128]{2,1,0:T(8,128)(2,1)S(1)}, bf16[8,128,128]{2,1,0:T(8,128)(2,1)S(1)}, u32[]{:S(2)}, u32[]{:S(2)}) collective-permute-start(bf16[8,128,128]{2,1,0:T(8,128)(2,1)S(1)} %bitcast.28), channel_id=1, source_target_pairs={{0,8},{8,0},{16,24},{24,16},{32,40},{40,32},{48,56},{56,48},{64,72... | collective-permute-start | bytes 786440 | tf_op jit(solution)/shard_map/ppermute | solution.py:262
  11.5 31.2 %collective-permute-start.1 = (bf16[8,128,128]{2,1,0:T(8,128)(2,1)S(1)}, bf16[8,128,128]{2,1,0:T(8,128)(2,1)S(1)}, u32[]{:S(2)}, u32[]{:S(2)}) collective-permute-start(bf16[8,128,128]{2,1,0:T(8,128)(2,1)S(1)} %bitcast.24), channel_id=1, source_target_pairs={{0,8},{8,0},{16,24},{24,16},{32,40},{40,32},{48,56},{56,48},{64,72... | collective-permute-start | bytes 786440 | tf_op jit(solution)/shard_map/ppermute | solution.py:262
  33.8 5.7 %copy-start = (f32[4,2048,512]{2,1,0:T(8,128)}, f32[4,2048,512]{2,1,0:T(8,128)S(1)}, u32[]{:S(2)}) copy-start(f32[4,2048,512]{2,1,0:T(8,128)S(1)} %get-tuple-element.13.scores) | copy-start | bytes 50331652
  39.5 4.0 %collective-permute-start.2 = (f32[512,128]{1,0:T(8,128)S(1)}, f32[512,128]{1,0:T(8,128)S(1)}, u32[]{:S(2)}, u32[]{:S(2)}) collective-permute-start(f32[512,128]{1,0:T(8,128)S(1)} %get-tuple-element.14.own_s), channel_id=1, source_target_pairs={{0,8},{8,0},{16,24},{24,16},{32,40},{40,32},{48,56},{56,48},{64,72... | collective-permute-start | bytes 786440 | tf_op jit(solution)/shard_map/ppermute | solution.py:273
  42.6 22.9 %collective-permute-start.3 = (bf16[128,1024]{1,0:T(8,128)(2,1)S(1)}, bf16[128,1024]{1,0:T(8,128)(2,1)S(1)}, u32[]{:S(2)}, u32[]{:S(2)}) collective-permute-start(bf16[128,1024]{1,0:T(8,128)(2,1)S(1)} %bitcast.26), channel_id=1, source_target_pairs={{0,8},{8,0},{16,24},{24,16},{32,40},{40,32},{48,56},{56,48},{64,72... | collective-permute-start | bytes 786440 | tf_op jit(solution)/shard_map/ppermute | solution.py:262
  43.5 5.8 %copy-start.1 = (f32[4,2048,512]{2,1,0:T(8,128)S(1)}, f32[4,2048,512]{2,1,0:T(8,128)}, u32[]{:S(2)}) copy-start(f32[4,2048,512]{2,1,0:T(8,128)} %copy-done) | copy-start | bytes 50331652
  53.4 3.2 %copy-start.2 = (bf16[4,2048,512]{2,1,0:T(8,128)(2,1)}, bf16[4,2048,512]{2,1,0:T(8,128)(2,1)S(1)}, u32[]{:S(2)}) copy-start(bf16[4,2048,512]{2,1,0:T(8,128)(2,1)S(1)} %get-tuple-element.15.weighted) | copy-start | bytes 25165828
  56.6 16.0 %all-to-all-start.1 = ((f32[16,8,128]{2,1,0:T(8,128)}), f32[16,8,128]{2,1,0:T(8,128)S(1)}, u32[]{:S(2)}, u32[]{:S(2)}) async-start(f32[16,8,128]{2,1,0:T(8,128)} %get-tuple-element.17), calls=%async_computation.1 | async-start | bytes 131072 | tf_op jit(solution)/shard_map/all_to_all | solution.py:289
  65.5 3.4 %copy-start.3 = (bf16[4,2048,512]{2,1,0:T(8,128)(2,1)S(1)}, bf16[4,2048,512]{2,1,0:T(8,128)(2,1)}, u32[]{:S(2)}) copy-start(bf16[4,2048,512]{2,1,0:T(8,128)(2,1)} %copy-done.2) | copy-start | bytes 25165828
  70.9 10.8 %collective-permute-start.4 = (f32[128,1024]{1,0:T(8,128)S(1)}, f32[128,1024]{1,0:T(8,128)S(1)}, u32[]{:S(2)}, u32[]{:S(2)}) collective-permute-start(f32[128,1024]{1,0:T(8,128)S(1)} %get-tuple-element.21), channel_id=1, source_target_pairs={{0,8},{8,0},{16,24},{24,16},{32,40},{40,32},{48,56},{56,48},{64,72... | collective-permute-start | bytes 1572872 | tf_op jit(solution)/shard_map/ppermute | solution.py:312
  73.7 19.4 %all-to-all-start.2 = ((f16[16,144,128]{2,1,0:T(8,128)(2,1)}), f16[16,144,128]{2,1,0:T(8,128)(2,1)S(1)}, u32[]{:S(2)}, u32[]{:S(2)}) async-start(f16[16,144,128]{2,1,0:T(8,128)(2,1)} %pad_maximum_fusion), calls=%async_computation.2 | async-start | bytes 1179648 | tf_op jit(solution)/shard_map/all_to_all | solution.py:311

commit v4 on v3

v4 whole, which is shorter than its diff:
```python
import functools
import math

import jax
import jax.numpy as jnp
from jax import lax
from jax.experimental import pallas as pl
from jax.experimental.pallas import tpu as pltpu
from jax.sharding import PartitionSpec as P

NEG = -1e30
LOG2E = math.log2(math.e)
TINY = 1e-30
FULL, SMALL, MATCH, GRADS = 60 << 20, 8 << 20, 48 << 20, 20 << 20


def dot(a, b):
    return jnp.dot(a, b, preferred_element_type=jnp.float32)


def dot_nt(a, b):
    return lax.dot_general(a, b, (((1,), (1,)), ((), ())), preferred_element_type=jnp.float32)


def pieces(x):
    high = x.astype(jnp.bfloat16)
    rest = x - high.astype(jnp.float32)
    mid = rest.astype(jnp.bfloat16)
    return high, mid, (rest - mid.astype(jnp.float32)).astype(jnp.bfloat16)


def exponent(x):
    return jnp.floor(jnp.log2(jnp.maximum(x, TINY)))


def block_kernel(keys, b_rows, log_decay, out):
    high, mid, low = pieces(log_decay[...])
    down = jnp.concatenate([high, mid, low, jnp.zeros((8, 128), jnp.bfloat16)], axis=0)
    key_cols, b_cols = keys[...].T, b_rows[...].T
    for k in range(out.shape[0]):
        out[k, 0:128] = key_cols
        out[k, 128:256] = b_cols
        out[k, 256:288] = down


def match_kernel(heads, scale2, group, place, own_b, other_b, q, c, c_cols, log_decay, weighted, own_grad, other_grad, loss,
                 scores, peak, total, fade, log_fade, key_fade, key_log, held, own_held, other_held, lost, sems):
    chip, core = place[0], place[1]
    chips, half = own_b.shape[0], q.shape[1]
    rows = heads * half
    full = chip // group

    u = lax.broadcasted_iota(jnp.int32, (128, 128), 0)
    v = lax.broadcasted_iota(jnp.int32, (128, 128), 1)
    after = jnp.where(u > v, 1.0, 0.0).astype(jnp.bfloat16)
    upto = jnp.where(u <= v, 1.0, 0.0).astype(jnp.bfloat16)
    lower = jnp.where(u >= v, 1.0, 0.0).astype(jnp.bfloat16)
    columns = jnp.concatenate([log_decay[...], jnp.zeros((128 - heads, 128), jnp.float32)], axis=0).T
    log_rows = sum(dot(lower, part) for part in pieces(columns)) * LOG2E
    for h in range(heads):
        row_log = jnp.broadcast_to(log_rows[:, h : h + 1], (half, 128))
        log_fade[h] = row_log
        fade[h] = jnp.exp2(row_log)
    def sums(ref, matrix):
        y = dot(ref[:, 256:288].reshape(chips * 32, 128), matrix).reshape(chips, 32, 128)
        return y[:, 0:8] + y[:, 8:16] + y[:, 16:24]

    ones = jnp.ones((128, 128), jnp.bfloat16)
    own_tail, other_tail = sums(own_b, after), sums(other_b, after)
    own_sum, other_sum = sums(own_b, ones), sums(other_b, ones)
    own_head = sums(own_b, upto)
    behind = jnp.zeros((8, 128), jnp.float32)
    for k in range(chips - 1, -1, -1):
        own = own_tail[k] + behind + jnp.where(core == 0, other_sum[k], 0.0)
        own = jnp.where(chip > k, own, -own_head[k]) * LOG2E
        other = behind + jnp.where(core == 0, 0.0, own_sum[k])
        other = (other_tail[k] + jnp.where(chip > k, other, 0.0)) * LOG2E
        for side, logs in enumerate((own, other)):
            key_log[2 * k + side] = logs
            key_fade[2 * k + side] = jnp.exp2(jnp.minimum(logs, 0.0))
        here = jnp.where(core == 0, 0.0, other_sum[k])
        behind = behind + jnp.where(chip > k, own_sum[k] + other_sum[k], jnp.where(chip == k, here, 0.0))

    def wide(x):
        return jnp.concatenate([x] * (2 * group), axis=1)

    def of_group(p, first):
        return jnp.concatenate(
            [ref[group * p + i, first : first + 128] for i in range(group) for ref in (own_b, other_b)], axis=1
        )

    def causal(p):
        apart = [2 * (group * p + i - chip) + side * (1 - 2 * core) for i in range(group) for side in range(2)]
        return jnp.concatenate([u - v >= 128 * x for x in apart], axis=1)

    peak[...] = jnp.full_like(peak, NEG)
    total[...] = jnp.zeros_like(total)

    def score(p, masked):
        s = dot(q[...].reshape(rows, 128), of_group(p, 0)) * scale2
        seen = causal(p) if masked else None
        for h in range(heads):
            at = slice(h * half, h * half + half)
            x = s[at]
            if masked:
                x = jnp.where(seen, x, NEG)
            scores[p, at] = x
            parts = [x[:, 128 * i : 128 * i + 128] for i in range(2 * group)]
            old = peak[h]
            top = functools.reduce(jnp.maximum, parts, old)
            total[h] = total[h] * jnp.exp2(old - top) + sum(jnp.exp2(y - top) for y in parts)
            peak[h] = top

    @pl.loop(0, full)
    def _(p):
        score(p, False)

    score(full, True)

    for h in range(heads):
        top = jnp.max(peak[h], axis=1, keepdims=True)
        summed = jnp.sum(total[h] * jnp.exp2(peak[h] - top), axis=1, keepdims=True)
        peak[h] = jnp.broadcast_to(top + jnp.log2(summed), (half, 128))
    lost[...] = jnp.zeros_like(lost)

    def copies(p):
        part = pl.ds(p * group, group)
        return (
            pltpu.make_async_copy(held.at[p], weighted.at[p], sems.at[0, p]),
            pltpu.make_async_copy(own_held.at[part], own_grad.at[part], sems.at[1, p]),
            pltpu.make_async_copy(other_held.at[part], other_grad.at[part], sems.at[2, p]),
        )

    @pl.loop(full + 1, chips // group)
    def _(p):
        for i in range(group):
            own_held[group * p + i] = jnp.zeros((128, 128), jnp.float32)
            other_held[group * p + i] = jnp.zeros((128, 128), jnp.float32)
        for x in copies(p)[1:]:
            x.start()

    def step(p, masked):
        kept = [2 * group * p + i for i in range(2 * group)]
        inner = dot(c[...].reshape(rows, 128), of_group(p, 128))
        seen = causal(p) if masked else None
        squares = jnp.zeros((8, 128), jnp.float32)
        for h in range(heads):
            at = slice(h * half, h * half + half)
            teacher = jnp.exp2(scores[p, at] - wide(peak[h]))
            if masked:
                logs = wide(log_fade[h]) + jnp.concatenate([key_log[k, h : h + 1] for k in kept], axis=1)
                decay = jnp.exp2(jnp.where(seen, logs, NEG))
            else:
                decay = wide(fade[h]) * jnp.concatenate([key_fade[k, h : h + 1] for k in kept], axis=1)
            mismatch = inner[at] * decay - teacher
            square = jnp.sum((mismatch * mismatch).reshape(half // 8, 8, 256 * group), axis=0)
            for i in range(2 * group):
                squares = squares + square[:, 128 * i : 128 * i + 128]
            held[p, at] = (mismatch * decay).astype(jnp.bfloat16)
        lost[...] += squares
        parts = dot(c_cols[...], held[p])
        for i in range(group):
            own_held[group * p + i] = parts[:, 256 * i : 256 * i + 128]
            other_held[group * p + i] = parts[:, 256 * i + 128 : 256 * i + 256]
        for x in copies(p):
            x.start()

    @pl.loop(0, full)
    def _(p):
        step(p, False)

    step(full, True)
    mean = jnp.broadcast_to(jnp.sum(lost[...], keepdims=True), (8, 128))
    for k in range(loss.shape[0]):
        loss[k] = mean

    @pl.loop(0, full + 1)
    def _(p):
        copies(p)[0].wait()

    @pl.loop(0, chips // group)
    def _(p):
        for x in copies(p)[1:]:
            x.wait()


def grad_kernel(group, place, own_b, other_b, weighted, grad_c, held, sems):
    full = place[0] // group

    def copy(p):
        return pltpu.make_async_copy(weighted.at[p], held.at[p], sems.at[p])

    @pl.loop(0, full + 1)
    def _(p):
        copy(p).start()

    grad_c[...] = jnp.zeros_like(grad_c)

    @pl.loop(0, full + 1)
    def _(p):
        copy(p).wait()
        b_cols = jnp.concatenate(
            [ref[group * p + i, 128:256] for i in range(group) for ref in (own_b, other_b)], axis=1
        )
        grad_c[...] += 2.0 * dot_nt(b_cols, held[p])


def scale_kernel(own, other, sent, power):
    blocks = own.shape[0]
    top = jnp.zeros((128, 128), jnp.float32)
    for k in range(blocks):
        x = own[k] + other[k]
        sent[k, 0:128] = x
        top = jnp.maximum(top, jnp.abs(x))
    level = exponent(jnp.broadcast_to(jnp.max(top, keepdims=True), (128, 128)))
    up = jnp.exp2(13.0 - level)
    for k in range(blocks):
        sent[k, 0:128] = sent[k, 0:128] * up
        sent[k, 128:144] = jnp.zeros((16, 128), jnp.float32)
    power[...] = level[0:8]


def extra_kernel(lost, power, extra):
    total = lost[0]
    for k in range(1, lost.shape[0]):
        total = total + lost[k]
    lost_power = exponent(total)
    share = total * jnp.exp2(-lost_power)
    coarse = jnp.floor(share * 1024.0) * (1.0 / 1024.0)
    lane = lax.broadcasted_iota(jnp.int32, (8, 128), 1)
    row = jnp.where(lane == 0, power[...], 0.0)
    row = jnp.where(lane == 1, lost_power, row)
    row = jnp.where(lane == 2, coarse, row)
    row = jnp.where(lane == 3, (share - coarse) * 1024.0, row)
    extra[...] = jnp.concatenate([row, row], axis=0)


def final_kernel(count, back, grad_b, mean):
    blocks = back.shape[0]
    total = jnp.zeros((128, 128), jnp.float32)
    loss = jnp.zeros((1, 128), jnp.float32)
    for k in range(blocks):
        extra = back[k, 128:129]
        power = jnp.broadcast_to(extra[:, 0:1], (1, 128))
        total = total + back[k, 0:128] * jnp.exp2(power - 13.0)
        share = extra[:, 2:3] + extra[:, 3:4] * (1.0 / 1024.0)
        loss = loss + jnp.broadcast_to(share * jnp.exp2(extra[:, 1:2]), (1, 128))
    grad_b[...] = 2.0 * total.T
    mean[...] = jnp.broadcast_to(loss * (1.0 / count), (8, 128))


def shards(queries, keys, c_proj, b_proj, log_decay):
    rows_dev, heads, size = queries.shape
    peers = lax.axis_size("context")
    z_size = lax.axis_size("head")
    chips = peers // 2
    rows = heads * rows_dev
    group = 4
    here = lax.axis_index("context")
    place = jnp.stack([here // 2, here % 2]).astype(jnp.int32)
    scale2 = LOG2E / math.sqrt(size)
    plane = [[2 * k + c for k in range(chips)] for c in range(2)]
    swap = [(i, i ^ 1) for i in range(peers)]

    f32 = functools.partial(jax.ShapeDtypeStruct, dtype=jnp.float32)
    bf16 = functools.partial(jax.ShapeDtypeStruct, dtype=jnp.bfloat16)
    smem = pl.BlockSpec(memory_space=pltpu.SMEM)
    vmem = pl.BlockSpec(memory_space=pltpu.VMEM)
    hbm = pl.BlockSpec(memory_space=pltpu.MemorySpace.HBM)
    work = rows * peers * 128
    steps = chips // group
    width = 256 * group

    down = log_decay.T
    block = pl.pallas_call(
        block_kernel,
        out_shape=bf16((chips, 288, 128)),
        in_specs=[vmem] * 3,
        out_specs=vmem,
        compiler_params=pltpu.CompilerParams(vmem_limit_bytes=FULL),
        name="block",
    )(keys[:, 0], b_proj[:, 0], down)
    own_b = lax.all_to_all(block, "context", 0, 0, axis_index_groups=plane)
    q, c = queries.transpose(1, 0, 2), c_proj.transpose(1, 0, 2)
    c_cols = c_proj.transpose(2, 1, 0).reshape(size, rows)
    own_b, q, c, c_cols, place = lax.optimization_barrier((own_b, q, c, c_cols, place))
    other_b = lax.ppermute(own_b, "context", swap)
    tile = pltpu.VMEM((heads, rows_dev, 128), jnp.float32)
    hbm_out = pltpu.MemorySpace.HBM
    weighted, own_sum, other_sum, lost = pl.pallas_call(
        functools.partial(match_kernel, heads, scale2, group),
        out_shape=(
            hbm_out((steps, rows, width), jnp.bfloat16),
            hbm_out((chips, size, 128), jnp.float32),
            hbm_out((chips, size, 128), jnp.float32),
            hbm_out((2 * z_size, 8, 128), jnp.float32),
        ),
        in_specs=[smem] + [vmem] * 6,
        out_specs=(hbm, hbm, hbm, pl.BlockSpec((2 * z_size, 8, 128), lambda: (0, 0, 0))),
        scratch_shapes=[pltpu.VMEM((steps, rows, width), jnp.float32)]
        + [tile] * 4
        + [pltpu.VMEM((peers, 8, 128), jnp.float32)] * 2
        + [pltpu.VMEM((steps, rows, width), jnp.bfloat16)]
        + [pltpu.VMEM((chips, size, 128), jnp.float32)] * 2
        + [pltpu.VMEM((8, 128), jnp.float32), pltpu.SemaphoreType.DMA((3, steps))],
        compiler_params=pltpu.CompilerParams(vmem_limit_bytes=MATCH),
        cost_estimate=pl.CostEstimate(flops=6 * work * size, bytes_accessed=12 << 20, transcendentals=3 * work),
        name="match",
    )(place, own_b, other_b, q, c, c_cols, down)

    columns = [[(2 * k + c) * z_size + z for c in range(2) for z in range(z_size)] for k in range(chips)]
    lost = lax.all_to_all(lost, ("context", "head"), 0, 0, axis_index_groups=columns)

    other_sum = lax.ppermute(other_sum, "context", swap)
    sent, power = pl.pallas_call(
        scale_kernel,
        out_shape=(f32((chips, 144, 128)), f32((8, 128))),
        in_specs=[vmem] * 2,
        out_specs=(vmem,) * 2,
        compiler_params=pltpu.CompilerParams(vmem_limit_bytes=SMALL),
        name="scale",
    )(own_sum, other_sum)
    sent, lost = lax.optimization_barrier((sent.astype(jnp.float16), lost))

    extra = pl.pallas_call(
        extra_kernel,
        out_shape=f32((16, 128)),
        in_specs=[vmem] * 2,
        out_specs=vmem,
        compiler_params=pltpu.CompilerParams(vmem_limit_bytes=SMALL),
        name="extra",
    )(lost, power)

    extra = jnp.broadcast_to(extra.astype(jnp.float16), (chips, 16, 128))
    sent = lax.dynamic_update_slice(sent, extra, (0, 128, 0))
    back = lax.all_to_all(sent, "context", 0, 0, axis_index_groups=plane)
    grad_c = pl.pallas_call(
        functools.partial(grad_kernel, group),
        out_shape=f32((size, rows)),
        in_specs=[smem, vmem, vmem, hbm],
        out_specs=vmem,
        scratch_shapes=[pltpu.VMEM((steps, rows, width), jnp.bfloat16), pltpu.SemaphoreType.DMA((steps,))],
        compiler_params=pltpu.CompilerParams(vmem_limit_bytes=GRADS),
        cost_estimate=pl.CostEstimate(flops=2 * work * size, bytes_accessed=10 << 20, transcendentals=0),
        name="grads",
    )(place, own_b, other_b, pltpu.with_memory_space_constraint(weighted, hbm_out))
    grad_c = grad_c.reshape(size, heads, rows_dev).transpose(2, 1, 0)
    mine, mean = pl.pallas_call(
        functools.partial(final_kernel, heads * z_size * peers * rows_dev),
        out_shape=(f32((rows_dev, size)), f32((8, 128))),
        in_specs=[vmem],
        out_specs=(vmem,) * 2,
        compiler_params=pltpu.CompilerParams(vmem_limit_bytes=SMALL),
        name="final",
    )(back.astype(jnp.float32))
    return mean[0, 0], grad_c, mine[:, None, :]


def solution(mesh):
    in_specs = (
        P("context", "head", None),
        P("context", "head", None),
        P("context", "head", None),
        P("context", "head", None),
        P("context", "head"),
    )
    out_specs = (P(), P("context", "head", None), P("context", "head", None))
    return jax.shard_map(shards, mesh=mesh, in_specs=in_specs, out_specs=out_specs, check_vma=False)
```

time: 95.3 us -> 80.6 us (0.85)
  local copies, waits for them, and re-layouts: 20.1 us -> 3.91 us
  waiting for transfers between devices: 28.4 us -> 30.8 us
  Pallas kernels: 15.1 us -> 13.1 us
  starting transfers between devices: 28.8 us -> 30.4 us
    unnamed x18 -> x10, local copies, waits for them, and re-layouts: 18.3 us -> 1.37 us
    all_to_all x1, waiting for transfers between devices: 1.43 us -> 4.5 us  [shards(): lax.all_to_all(lost, ('context', 'head'), 0, 0, axis_index_groups=columns)]
    all_to_all x2, starting transfers between devices: 15.7 us -> 18.6 us  [the longest x1 10.8 us: shards(): back = lax.all_to_all(sent, 'context', 0, 0, axis_index_groups=plane)]
    pallas_call x3, Pallas kernels: 12.2 us -> 10.2 us  [the longest x1 6.7 us: shards(): pl.pallas_call(functools.partial(match_kernel, heads, scale2, group), out...]
    all_to_all x2, waiting for transfers between devices: 25.3 us -> 23.8 us  [the longest x1 16.9 us: shards(): own_b = lax.all_to_all(block, 'context', 0, 0, axis_index_groups=plane)]
    concatenate x1 -> x0, other arithmetic: 0.98 us -> none  [shards(): jnp.concatenate([sent, jnp.broadcast_to(extra, (chips, 16, 128))], axis=1)]
    ppermute x5 -> x2, starting transfers between devices: 4.22 us -> 3.25 us  [the longest x1 2.79 us: shards(): other_b = lax.ppermute(own_b, 'context', swap)]
    ppermute x5 -> x2, waiting for transfers between devices: 1.68 us -> 2.48 us  [the longest x1 2.47 us: shards(): other_b = lax.ppermute(own_b, 'context', swap)]
  transfers between devices with their start and end apart: 8 -> 5, of which waited for: 5 -> 4; matrix products, arithmetic and copies ran while one was open for 3% -> 3% of each run, Pallas kernels for 13% -> 4%
where the time goes in v4:
time: 80.6 us; the launch traced here: 80.1 us
  waiting for transfers between devices  30.8 us (38%)
  starting transfers between devices  30.4 us (38%)
  Pallas kernels  13.1 us (16%)
  local copies, waits for them, and re-layouts  3.91 us (5%)
  other arithmetic  1.1 us (1%)
    all_to_all x1, waiting for transfers between devices, shards(): own_b = lax.all_to_all(block, 'context', 0, 0, axis_index_groups=plane)  16.9 us
    all_to_all x1, starting transfers between devices, shards(): back = lax.all_to_all(sent, 'context', 0, 0, axis_index_groups=plane)  10.8 us
    all_to_all x1, starting transfers between devices, shards(): lax.all_to_all(lost, ('context', 'head'), 0, 0, axis_index_groups=columns)  8.63 us
    all_to_all x1, starting transfers between devices, shards(): own_b = lax.all_to_all(block, 'context', 0, 0, axis_index_groups=plane)  7.72 us
    all_to_all x1, waiting for transfers between devices, shards(): back = lax.all_to_all(sent, 'context', 0, 0, axis_index_groups=plane)  6.99 us
    pallas_call x1, Pallas kernels, shards(): pl.pallas_call(functools.partial(match_kernel, heads, scale2, group), out...  6.7 us
    all_to_all x1, waiting for transfers between devices, shards(): lax.all_to_all(lost, ('context', 'head'), 0, 0, axis_index_groups=columns)  4.5 us
    pallas_call x1, Pallas kernels, shards(): pl.pallas_call(functools.partial(grad_kernel, group), out_shape=f32((size...  3 us
  transfers between devices with their start and end apart: 5, of which 4 were waited for; matrix products, arithmetic and copies ran while one was open for 3% of the time, Pallas kernels for 4%

profile of v4, /device:TPU:1, one launch (start us, length us, event | category | flops | bytes accessed | tf_op | source)
XLA Modules:
  0.0 80.1 jit_solution(4986754918560968681)
XLA Ops:
  0.6 2.0 %block.1 = bf16[16,288,128]{2,1,0:T(8,128)(2,1)} custom-call(bf16[128,128]{1,0:T(8,128)(2,1)} %bitcast.29, bf16[128,128]{1,0:T(8,128)(2,1)} %bitcast.30, f32[8,128]{1,0:T(8,128)} %bitcast.23), custom_call_target="tpu_custom_call" | custom-call | tf_op jit(solution)/shard_map/block/pallas_call | solution.py:275
  2.6 0.0 copy-start.2
  2.6 0.0 copy-start.3
  2.6 7.7 %all-to-all-start = ((bf16[16,288,128]{2,1,0:T(8,128)(2,1)}), bf16[16,288,128]{2,1,0:T(8,128)(2,1)S(1)}, u32[]{:S(2)}, u32[]{:S(2)}) async-start(bf16[16,288,128]{2,1,0:T(8,128)(2,1)} %block.1), calls=%async_computation | async-start | bytes 2359296 | tf_op jit(solution)/shard_map/all_to_all | solution.py:283
  10.4 0.0 copy-start.1
  10.4 0.0 copy-done.2
  10.4 0.2 copy.10
  10.7 0.1 pad_add_fusion.place
  10.8 0.0 copy-done.3
  10.8 0.1 copy_bitcast_fusion.1
  10.9 16.9 %all-to-all-done.own_b = bf16[16,288,128]{2,1,0:T(8,128)(2,1)S(1)} async-done(((bf16[16,288,128]{2,1,0:T(8,128)(2,1)}), bf16[16,288,128]{2,1,0:T(8,128)(2,1)S(1)}, u32[]{:S(2)}, u32[]{:S(2)}) %all-to-all-start) | async-done | bytes 1179680 | tf_op jit(solution)/shard_map/all_to_all | solution.py:283
  27.8 2.8 %collective-permute-start = (bf16[16,288,128]{2,1,0:T(8,128)(2,1)S(1)}, bf16[16,288,128]{2,1,0:T(8,128)(2,1)S(1)}, u32[]{:S(2)}, u32[]{:S(2)}) collective-permute-start(bf16[16,288,128]{2,1,0:T(8,128)(2,1)S(1)} %all-to-all-done.own_b), channel_id=1, source_target_pairs={{0,8},{8,0},{16,24},{24,16},{32,40},{40,32},{48,56},{56,48},{64,72... | collective-permute-start | bytes 3538952 | tf_op jit(solution)/shard_map/ppermute | solution.py:287
  30.5 2.5 %collective-permute-done.other_b = bf16[16,288,128]{2,1,0:T(8,128)(2,1)S(1)} collective-permute-done((bf16[16,288,128]{2,1,0:T(8,128)(2,1)S(1)}, bf16[16,288,128]{2,1,0:T(8,128)(2,1)S(1)}, u32[]{:S(2)}, u32[]{:S(2)}) %collective-permute-start) | collective-permute-done | bytes 1179680 | tf_op jit(solution)/shard_map/ppermute | solution.py:287
  33.0 0.0 copy-done.1
  33.0 6.7 %match.1 = (bf16[4,1024,1024]{2,1,0:T(8,128)(2,1)}, f32[16,128,128]{2,1,0:T(8,128)}, f32[16,128,128]{2,1,0:T(8,128)}, f32[16,8,128]{2,1,0:T(8,128)}) custom-call(s32[2]{0:T(128)S(1)} %pad_add_fusion.place, bf16[16,288,128]{2,1,0:T(8,128)(2,1)S(1)} %all-to-all-done.own_b, bf16[16,288,128]{2,1,0:T(8,128)(2,1)S(1)} %collective-permute-done.other_b, ...), custom_call_target="tpu_custom_call" | custom-call | flops 3221225472 | bytes 12582912 | tf_op jit(solution)/shard_map/match/pallas_call | solution.py:290
  39.7 0.5 collective-permute-start.1
  40.2 8.6 %all-to-all-start.1 = ((f32[16,8,128]{2,1,0:T(8,128)}), f32[16,8,128]{2,1,0:T(8,128)S(1)}, u32[]{:S(2)}, u32[]{:S(2)}) async-start(f32[16,8,128]{2,1,0:T(8,128)} %get-tuple-element.26), calls=%async_computation.1 | async-start | bytes 131072 | tf_op jit(solution)/shard_map/all_to_all | solution.py:312
  48.8 0.0 collective-permute-done.1.other
  48.8 0.0 copy-start
  48.8 1.2 %copy-done = f32[16,128,128]{2,1,0:T(8,128)S(1)} copy-done((f32[16,128,128]{2,1,0:T(8,128)S(1)}, f32[16,128,128]{2,1,0:T(8,128)}, u32[]{:S(2)}) %copy-start) | copy-done | bytes 1048600
  50.1 0.5 scale.1
  50.5 0.9 %convert_element_type.9 = f16[16,144,128]{2,1,0:T(8,128)(2,1)} convert(f32[16,144,128]{2,1,0:T(8,128)S(1)} %get-tuple-element.25) | non-fusion elementwise | flops 294912 | bytes 1769472 | tf_op jit(solution)/shard_map/convert_element_type | solution.py:323
  51.5 4.5 %all-to-all-done.1.lost = f32[16,8,128]{2,1,0:T(8,128)S(1)} async-done(((f32[16,8,128]{2,1,0:T(8,128)}), f32[16,8,128]{2,1,0:T(8,128)S(1)}, u32[]{:S(2)}, u32[]{:S(2)}) %all-to-all-start.1) | async-done | bytes 65568 | tf_op jit(solution)/shard_map/all_to_all | solution.py:312
  56.0 0.7 broadcast_dynamic-update-slice_fusion
  56.7 10.8 %all-to-all-start.2 = ((f16[16,144,128]{2,1,0:T(8,128)(2,1)}), f16[16,144,128]{2,1,0:T(8,128)(2,1)S(1)}, u32[]{:S(2)}, u32[]{:S(2)}) async-start(f16[16,144,128]{2,1,0:T(8,128)(2,1)} %broadcast_dynamic-update-slice_fusion), calls=%async_computation.2 | async-start | bytes 1179648 | tf_op jit(solution)/shard_map/all_to_all | solution.py:336
  67.5 3.0 %grads.1 = f32[128,1024]{1,0:T(8,128)S(1)} custom-call(s32[2]{0:T(128)S(1)} %pad_add_fusion.place, bf16[16,288,128]{2,1,0:T(8,128)(2,1)S(1)} %all-to-all-done.own_b, bf16[16,288,128]{2,1,0:T(8,128)(2,1)S(1)} %collective-permute-done.other_b, bf16[4,1024,1024]{2,1,0:T(8,128)(2,1)} %get-tuple-element.31.weighted), custom_call_target="tpu_custom_call" | custom-call | flops 1073741824 | bytes 10485760 | tf_op jit(solution)/shard_map/grads/pallas_call | solution.py:337
  70.5 0.1 copy.14
  70.6 1.0 %copy.11 = f32[128,8,128]{0,1,2:T(8,128)} copy(f32[128,8,128]{2,1,0:T(8,128)S(1)} %bitcast.25) | data formatting | bytes 1048576 | tf_op jit(solution)/shard_map/reshape | solution.py:347
  71.7 7.0 %all-to-all-done.2 = f16[16,144,128]{2,1,0:T(8,128)(2,1)S(1)} async-done(((f16[16,144,128]{2,1,0:T(8,128)(2,1)}), f16[16,144,128]{2,1,0:T(8,128)(2,1)S(1)}, u32[]{:S(2)}, u32[]{:S(2)}) %all-to-all-start.2) | async-done | bytes 589856 | tf_op jit(solution)/shard_map/all_to_all | solution.py:336
  78.7 0.1 convert_element_type.11.back
  78.7 0.9 %final.1 = (f32[128,128]{1,0:T(8,128)}, f32[8,128]{1,0:T(8,128)S(1)}) custom-call(f32[16,144,128]{2,1,0:T(8,128)S(1)} %convert_element_type.11.back), custom_call_target="tpu_custom_call" | custom-call | tf_op jit(solution)/shard_map/final/pallas_call | solution.py:348
  79.6 0.5 slice.3
  (3 shorter events, 0.1 us)
Async XLA Ops:
  2.6 7.8 %copy-start.2 = (bf16[128,8,128]{2,1,0:T(8,128)(2,1)S(1)}, bf16[128,8,128]{2,1,0:T(8,128)(2,1)}, u32[]{:S(2)}) copy-start(bf16[128,8,128]{2,1,0:T(8,128)(2,1)} %param.7) | copy-start | bytes 786436
  2.6 8.2 %copy-start.3 = (bf16[128,8,128]{2,1,0:T(8,128)(2,1)S(1)}, bf16[128,8,128]{2,1,0:T(8,128)(2,1)}, u32[]{:S(2)}) copy-start(bf16[128,8,128]{2,1,0:T(8,128)(2,1)} %param.5) | copy-start | bytes 786436
  2.6 25.1 %all-to-all-start = ((bf16[16,288,128]{2,1,0:T(8,128)(2,1)}), bf16[16,288,128]{2,1,0:T(8,128)(2,1)S(1)}, u32[]{:S(2)}, u32[]{:S(2)}) async-start(bf16[16,288,128]{2,1,0:T(8,128)(2,1)} %block.1), calls=%async_computation | async-start | bytes 2359296 | tf_op jit(solution)/shard_map/all_to_all | solution.py:283
  10.4 22.7 %copy-start.1 = (f32[128,8]{0,1:T(8,128)S(1)}, f32[128,8]{0,1:T(8,128)}, u32[]{:S(2)}) copy-start(f32[128,8]{0,1:T(8,128)} %param.9) | copy-start | bytes 12292
  27.8 5.3 %collective-permute-start = (bf16[16,288,128]{2,1,0:T(8,128)(2,1)S(1)}, bf16[16,288,128]{2,1,0:T(8,128)(2,1)S(1)}, u32[]{:S(2)}, u32[]{:S(2)}) collective-permute-start(bf16[16,288,128]{2,1,0:T(8,128)(2,1)S(1)} %all-to-all-done.own_b), channel_id=1, source_target_pairs={{0,8},{8,0},{16,24},{24,16},{32,40},{40,32},{48,56},{56,48},{64,72... | collective-permute-start | bytes 3538952 | tf_op jit(solution)/shard_map/ppermute | solution.py:287
  39.7 9.1 %collective-permute-start.1 = (f32[16,128,128]{2,1,0:T(8,128)}, f32[16,128,128]{2,1,0:T(8,128)S(1)}, u32[]{:S(2)}, u32[]{:S(2)}) collective-permute-start(f32[16,128,128]{2,1,0:T(8,128)} %get-tuple-element.24), channel_id=1, source_target_pairs={{0,8},{8,0},{16,24},{24,16},{32,40},{40,32},{48,56},{56,48},{64,72... | collective-permute-start | bytes 3145736 | tf_op jit(solution)/shard_map/ppermute | solution.py:314
  40.2 15.8 %all-to-all-start.1 = ((f32[16,8,128]{2,1,0:T(8,128)}), f32[16,8,128]{2,1,0:T(8,128)S(1)}, u32[]{:S(2)}, u32[]{:S(2)}) async-start(f32[16,8,128]{2,1,0:T(8,128)} %get-tuple-element.26), calls=%async_computation.1 | async-start | bytes 131072 | tf_op jit(solution)/shard_map/all_to_all | solution.py:312
  48.8 1.2 %copy-start = (f32[16,128,128]{2,1,0:T(8,128)S(1)}, f32[16,128,128]{2,1,0:T(8,128)}, u32[]{:S(2)}) copy-start(f32[16,128,128]{2,1,0:T(8,128)} %get-tuple-element.23.own) | copy-start | bytes 3145732
  56.7 22.0 %all-to-all-start.2 = ((f16[16,144,128]{2,1,0:T(8,128)(2,1)}), f16[16,144,128]{2,1,0:T(8,128)(2,1)S(1)}, u32[]{:S(2)}, u32[]{:S(2)}) async-start(f16[16,144,128]{2,1,0:T(8,128)(2,1)} %broadcast_dynamic-update-slice_fusion), calls=%async_computation.2 | async-start | bytes 1179648 | tf_op jit(solution)/shard_map/all_to_all | solution.py:336

commit v5 on v4

v5 whole, which is shorter than its diff:
```python
import functools
import math

import jax
import jax.numpy as jnp
from jax import lax
from jax.experimental import pallas as pl
from jax.experimental.pallas import tpu as pltpu
from jax.sharding import PartitionSpec as P

NEG = -1e30
LOG2E = math.log2(math.e)
TINY = 1e-30
FULL, SMALL, MATCH = 60 << 20, 8 << 20, 40 << 20


def dot(a, b):
    return jnp.dot(a, b, preferred_element_type=jnp.float32)


def dot_nt(a, b):
    return lax.dot_general(a, b, (((1,), (1,)), ((), ())), preferred_element_type=jnp.float32)


def pieces(x):
    high = x.astype(jnp.bfloat16)
    rest = x - high.astype(jnp.float32)
    mid = rest.astype(jnp.bfloat16)
    return high, mid, (rest - mid.astype(jnp.float32)).astype(jnp.bfloat16)


def exponent(x):
    return jnp.floor(jnp.log2(jnp.maximum(x, TINY)))


def block_kernel(keys, b_rows, log_decay, out):
    high, mid, low = pieces(log_decay[...])
    down = jnp.concatenate([high, mid, low, jnp.zeros((8, 128), jnp.bfloat16)], axis=0)
    key_cols, b_cols = keys[...].T, b_rows[...].T
    for k in range(out.shape[0]):
        out[k, 0:128] = key_cols
        out[k, 128:256] = b_cols
        out[k, 256:288] = down


def match_kernel(scale2, group, place, own_b, other_b, own_qc, got_qc, own_sum, other_sum, keep, give, loss,
                 scores, peak, total, fade, log_fade, key_fade, key_log, sums_to, weighted, lost):
    chip, core, upper = place[0], place[1], place[2]
    chips, heads, half = own_b.shape[0], own_qc.shape[1], own_qc.shape[2]
    rows = heads * half
    q_c = (own_qc, got_qc)
    chip_of = (chip, chips - 1 - chip)
    core_of = (core, 1 - core)

    u = lax.broadcasted_iota(jnp.int32, (128, 128), 0)
    v = lax.broadcasted_iota(jnp.int32, (128, 128), 1)
    after = jnp.where(u > v, 1.0, 0.0).astype(jnp.bfloat16)
    upto = jnp.where(u <= v, 1.0, 0.0).astype(jnp.bfloat16)
    ones = jnp.ones((128, 128), jnp.bfloat16)

    def sums(ref, matrix):
        y = dot(ref[:, 256:288].reshape(chips * 32, 128), matrix).reshape(chips, 32, 128)
        y = (y[:, 0:8] + y[:, 8:16] + y[:, 16:24]) * LOG2E
        return jnp.where(upper == 0, y, jnp.concatenate([y[:, 4:8], y[:, 0:4]], axis=1))

    tails = sums(own_b, after), sums(other_b, after)
    whole = sums(own_b, ones), sums(other_b, ones)
    heads_of = sums(own_b, upto), sums(other_b, upto)
    low = jnp.where(core == 0, whole[0], whole[1])
    high = jnp.where(core == 0, whole[1], whole[0])
    for side in range(2):
        sums_to[side] = heads_of[side]
    for s in range(2):
        columns = jnp.concatenate([sums_to[s, chip_of[s]], jnp.zeros((120, 128), jnp.float32)], axis=0).T
        for h in range(heads):
            row_log = jnp.broadcast_to(columns[:, h : h + 1], (half, 128))
            log_fade[s, h] = row_log
            fade[s, h] = jnp.exp2(row_log)
        behind = jnp.zeros((8, 128), jnp.float32)
        for k in range(chips - 1, -1, -1):
            before, same = chip_of[s] > k, chip_of[s] == k
            for side in range(2):
                is_low = core == side
                more = behind + jnp.where(is_low, high[k], 0.0)
                logs = tails[side][k] + jnp.where(before, more, 0.0)
                if side == s:
                    logs = jnp.where(before, logs, -heads_of[side][k])
                key_log[s, 2 * k + side] = logs
                key_fade[s, 2 * k + side] = jnp.exp2(jnp.minimum(logs, 0.0))
            here = jnp.where(core_of[s] == 1, low[k], 0.0)
            behind = behind + jnp.where(before, low[k] + high[k], jnp.where(same, here, 0.0))

    def wide(x):
        return jnp.concatenate([x] * (2 * group), axis=1)

    def of_group(p, first):
        return jnp.concatenate(
            [ref[group * p + i, first : first + 128] for i in range(group) for ref in (own_b, other_b)], axis=1
        )

    def causal(s, p):
        other = (1 - 2 * core) * (1 - 2 * s)
        apart = [
            2 * (group * p + i - chip_of[s]) + (0 if side == s else other) for i in range(group) for side in range(2)
        ]
        return jnp.concatenate([u - v >= 128 * x for x in apart], axis=1)

    peak[...] = jnp.full_like(peak, NEG)
    total[...] = jnp.zeros_like(total)
    lost[...] = jnp.zeros_like(lost)
    keep[...] = jnp.zeros_like(keep)
    give[...] = jnp.zeros_like(give)
    own_sum[...] = jnp.zeros_like(own_sum)
    other_sum[...] = jnp.zeros_like(other_sum)

    def score(s, p, masked):
        x_all = dot(q_c[s][0].reshape(rows, 128), of_group(p, 0)) * scale2
        seen = causal(s, p) if masked else None
        for h in range(heads):
            at = slice(h * half, h * half + half)
            x = x_all[at]
            if masked:
                x = jnp.where(seen, x, NEG)
            scores[s, p, at] = x
            parts = [x[:, 128 * i : 128 * i + 128] for i in range(2 * group)]
            old = peak[s, h]
            top = functools.reduce(jnp.maximum, parts, old)
            total[s, h] = total[s, h] * jnp.exp2(old - top) + sum(jnp.exp2(y - top) for y in parts)
            peak[s, h] = top

    def step(s, p, masked):
        kept = [2 * group * p + i for i in range(2 * group)]
        b_cols = of_group(p, 128)
        inner = dot(q_c[s][1].reshape(rows, 128), b_cols)
        seen = causal(s, p) if masked else None
        squares = jnp.zeros((8, 128), jnp.float32)
        for h in range(heads):
            at = slice(h * half, h * half + half)
            teacher = jnp.exp2(scores[s, p, at] - wide(peak[s, h]))
            if masked:
                logs = wide(log_fade[s, h]) + jnp.concatenate([key_log[s, k, h : h + 1] for k in kept], axis=1)
                decay = jnp.exp2(jnp.where(seen, logs, NEG))
            else:
                decay = wide(fade[s, h]) * jnp.concatenate([key_fade[s, k, h : h + 1] for k in kept], axis=1)
            mismatch = inner[at] * decay - teacher
            square = jnp.sum((mismatch * mismatch).reshape(half // 8, 8, 256 * group), axis=0)
            for i in range(2 * group):
                squares = squares + square[:, 128 * i : 128 * i + 128]
            weighted[at] = (mismatch * decay).astype(jnp.bfloat16)
        lost[...] += squares
        c_cols = jnp.concatenate([q_c[s][1, h].T for h in range(heads)], axis=1)
        parts = dot(c_cols, weighted[...])
        for i in range(group):
            own_sum[group * p + i] += parts[:, 256 * i : 256 * i + 128]
            other_sum[group * p + i] += parts[:, 256 * i + 128 : 256 * i + 256]
        to = (keep, give)[s]
        to[...] += 2.0 * dot_nt(b_cols, weighted[...])

    for s in range(2):
        full = chip_of[s] // group

        @pl.loop(0, full)
        def _(p):
            score(s, p, False)

        score(s, full, True)

    for s in range(2):
        for h in range(heads):
            top = jnp.max(peak[s, h], axis=1, keepdims=True)
            summed = jnp.sum(total[s, h] * jnp.exp2(peak[s, h] - top), axis=1, keepdims=True)
            peak[s, h] = jnp.broadcast_to(top + jnp.log2(summed), (half, 128))

    for s in range(2):
        full = chip_of[s] // group

        @pl.loop(0, full)
        def _(p):
            step(s, p, False)

        step(s, full, True)

    loss[...] = jnp.broadcast_to(jnp.sum(lost[...], keepdims=True)[None], loss.shape)


def scale_kernel(own, other, sent, power):
    blocks = own.shape[0]
    top = jnp.zeros((128, 128), jnp.float32)
    for k in range(blocks):
        x = own[k] + other[k]
        sent[k, 0:128] = x
        top = jnp.maximum(top, jnp.abs(x))
    level = exponent(jnp.broadcast_to(jnp.max(top, keepdims=True), (128, 128)))
    up = jnp.exp2(13.0 - level)
    for k in range(blocks):
        sent[k, 0:128] = sent[k, 0:128] * up
        sent[k, 128:144] = jnp.zeros((16, 128), jnp.float32)
    power[...] = level[0:8]


def extra_kernel(lost, power, extra):
    total = jnp.broadcast_to(jnp.sum(lost[...], axis=0), (8, 128))
    lost_power = exponent(total)
    share = total * jnp.exp2(-lost_power)
    coarse = jnp.floor(share * 1024.0) * (1.0 / 1024.0)
    lane = lax.broadcasted_iota(jnp.int32, (8, 128), 1)
    row = jnp.where(lane == 0, power[...], 0.0)
    row = jnp.where(lane == 1, lost_power, row)
    row = jnp.where(lane == 2, coarse, row)
    row = jnp.where(lane == 3, (share - coarse) * 1024.0, row)
    extra[...] = jnp.concatenate([row, row], axis=0)


def final_kernel(count, back, grad_b, mean):
    blocks = back.shape[0]
    total = jnp.zeros((128, 128), jnp.float32)
    loss = jnp.zeros((1, 128), jnp.float32)
    for k in range(blocks):
        extra = back[k, 128:129]
        power = jnp.broadcast_to(extra[:, 0:1], (1, 128))
        total = total + back[k, 0:128] * jnp.exp2(power - 13.0)
        share = extra[:, 2:3] + extra[:, 3:4] * (1.0 / 1024.0)
        loss = loss + jnp.broadcast_to(share * jnp.exp2(extra[:, 1:2]), (1, 128))
    grad_b[...] = 2.0 * total.T
    mean[0, 0] = jnp.max(loss) * (1.0 / count)


def shards(queries, keys, c_proj, b_proj, log_decay):
    rows_dev, heads, size = queries.shape
    peers = lax.axis_size("context")
    z_size = lax.axis_size("head")
    chips = peers // 2
    rows = heads * rows_dev // 2
    group = 4
    here = lax.axis_index("context")
    upper = here // chips
    place = jnp.stack([here // 2, here % 2, upper]).astype(jnp.int32)
    scale2 = LOG2E / math.sqrt(size)
    plane = [[2 * k + c for k in range(chips)] for c in range(2)]
    swap = [(i, i ^ 1) for i in range(peers)]
    mirror = [(i, peers - 1 - i) for i in range(peers)]

    f32 = functools.partial(jax.ShapeDtypeStruct, dtype=jnp.float32)
    bf16 = functools.partial(jax.ShapeDtypeStruct, dtype=jnp.bfloat16)
    smem = pl.BlockSpec(memory_space=pltpu.SMEM)
    vmem = pl.BlockSpec(memory_space=pltpu.VMEM)
    work = rows * peers * 128
    steps = chips // group
    width = 256 * group

    down = log_decay.T
    block = pl.pallas_call(
        block_kernel,
        out_shape=bf16((chips, 288, 128)),
        in_specs=[vmem] * 3,
        out_specs=vmem,
        compiler_params=pltpu.CompilerParams(vmem_limit_bytes=FULL),
        name="block",
    )(keys[:, 0], b_proj[:, 0], down)
    own_b = lax.all_to_all(block, "context", 0, 0, axis_index_groups=plane)
    q_c = jnp.stack([queries, c_proj]).transpose(0, 2, 1, 3).reshape(2, 2, heads // 2, rows_dev, size)
    own_qc = jnp.where(upper == 0, q_c[:, 0], q_c[:, 1])
    got_qc = lax.ppermute(jnp.where(upper == 0, q_c[:, 1], q_c[:, 0]), "context", mirror)
    own_b, own_qc, got_qc, place = lax.optimization_barrier((own_b, own_qc, got_qc, place))
    other_b = lax.ppermute(own_b, "context", swap)

    tile = pltpu.VMEM((2, heads // 2, rows_dev, 128), jnp.float32)
    own_sum, other_sum, keep, give, lost = pl.pallas_call(
        functools.partial(match_kernel, scale2, group),
        out_shape=(f32((chips, size, 128)),) * 2
        + (f32((size, rows)),) * 2
        + (pltpu.MemorySpace.HBM((2 * z_size, 1, 128), jnp.float32),),
        in_specs=[smem] + [vmem] * 4,
        out_specs=(vmem,) * 4 + (pl.BlockSpec((2 * z_size, 1, 128), lambda: (0, 0, 0)),),
        scratch_shapes=[pltpu.VMEM((2, steps, rows, width), jnp.float32)]
        + [tile] * 4
        + [pltpu.VMEM((2, peers, 8, 128), jnp.float32)] * 2
        + [pltpu.VMEM((2, chips, 8, 128), jnp.float32), pltpu.VMEM((rows, width), jnp.bfloat16)]
        + [pltpu.VMEM((8, 128), jnp.float32)],
        compiler_params=pltpu.CompilerParams(vmem_limit_bytes=MATCH),
        cost_estimate=pl.CostEstimate(flops=6 * work * size, bytes_accessed=6 << 20, transcendentals=3 * work),
        name="match",
    )(place, own_b, other_b, own_qc, got_qc)

    columns = [[(2 * k + c) * z_size + z for c in range(2) for z in range(z_size)] for k in range(chips)]
    lost = lax.all_to_all(lost, ("context", "head"), 0, 0, axis_index_groups=columns)

    other_sum = lax.ppermute(other_sum, "context", swap)
    sent, power = pl.pallas_call(
        scale_kernel,
        out_shape=(f32((chips, 144, 128)), f32((8, 128))),
        in_specs=[vmem] * 2,
        out_specs=(vmem,) * 2,
        compiler_params=pltpu.CompilerParams(vmem_limit_bytes=SMALL),
        name="scale",
    )(own_sum, other_sum)
    sent, lost = lax.optimization_barrier((sent.astype(jnp.float16), lost))

    extra = pl.pallas_call(
        extra_kernel,
        out_shape=f32((16, 128)),
        in_specs=[vmem] * 2,
        out_specs=vmem,
        compiler_params=pltpu.CompilerParams(vmem_limit_bytes=SMALL),
        name="extra",
    )(lost, power)

    extra = jnp.broadcast_to(extra.astype(jnp.float16), (chips, 16, 128))
    sent = lax.dynamic_update_slice(sent, extra, (0, 128, 0))
    back = lax.all_to_all(sent, "context", 0, 0, axis_index_groups=plane)
    back_c = lax.ppermute(give, "context", mirror)
    grad_c = jnp.concatenate(
        [jnp.where(upper == 0, keep, back_c), jnp.where(upper == 0, back_c, keep)], axis=1
    )
    grad_c = grad_c.reshape(size, heads, rows_dev).transpose(2, 1, 0)
    mine, mean = pl.pallas_call(
        functools.partial(final_kernel, heads * z_size * peers * rows_dev),
        out_shape=(f32((rows_dev, size)), f32((1, 1))),
        in_specs=[vmem],
        out_specs=(vmem, smem),
        compiler_params=pltpu.CompilerParams(vmem_limit_bytes=SMALL),
        name="final",
    )(back.astype(jnp.float32))
    return mean[0, 0], grad_c, mine[:, None, :]


def solution(mesh):
    in_specs = (
        P("context", "head", None),
        P("context", "head", None),
        P("context", "head", None),
        P("context", "head", None),
        P("context", "head"),
    )
    out_specs = (P(), P("context", "head", None), P("context", "head", None))
    return jax.shard_map(shards, mesh=mesh, in_specs=in_specs, out_specs=out_specs, check_vma=False)
```

time: 80.6 us -> 83 us (1.030)
  waiting for transfers between devices: 30.8 us -> 34.5 us
  Pallas kernels: 13.1 us -> 16.1 us
  starting transfers between devices: 30.4 us -> 28.1 us
  local copies, waits for them, and re-layouts: 3.91 us -> 1.88 us
    ppermute x0 -> x2, waiting for transfers between devices: none -> 18.3 us  [the longest x1 18.1 us: shards(): lax.ppermute(jnp.where(upper == 0, q_c[:, 1], q_c[:, 0]), 'context', mirror)]
    all_to_all x1, waiting for transfers between devices: 16.9 us -> 0.01 us  [shards(): own_b = lax.all_to_all(block, 'context', 0, 0, axis_index_groups=plane)]
    ppermute x0 -> x2, starting transfers between devices: none -> 7.56 us  [the longest x1 5.88 us: shards(): lax.ppermute(jnp.where(upper == 0, q_c[:, 1], q_c[:, 0]), 'context', mirror)]
    all_to_all x1, starting transfers between devices: 10.8 us -> 3.58 us  [shards(): back = lax.all_to_all(sent, 'context', 0, 0, axis_index_groups=plane)]
    pallas_call x2 -> x1, Pallas kernels: 9.71 us -> 12.7 us  [shards(): pl.pallas_call(functools.partial(match_kernel, scale2, group), out_shape=...]
    all_to_all x1, waiting for transfers between devices: 6.99 us -> 9.82 us  [shards(): back = lax.all_to_all(sent, 'context', 0, 0, axis_index_groups=plane)]
    ppermute x1, starting transfers between devices: 2.79 us -> 0.25 us  [shards(): other_b = lax.ppermute(own_b, 'context', swap)]
    unnamed x10 -> x5, local copies, waits for them, and re-layouts: 1.37 us -> 0.1 us
  transfers between devices with their start and end apart: 5 -> 7, of which waited for: 4 -> 5; matrix products, arithmetic and copies ran while one was open for 3% -> 4% of each run, Pallas kernels for 4% -> 1%
where the time goes in v5:
time: 83 us; the launch traced here: 82.6 us
  waiting for transfers between devices  34.5 us (42%)
  starting transfers between devices  28.1 us (34%)
  Pallas kernels  16.1 us (19%)
  local copies, waits for them, and re-layouts  1.88 us (2%)
  other arithmetic  1.23 us (1%)
    ppermute x1, waiting for transfers between devices, shards(): lax.ppermute(jnp.where(upper == 0, q_c[:, 1], q_c[:, 0]), 'context', mirror)  18.1 us
    pallas_call x1, Pallas kernels, shards(): pl.pallas_call(functools.partial(match_kernel, scale2, group), out_shape=...  12.7 us
    all_to_all x1, waiting for transfers between devices, shards(): back = lax.all_to_all(sent, 'context', 0, 0, axis_index_groups=plane)  9.82 us
    all_to_all x1, starting transfers between devices, shards(): lax.all_to_all(lost, ('context', 'head'), 0, 0, axis_index_groups=columns)  8.73 us
    all_to_all x1, starting transfers between devices, shards(): own_b = lax.all_to_all(block, 'context', 0, 0, axis_index_groups=plane)  7.72 us
    ppermute x1, starting transfers between devices, shards(): lax.ppermute(jnp.where(upper == 0, q_c[:, 1], q_c[:, 0]), 'context', mirror)  5.88 us
    all_to_all x1, waiting for transfers between devices, shards(): lax.all_to_all(lost, ('context', 'head'), 0, 0, axis_index_groups=columns)  3.85 us
    all_to_all x1, starting transfers between devices, shards(): back = lax.all_to_all(sent, 'context', 0, 0, axis_index_groups=plane)  3.58 us
  transfers between devices with their start and end apart: 7, of which 5 were waited for; matrix products, arithmetic and copies ran while one was open for 4% of the time, Pallas kernels for 1%

profile of v5, /device:TPU:1, one launch (start us, length us, event | category | flops | bytes accessed | tf_op | source)
XLA Modules:
  0.0 82.6 jit_solution(414049078774025025)
XLA Ops:
  0.6 2.0 %block.1 = bf16[16,288,128]{2,1,0:T(8,128)(2,1)} custom-call(bf16[128,128]{1,0:T(8,128)(2,1)} %bitcast.40, bf16[128,128]{1,0:T(8,128)(2,1)} %bitcast.41, f32[8,128]{1,0:T(8,128)} %bitcast.42), custom_call_target="tpu_custom_call" | custom-call | tf_op jit(solution)/shard_map/block/pallas_call | solution.py:252
  2.6 0.0 copy-start
  2.6 0.0 copy-start.1
  2.6 7.7 %all-to-all-start = ((bf16[16,288,128]{2,1,0:T(8,128)(2,1)}), bf16[16,288,128]{2,1,0:T(8,128)(2,1)S(1)}, u32[]{:S(2)}, u32[]{:S(2)}) async-start(bf16[16,288,128]{2,1,0:T(8,128)(2,1)} %block.1), calls=%async_computation | async-start | bytes 2359296 | tf_op jit(solution)/shard_map/all_to_all | solution.py:260
  10.4 0.0 copy-done
  10.4 0.0 copy-done.1
  10.4 0.1 copy_bitcast_fusion
  10.5 0.1 pad_maximum_fusion
  10.6 5.9 %collective-permute-start = (bf16[2,4,128,128]{3,2,1,0:T(8,128)(2,1)S(1)}, bf16[2,4,128,128]{3,2,1,0:T(8,128)(2,1)S(1)}, u32[]{:S(2)}, u32[]{:S(2)}) collective-permute-start(bf16[2,4,128,128]{3,2,1,0:T(8,128)(2,1)S(1)} %get-tuple-element.41), channel_id=1, source_target_pairs={{0,248},{8,240},{16,232},{24,224},{32,216},{40,208},{48,200},{56,1... | collective-permute-start | bytes 786440 | tf_op jit(solution)/shard_map/ppermute | solution.py:263
  16.5 0.1 pad_add_fusion.place
  16.6 18.1 %collective-permute-done.got_qc = bf16[2,4,128,128]{3,2,1,0:T(8,128)(2,1)S(1)} collective-permute-done((bf16[2,4,128,128]{3,2,1,0:T(8,128)(2,1)S(1)}, bf16[2,4,128,128]{3,2,1,0:T(8,128)(2,1)S(1)}, u32[]{:S(2)}, u32[]{:S(2)}) %collective-permute-start) | collective-permute-done | bytes 262176 | tf_op jit(solution)/shard_map/ppermute | solution.py:263
  34.6 0.0 all-to-all-done.own_b
  34.6 0.2 collective-permute-start.1
  34.9 2.6 %collective-permute-done.1.other_b = bf16[16,288,128]{2,1,0:T(8,128)(2,1)S(1)} collective-permute-done((bf16[16,288,128]{2,1,0:T(8,128)(2,1)S(1)}, bf16[16,288,128]{2,1,0:T(8,128)(2,1)S(1)}, u32[]{:S(2)}, u32[]{:S(2)}) %collective-permute-start.1) | collective-permute-done | bytes 1179680 | tf_op jit(solution)/shard_map/ppermute | solution.py:265
  37.5 12.7 %match.1 = (f32[16,128,128]{2,1,0:T(8,128)S(1)}, f32[16,128,128]{2,1,0:T(8,128)}, f32[128,512]{1,0:T(8,128)S(1)}, f32[128,512]{1,0:T(8,128)S(1)}, f32[16,1,128]{2,1,0:T(1,128)}) custom-call(s32[3]{0:T(128)S(1)} %pad_add_fusion.place, bf16[16,288,128]{2,1,0:T(8,128)(2,1)S(1)} %all-to-all-done.own_b, bf16[16,288,128]{2,1,0:T(8,128)(2,1)S(1)} %collective-permute-done.1.other_b, ...), custom_call_target="tpu_custom_call" | custom-call | flops 1610612736 | bytes 6291456 | tf_op jit(solution)/shard_map/match/pallas_call | solution.py:268
  50.2 0.3 collective-permute-start.2
  50.5 8.7 %all-to-all-start.1 = ((f32[16,1,128]{2,1,0:T(1,128)}), f32[16,1,128]{2,1,0:T(1,128)S(1)}, u32[]{:S(2)}, u32[]{:S(2)}) async-start(f32[16,1,128]{2,1,0:T(1,128)} %get-tuple-element.25), calls=%async_computation.1 | async-start | bytes 16384 | tf_op jit(solution)/shard_map/all_to_all | solution.py:286
  59.2 1.7 %collective-permute-start.3 = (f32[128,512]{1,0:T(8,128)S(1)}, f32[128,512]{1,0:T(8,128)S(1)}, u32[]{:S(2)}, u32[]{:S(2)}) collective-permute-start(f32[128,512]{1,0:T(8,128)S(1)} %get-tuple-element.31), channel_id=1, source_target_pairs={{0,248},{8,240},{16,232},{24,224},{32,216},{40,208},{48,200},{56,1... | collective-permute-start | bytes 786440 | tf_op jit(solution)/shard_map/ppermute | solution.py:311
  60.9 0.0 collective-permute-done.2.other
  60.9 0.5 scale.1
  61.4 0.9 %convert_element_type.9 = f16[16,144,128]{2,1,0:T(8,128)(2,1)} convert(f32[16,144,128]{2,1,0:T(8,128)S(1)} %get-tuple-element.24) | non-fusion elementwise | flops 294912 | bytes 1769472 | tf_op jit(solution)/shard_map/convert_element_type | solution.py:297
  62.3 3.8 %all-to-all-done.1.lost = f32[16,1,128]{2,1,0:T(1,128)S(1)} async-done(((f32[16,1,128]{2,1,0:T(1,128)}), f32[16,1,128]{2,1,0:T(1,128)S(1)}, u32[]{:S(2)}, u32[]{:S(2)}) %all-to-all-start.1) | async-done | bytes 8224 | tf_op jit(solution)/shard_map/all_to_all | solution.py:286
  66.2 0.7 broadcast_dynamic-update-slice_fusion
  66.8 3.6 %all-to-all-start.2 = ((f16[16,144,128]{2,1,0:T(8,128)(2,1)}), f16[16,144,128]{2,1,0:T(8,128)(2,1)S(1)}, u32[]{:S(2)}, u32[]{:S(2)}) async-start(f16[16,144,128]{2,1,0:T(8,128)(2,1)} %broadcast_dynamic-update-slice_fusion), calls=%async_computation.2 | async-start | bytes 1179648 | tf_op jit(solution)/shard_map/all_to_all | solution.py:310
  70.4 0.2 collective-permute-done.3
  70.7 0.1 copy.18
  70.8 1.0 %copy.14 = f32[128,8,128]{0,1,2:T(8,128)} copy(f32[128,8,128]{2,1,0:T(8,128)S(1)} %bitcast.38) | data formatting | bytes 1048576 | tf_op jit(solution)/shard_map/reshape | solution.py:315
  71.8 9.8 %all-to-all-done.2 = f16[16,144,128]{2,1,0:T(8,128)(2,1)S(1)} async-done(((f16[16,144,128]{2,1,0:T(8,128)(2,1)}), f16[16,144,128]{2,1,0:T(8,128)(2,1)S(1)}, u32[]{:S(2)}, u32[]{:S(2)}) %all-to-all-start.2) | async-done | bytes 589856 | tf_op jit(solution)/shard_map/all_to_all | solution.py:310
  81.7 0.1 convert_element_type.11.back
  81.7 0.9 %final.1 = (f32[128,128]{1,0:T(8,128)}, f32[1,1]{1,0:T(1,128)}) custom-call(f32[16,144,128]{2,1,0:T(8,128)S(1)} %convert_element_type.11.back), custom_call_target="tpu_custom_call" | custom-call | tf_op jit(solution)/shard_map/final/pallas_call | solution.py:316
  (5 shorter events, 0.2 us)
Async XLA Ops:
  2.6 7.7 %copy-start = (bf16[128,8,128]{2,1,0:T(8,128)(2,1)S(1)}, bf16[128,8,128]{2,1,0:T(8,128)(2,1)}, u32[]{:S(2)}) copy-start(bf16[128,8,128]{2,1,0:T(8,128)(2,1)} %param.7) | copy-start | bytes 786436
  2.6 7.8 %copy-start.1 = (bf16[128,8,128]{2,1,0:T(8,128)(2,1)S(1)}, bf16[128,8,128]{2,1,0:T(8,128)(2,1)}, u32[]{:S(2)}) copy-start(bf16[128,8,128]{2,1,0:T(8,128)(2,1)} %param.5) | copy-start | bytes 786436
  2.6 32.0 %all-to-all-start = ((bf16[16,288,128]{2,1,0:T(8,128)(2,1)}), bf16[16,288,128]{2,1,0:T(8,128)(2,1)S(1)}, u32[]{:S(2)}, u32[]{:S(2)}) async-start(bf16[16,288,128]{2,1,0:T(8,128)(2,1)} %block.1), calls=%async_computation | async-start | bytes 2359296 | tf_op jit(solution)/shard_map/all_to_all | solution.py:260
  10.6 24.0 %collective-permute-start = (bf16[2,4,128,128]{3,2,1,0:T(8,128)(2,1)S(1)}, bf16[2,4,128,128]{3,2,1,0:T(8,128)(2,1)S(1)}, u32[]{:S(2)}, u32[]{:S(2)}) collective-permute-start(bf16[2,4,128,128]{3,2,1,0:T(8,128)(2,1)S(1)} %get-tuple-element.41), channel_id=1, source_target_pairs={{0,248},{8,240},{16,232},{24,224},{32,216},{40,208},{48,200},{56,1... | collective-permute-start | bytes 786440 | tf_op jit(solution)/shard_map/ppermute | solution.py:263
  34.6 2.8 %collective-permute-start.1 = (bf16[16,288,128]{2,1,0:T(8,128)(2,1)S(1)}, bf16[16,288,128]{2,1,0:T(8,128)(2,1)S(1)}, u32[]{:S(2)}, u32[]{:S(2)}) collective-permute-start(bf16[16,288,128]{2,1,0:T(8,128)(2,1)S(1)} %all-to-all-done.own_b), channel_id=1, source_target_pairs={{0,8},{8,0},{16,24},{24,16},{32,40},{40,32},{48,56},{56,48},{64,72... | collective-permute-start | bytes 3538952 | tf_op jit(solution)/shard_map/ppermute | solution.py:265
  50.2 10.7 %collective-permute-start.2 = (f32[16,128,128]{2,1,0:T(8,128)}, f32[16,128,128]{2,1,0:T(8,128)S(1)}, u32[]{:S(2)}, u32[]{:S(2)}) collective-permute-start(f32[16,128,128]{2,1,0:T(8,128)} %get-tuple-element.23), channel_id=1, source_target_pairs={{0,8},{8,0},{16,24},{24,16},{32,40},{40,32},{48,56},{56,48},{64,72... | collective-permute-start | bytes 3145736 | tf_op jit(solution)/shard_map/ppermute | solution.py:288
  50.5 15.7 %all-to-all-start.1 = ((f32[16,1,128]{2,1,0:T(1,128)}), f32[16,1,128]{2,1,0:T(1,128)S(1)}, u32[]{:S(2)}, u32[]{:S(2)}) async-start(f32[16,1,128]{2,1,0:T(1,128)} %get-tuple-element.25), calls=%async_computation.1 | async-start | bytes 16384 | tf_op jit(solution)/shard_map/all_to_all | solution.py:286
  59.2 11.4 %collective-permute-start.3 = (f32[128,512]{1,0:T(8,128)S(1)}, f32[128,512]{1,0:T(8,128)S(1)}, u32[]{:S(2)}, u32[]{:S(2)}) collective-permute-start(f32[128,512]{1,0:T(8,128)S(1)} %get-tuple-element.31), channel_id=1, source_target_pairs={{0,248},{8,240},{16,232},{24,224},{32,216},{40,208},{48,200},{56,1... | collective-permute-start | bytes 786440 | tf_op jit(solution)/shard_map/ppermute | solution.py:311
  66.8 14.8 %all-to-all-start.2 = ((f16[16,144,128]{2,1,0:T(8,128)(2,1)}), f16[16,144,128]{2,1,0:T(8,128)(2,1)S(1)}, u32[]{:S(2)}, u32[]{:S(2)}) async-start(f16[16,144,128]{2,1,0:T(8,128)(2,1)} %broadcast_dynamic-update-slice_fusion), calls=%async_computation.2 | async-start | bytes 1179648 | tf_op jit(solution)/shard_map/all_to_all | solution.py:310

commit v6 on v4

--- a/solution.py
+++ b/solution.py
@@ -33,7 +33,15 @@
     return jnp.floor(jnp.log2(jnp.maximum(x, TINY)))
 
 
-def block_kernel(keys, b_rows, log_decay, out):
+def block_kernel(keys_from, b_from, log_from, out, keys, b_rows, log_decay, sems):
+    copies = [
+        pltpu.make_async_copy(x, y, sems.at[i])
+        for i, (x, y) in enumerate(((keys_from, keys), (b_from, b_rows), (log_from, log_decay)))
+    ]
+    for x in copies:
+        x.start()
+    for x in copies:
+        x.wait()
     high, mid, low = pieces(log_decay[...])
     down = jnp.concatenate([high, mid, low, jnp.zeros((8, 128), jnp.bfloat16)], axis=0)
     key_cols, b_cols = keys[...].T, b_rows[...].T
@@ -44,7 +52,7 @@
 
 
 def match_kernel(heads, scale2, group, place, own_b, other_b, q, c, c_cols, log_decay, weighted, own_grad, other_grad, loss,
-                 scores, peak, total, fade, log_fade, key_fade, key_log, held, own_held, other_held, lost, sems):
+                 scores, tops, peak, total, fade, log_fade, key_fade, key_log, held, own_held, other_held, lost, sems):
     chip, core = place[0], place[1]
     chips, half = own_b.shape[0], q.shape[1]
     rows = heads * half
@@ -104,12 +112,15 @@
             x = s[at]
             if masked:
                 x = jnp.where(seen, x, NEG)
-            scores[p, at] = x
             parts = [x[:, 128 * i : 128 * i + 128] for i in range(2 * group)]
             old = peak[h]
             top = functools.reduce(jnp.maximum, parts, old)
-            total[h] = total[h] * jnp.exp2(old - top) + sum(jnp.exp2(y - top) for y in parts)
+            grown = [jnp.exp2(y - top) for y in parts]
+            for i in range(2 * group):
+                scores[p, at, 128 * i : 128 * i + 128] = grown[i]
+            total[h] = total[h] * jnp.exp2(old - top) + sum(grown)
             peak[h] = top
+            tops[p, h] = top
 
     @pl.loop(0, full)
     def _(p):
@@ -126,17 +137,20 @@
     def copies(p):
         part = pl.ds(p * group, group)
         return (
-            pltpu.make_async_copy(held.at[p], weighted.at[p], sems.at[0, p]),
-            pltpu.make_async_copy(own_held.at[part], own_grad.at[part], sems.at[1, p]),
-            pltpu.make_async_copy(other_held.at[part], other_grad.at[part], sems.at[2, p]),
+            pltpu.make_async_copy(own_held.at[part], own_grad.at[part], sems.at[heads, p]),
+            pltpu.make_async_copy(other_held.at[part], other_grad.at[part], sems.at[heads + 1, p]),
         )
+
+    def copy(p, h):
+        at = pl.ds(h * half, half)
+        return pltpu.make_async_copy(held.at[p, at], weighted.at[p, at], sems.at[h, p])
 
     @pl.loop(full + 1, chips // group)
     def _(p):
         for i in range(group):
             own_held[group * p + i] = jnp.zeros((128, 128), jnp.float32)
             other_held[group * p + i] = jnp.zeros((128, 128), jnp.float32)
-        for x in copies(p)[1:]:
+        for x in copies(p):
             x.start()
 
     def step(p, masked):
@@ -146,7 +160,7 @@
         squares = jnp.zeros((8, 128), jnp.float32)
         for h in range(heads):
             at = slice(h * half, h * half + half)
-            teacher = jnp.exp2(scores[p, at] - wide(peak[h]))
+            teacher = scores[p, at] * wide(jnp.exp2(tops[p, h] - peak[h]))
             if masked:
                 logs = wide(log_fade[h]) + jnp.concatenate([key_log[k, h : h + 1] for k in kept], axis=1)
                 decay = jnp.exp2(jnp.where(seen, logs, NEG))
@@ -157,6 +171,7 @@
             for i in range(2 * group):
                 squares = squares + square[:, 128 * i : 128 * i + 128]
             held[p, at] = (mismatch * decay).astype(jnp.bfloat16)
+            copy(p, h).start()
         lost[...] += squares
         parts = dot(c_cols[...], held[p])
         for i in range(group):
@@ -170,17 +185,16 @@
         step(p, False)
 
     step(full, True)
-    mean = jnp.broadcast_to(jnp.sum(lost[...], keepdims=True), (8, 128))
-    for k in range(loss.shape[0]):
-        loss[k] = mean
+    loss[...] = jnp.broadcast_to(jnp.sum(lost[...], keepdims=True)[None], loss.shape)
 
     @pl.loop(0, full + 1)
     def _(p):
-        copies(p)[0].wait()
+        for h in range(heads):
+            copy(p, h).wait()
 
     @pl.loop(0, chips // group)
     def _(p):
-        for x in copies(p)[1:]:
+        for x in copies(p):
             x.wait()
 
 
@@ -221,9 +235,7 @@
 
 
 def extra_kernel(lost, power, extra):
-    total = lost[0]
-    for k in range(1, lost.shape[0]):
-        total = total + lost[k]
+    total = jnp.broadcast_to(jnp.sum(lost[...], axis=0), (8, 128))
     lost_power = exponent(total)
     share = total * jnp.exp2(-lost_power)
     coarse = jnp.floor(share * 1024.0) * (1.0 / 1024.0)
@@ -246,7 +258,7 @@
         share = extra[:, 2:3] + extra[:, 3:4] * (1.0 / 1024.0)
         loss = loss + jnp.broadcast_to(share * jnp.exp2(extra[:, 1:2]), (1, 128))
     grad_b[...] = 2.0 * total.T
-    mean[...] = jnp.broadcast_to(loss * (1.0 / count), (8, 128))
+    mean[0, 0] = jnp.max(loss) * (1.0 / count)
 
 
 def shards(queries, keys, c_proj, b_proj, log_decay):
@@ -266,7 +278,8 @@
     bf16 = functools.partial(jax.ShapeDtypeStruct, dtype=jnp.bfloat16)
     smem = pl.BlockSpec(memory_space=pltpu.SMEM)
     vmem = pl.BlockSpec(memory_space=pltpu.VMEM)
-    hbm = pl.BlockSpec(memory_space=pltpu.MemorySpace.HBM)
+    hbm_out = pltpu.MemorySpace.HBM
+    hbm = pl.BlockSpec(memory_space=hbm_out)
     work = rows * peers * 128
     steps = chips // group
     width = 256 * group
@@ -275,34 +288,36 @@
     block = pl.pallas_call(
         block_kernel,
         out_shape=bf16((chips, 288, 128)),
-        in_specs=[vmem] * 3,
+        in_specs=[hbm] * 3,
         out_specs=vmem,
-        compiler_params=pltpu.CompilerParams(vmem_limit_bytes=FULL),
+        scratch_shapes=[pltpu.VMEM((rows_dev, size), jnp.bfloat16)] * 2
+        + [pltpu.VMEM((heads, rows_dev), jnp.float32), pltpu.SemaphoreType.DMA((3,))],
+        compiler_params=pltpu.CompilerParams(vmem_limit_bytes=SMALL),
         name="block",
-    )(keys[:, 0], b_proj[:, 0], down)
+    )(*(pltpu.with_memory_space_constraint(x, hbm_out) for x in (keys[:, 0], b_proj[:, 0], down)))
     own_b = lax.all_to_all(block, "context", 0, 0, axis_index_groups=plane)
     q, c = queries.transpose(1, 0, 2), c_proj.transpose(1, 0, 2)
     c_cols = c_proj.transpose(2, 1, 0).reshape(size, rows)
     own_b, q, c, c_cols, place = lax.optimization_barrier((own_b, q, c, c_cols, place))
     other_b = lax.ppermute(own_b, "context", swap)
     tile = pltpu.VMEM((heads, rows_dev, 128), jnp.float32)
-    hbm_out = pltpu.MemorySpace.HBM
     weighted, own_sum, other_sum, lost = pl.pallas_call(
         functools.partial(match_kernel, heads, scale2, group),
         out_shape=(
             hbm_out((steps, rows, width), jnp.bfloat16),
             hbm_out((chips, size, 128), jnp.float32),
             hbm_out((chips, size, 128), jnp.float32),
-            hbm_out((2 * z_size, 8, 128), jnp.float32),
+            hbm_out((2 * z_size, 1, 128), jnp.float32),
         ),
         in_specs=[smem] + [vmem] * 6,
-        out_specs=(hbm, hbm, hbm, pl.BlockSpec((2 * z_size, 8, 128), lambda: (0, 0, 0))),
+        out_specs=(hbm, hbm, hbm, pl.BlockSpec((2 * z_size, 1, 128), lambda: (0, 0, 0))),
         scratch_shapes=[pltpu.VMEM((steps, rows, width), jnp.float32)]
+        + [pltpu.VMEM((steps, heads, rows_dev, 128), jnp.float32)]
         + [tile] * 4
         + [pltpu.VMEM((peers, 8, 128), jnp.float32)] * 2
         + [pltpu.VMEM((steps, rows, width), jnp.bfloat16)]
         + [pltpu.VMEM((chips, size, 128), jnp.float32)] * 2
-        + [pltpu.VMEM((8, 128), jnp.float32), pltpu.SemaphoreType.DMA((3, steps))],
+        + [pltpu.VMEM((8, 128), jnp.float32), pltpu.SemaphoreType.DMA((heads + 2, steps))],
         compiler_params=pltpu.CompilerParams(vmem_limit_bytes=MATCH),
         cost_estimate=pl.CostEstimate(flops=6 * work * size, bytes_accessed=12 << 20, transcendentals=3 * work),
         name="match",
@@ -347,9 +362,9 @@
     grad_c = grad_c.reshape(size, heads, rows_dev).transpose(2, 1, 0)
     mine, mean = pl.pallas_call(
         functools.partial(final_kernel, heads * z_size * peers * rows_dev),
-        out_shape=(f32((rows_dev, size)), f32((8, 128))),
+        out_shape=(f32((rows_dev, size)), f32((1, 1))),
         in_specs=[vmem],
-        out_specs=(vmem,) * 2,
+        out_specs=(vmem, smem),
         compiler_params=pltpu.CompilerParams(vmem_limit_bytes=SMALL),
         name="final",
     )(back.astype(jnp.float32))

time: 80.6 us -> 79.5 us (0.986)
  no operation moved by 1% of the time
where the time goes in v6:
time: 79.5 us; the launch traced here: 79.1 us
  waiting for transfers between devices  30.5 us (38%)
  starting transfers between devices  30.4 us (38%)
  Pallas kernels  12.9 us (16%)
  local copies, waits for them, and re-layouts  3.4 us (4%)
  other arithmetic  1.1 us (1%)
    all_to_all x1, waiting for transfers between devices, shards(): own_b = lax.all_to_all(block, 'context', 0, 0, axis_index_groups=plane)  16.9 us
    all_to_all x1, starting transfers between devices, shards(): back = lax.all_to_all(sent, 'context', 0, 0, axis_index_groups=plane)  10.8 us
    all_to_all x1, starting transfers between devices, shards(): lax.all_to_all(lost, ('context', 'head'), 0, 0, axis_index_groups=columns)  8.65 us
    all_to_all x1, starting transfers between devices, shards(): own_b = lax.all_to_all(block, 'context', 0, 0, axis_index_groups=plane)  7.73 us
    all_to_all x1, waiting for transfers between devices, shards(): back = lax.all_to_all(sent, 'context', 0, 0, axis_index_groups=plane)  6.89 us
    pallas_call x1, Pallas kernels, shards(): pl.pallas_call(functools.partial(match_kernel, heads, scale2, group), out...  6.45 us
    all_to_all x1, waiting for transfers between devices, shards(): lax.all_to_all(lost, ('context', 'head'), 0, 0, axis_index_groups=columns)  4.24 us
    pallas_call x1, Pallas kernels, shards(): pl.pallas_call(functools.partial(grad_kernel, group), out_shape=f32((size...  3 us
  transfers between devices with their start and end apart: 5, of which 4 were waited for; matrix products, arithmetic and copies ran while one was open for 3% of the time, Pallas kernels for 4%

profile of v6, /device:TPU:1, one launch (start us, length us, event | category | flops | bytes accessed | tf_op | source)
XLA Modules:
  0.0 79.1 jit_solution(10818097687453953709)
XLA Ops:
  0.6 2.0 %block.1 = bf16[16,288,128]{2,1,0:T(8,128)(2,1)} custom-call(bf16[128,128]{1,0:T(8,128)(2,1)} %bitcast.29, bf16[128,128]{1,0:T(8,128)(2,1)} %bitcast.30, f32[8,128]{1,0:T(8,128)} %bitcast.23), custom_call_target="tpu_custom_call" | custom-call | tf_op jit(solution)/shard_map/block/pallas_call | solution.py:288
  2.7 0.0 copy-start.2
  2.7 0.0 copy-start.3
  2.7 7.7 %all-to-all-start = ((bf16[16,288,128]{2,1,0:T(8,128)(2,1)}), bf16[16,288,128]{2,1,0:T(8,128)(2,1)S(1)}, u32[]{:S(2)}, u32[]{:S(2)}) async-start(bf16[16,288,128]{2,1,0:T(8,128)(2,1)} %block.1), calls=%async_computation | async-start | bytes 2359296 | tf_op jit(solution)/shard_map/all_to_all | solution.py:298
  10.4 0.0 copy-start.1
  10.5 0.0 copy-done.2
  10.5 0.2 copy.10
  10.8 0.1 pad_add_fusion.place
  10.9 0.0 copy-done.3
  10.9 0.1 copy_bitcast_fusion.1
  11.0 16.9 %all-to-all-done.own_b = bf16[16,288,128]{2,1,0:T(8,128)(2,1)S(1)} async-done(((bf16[16,288,128]{2,1,0:T(8,128)(2,1)}), bf16[16,288,128]{2,1,0:T(8,128)(2,1)S(1)}, u32[]{:S(2)}, u32[]{:S(2)}) %all-to-all-start) | async-done | bytes 1179680 | tf_op jit(solution)/shard_map/all_to_all | solution.py:298
  27.8 2.8 %collective-permute-start = (bf16[16,288,128]{2,1,0:T(8,128)(2,1)S(1)}, bf16[16,288,128]{2,1,0:T(8,128)(2,1)S(1)}, u32[]{:S(2)}, u32[]{:S(2)}) collective-permute-start(bf16[16,288,128]{2,1,0:T(8,128)(2,1)S(1)} %all-to-all-done.own_b), channel_id=1, source_target_pairs={{0,8},{8,0},{16,24},{24,16},{32,40},{40,32},{48,56},{56,48},{64,72... | collective-permute-start | bytes 3538952 | tf_op jit(solution)/shard_map/ppermute | solution.py:302
  30.6 2.5 %collective-permute-done.other_b = bf16[16,288,128]{2,1,0:T(8,128)(2,1)S(1)} collective-permute-done((bf16[16,288,128]{2,1,0:T(8,128)(2,1)S(1)}, bf16[16,288,128]{2,1,0:T(8,128)(2,1)S(1)}, u32[]{:S(2)}, u32[]{:S(2)}) %collective-permute-start) | collective-permute-done | bytes 1179680 | tf_op jit(solution)/shard_map/ppermute | solution.py:302
  33.1 0.0 copy-done.1
  33.1 6.5 %match.1 = (bf16[4,1024,1024]{2,1,0:T(8,128)(2,1)}, f32[16,128,128]{2,1,0:T(8,128)}, f32[16,128,128]{2,1,0:T(8,128)}, f32[16,1,128]{2,1,0:T(1,128)}) custom-call(s32[2]{0:T(128)S(1)} %pad_add_fusion.place, bf16[16,288,128]{2,1,0:T(8,128)(2,1)S(1)} %all-to-all-done.own_b, bf16[16,288,128]{2,1,0:T(8,128)(2,1)S(1)} %collective-permute-done.other_b, ...), custom_call_target="tpu_custom_call" | custom-call | flops 3221225472 | bytes 12582912 | tf_op jit(solution)/shard_map/match/pallas_call | solution.py:304
  39.5 0.5 collective-permute-start.1
  40.0 8.7 %all-to-all-start.1 = ((f32[16,1,128]{2,1,0:T(1,128)}), f32[16,1,128]{2,1,0:T(1,128)S(1)}, u32[]{:S(2)}, u32[]{:S(2)}) async-start(f32[16,1,128]{2,1,0:T(1,128)} %get-tuple-element.26), calls=%async_computation.1 | async-start | bytes 16384 | tf_op jit(solution)/shard_map/all_to_all | solution.py:327
  48.6 0.0 collective-permute-done.1.other
  48.7 0.0 copy-start
  48.7 1.2 %copy-done = f32[16,128,128]{2,1,0:T(8,128)S(1)} copy-done((f32[16,128,128]{2,1,0:T(8,128)S(1)}, f32[16,128,128]{2,1,0:T(8,128)}, u32[]{:S(2)}) %copy-start) | copy-done | bytes 1048600
  49.9 0.5 scale.1
  50.4 0.9 %convert_element_type.9 = f16[16,144,128]{2,1,0:T(8,128)(2,1)} convert(f32[16,144,128]{2,1,0:T(8,128)S(1)} %get-tuple-element.25) | non-fusion elementwise | flops 294912 | bytes 1769472 | tf_op jit(solution)/shard_map/convert_element_type | solution.py:338
  51.3 4.2 %all-to-all-done.1.lost = f32[16,1,128]{2,1,0:T(1,128)S(1)} async-done(((f32[16,1,128]{2,1,0:T(1,128)}), f32[16,1,128]{2,1,0:T(1,128)S(1)}, u32[]{:S(2)}, u32[]{:S(2)}) %all-to-all-start.1) | async-done | bytes 8224 | tf_op jit(solution)/shard_map/all_to_all | solution.py:327
  55.6 0.7 broadcast_dynamic-update-slice_fusion
  56.2 10.8 %all-to-all-start.2 = ((f16[16,144,128]{2,1,0:T(8,128)(2,1)}), f16[16,144,128]{2,1,0:T(8,128)(2,1)S(1)}, u32[]{:S(2)}, u32[]{:S(2)}) async-start(f16[16,144,128]{2,1,0:T(8,128)(2,1)} %broadcast_dynamic-update-slice_fusion), calls=%async_computation.2 | async-start | bytes 1179648 | tf_op jit(solution)/shard_map/all_to_all | solution.py:351
  67.1 3.0 %grads.1 = f32[128,1024]{1,0:T(8,128)S(1)} custom-call(s32[2]{0:T(128)S(1)} %pad_add_fusion.place, bf16[16,288,128]{2,1,0:T(8,128)(2,1)S(1)} %all-to-all-done.own_b, bf16[16,288,128]{2,1,0:T(8,128)(2,1)S(1)} %collective-permute-done.other_b, bf16[4,1024,1024]{2,1,0:T(8,128)(2,1)} %get-tuple-element.31.weighted), custom_call_target="tpu_custom_call" | custom-call | flops 1073741824 | bytes 10485760 | tf_op jit(solution)/shard_map/grads/pallas_call | solution.py:352
  70.1 0.1 copy.14
  70.2 1.0 %copy.11 = f32[128,8,128]{0,1,2:T(8,128)} copy(f32[128,8,128]{2,1,0:T(8,128)S(1)} %bitcast.25) | data formatting | bytes 1048576 | tf_op jit(solution)/shard_map/reshape | solution.py:362
  71.2 6.9 %all-to-all-done.2 = f16[16,144,128]{2,1,0:T(8,128)(2,1)S(1)} async-done(((f16[16,144,128]{2,1,0:T(8,128)(2,1)}), f16[16,144,128]{2,1,0:T(8,128)(2,1)S(1)}, u32[]{:S(2)}, u32[]{:S(2)}) %all-to-all-start.2) | async-done | bytes 589856 | tf_op jit(solution)/shard_map/all_to_all | solution.py:351
  78.1 0.1 convert_element_type.11.back
  78.2 0.9 %final.1 = (f32[128,128]{1,0:T(8,128)}, f32[1,1]{1,0:T(1,128)}) custom-call(f32[16,144,128]{2,1,0:T(8,128)S(1)} %convert_element_type.11.back), custom_call_target="tpu_custom_call" | custom-call | tf_op jit(solution)/shard_map/final/pallas_call | solution.py:363
  (3 shorter events, 0.1 us)
Async XLA Ops:
  2.7 7.8 %copy-start.2 = (bf16[128,8,128]{2,1,0:T(8,128)(2,1)S(1)}, bf16[128,8,128]{2,1,0:T(8,128)(2,1)}, u32[]{:S(2)}) copy-start(bf16[128,8,128]{2,1,0:T(8,128)(2,1)} %param.7) | copy-start | bytes 786436
  2.7 8.2 %copy-start.3 = (bf16[128,8,128]{2,1,0:T(8,128)(2,1)S(1)}, bf16[128,8,128]{2,1,0:T(8,128)(2,1)}, u32[]{:S(2)}) copy-start(bf16[128,8,128]{2,1,0:T(8,128)(2,1)} %param.5) | copy-start | bytes 786436
  2.7 25.1 %all-to-all-start = ((bf16[16,288,128]{2,1,0:T(8,128)(2,1)}), bf16[16,288,128]{2,1,0:T(8,128)(2,1)S(1)}, u32[]{:S(2)}, u32[]{:S(2)}) async-start(bf16[16,288,128]{2,1,0:T(8,128)(2,1)} %block.1), calls=%async_computation | async-start | bytes 2359296 | tf_op jit(solution)/shard_map/all_to_all | solution.py:298
  10.4 22.7 %copy-start.1 = (f32[128,8]{0,1:T(8,128)S(1)}, f32[128,8]{0,1:T(8,128)}, u32[]{:S(2)}) copy-start(f32[128,8]{0,1:T(8,128)} %param.9) | copy-start | bytes 12292
  27.8 5.3 %collective-permute-start = (bf16[16,288,128]{2,1,0:T(8,128)(2,1)S(1)}, bf16[16,288,128]{2,1,0:T(8,128)(2,1)S(1)}, u32[]{:S(2)}, u32[]{:S(2)}) collective-permute-start(bf16[16,288,128]{2,1,0:T(8,128)(2,1)S(1)} %all-to-all-done.own_b), channel_id=1, source_target_pairs={{0,8},{8,0},{16,24},{24,16},{32,40},{40,32},{48,56},{56,48},{64,72... | collective-permute-start | bytes 3538952 | tf_op jit(solution)/shard_map/ppermute | solution.py:302
  39.5 9.1 %collective-permute-start.1 = (f32[16,128,128]{2,1,0:T(8,128)}, f32[16,128,128]{2,1,0:T(8,128)S(1)}, u32[]{:S(2)}, u32[]{:S(2)}) collective-permute-start(f32[16,128,128]{2,1,0:T(8,128)} %get-tuple-element.24), channel_id=1, source_target_pairs={{0,8},{8,0},{16,24},{24,16},{32,40},{40,32},{48,56},{56,48},{64,72... | collective-permute-start | bytes 3145736 | tf_op jit(solution)/shard_map/ppermute | solution.py:329
  40.0 15.5 %all-to-all-start.1 = ((f32[16,1,128]{2,1,0:T(1,128)}), f32[16,1,128]{2,1,0:T(1,128)S(1)}, u32[]{:S(2)}, u32[]{:S(2)}) async-start(f32[16,1,128]{2,1,0:T(1,128)} %get-tuple-element.26), calls=%async_computation.1 | async-start | bytes 16384 | tf_op jit(solution)/shard_map/all_to_all | solution.py:327
  48.7 1.2 %copy-start = (f32[16,128,128]{2,1,0:T(8,128)S(1)}, f32[16,128,128]{2,1,0:T(8,128)}, u32[]{:S(2)}) copy-start(f32[16,128,128]{2,1,0:T(8,128)} %get-tuple-element.23.own) | copy-start | bytes 3145732
  56.2 21.9 %all-to-all-start.2 = ((f16[16,144,128]{2,1,0:T(8,128)(2,1)}), f16[16,144,128]{2,1,0:T(8,128)(2,1)S(1)}, u32[]{:S(2)}, u32[]{:S(2)}) async-start(f16[16,144,128]{2,1,0:T(8,128)(2,1)} %broadcast_dynamic-update-slice_fusion), calls=%async_computation.2 | async-start | bytes 1179648 | tf_op jit(solution)/shard_map/all_to_all | solution.py:351

commit v7 on v6

--- a/solution.py
+++ b/solution.py
@@ -33,7 +33,7 @@
     return jnp.floor(jnp.log2(jnp.maximum(x, TINY)))
 
 
-def block_kernel(keys_from, b_from, log_from, out, keys, b_rows, log_decay, sems):
+def block_kernel(keys_from, b_from, log_from, out, keys, b_rows, log_decay, block, sems):
     copies = [
         pltpu.make_async_copy(x, y, sems.at[i])
         for i, (x, y) in enumerate(((keys_from, keys), (b_from, b_rows), (log_from, log_decay)))
@@ -42,13 +42,14 @@
         x.start()
     for x in copies:
         x.wait()
-    high, mid, low = pieces(log_decay[...])
-    down = jnp.concatenate([high, mid, low, jnp.zeros((8, 128), jnp.bfloat16)], axis=0)
-    key_cols, b_cols = keys[...].T, b_rows[...].T
-    for k in range(out.shape[0]):
-        out[k, 0:128] = key_cols
-        out[k, 128:256] = b_cols
-        out[k, 256:288] = down
+    block[0:128] = keys[...].T
+    block[128:256] = b_rows[...].T
+    block[256:272] = jnp.concatenate(pieces(log_decay[...])[:2], axis=0)
+    copies = [pltpu.make_async_copy(block, out.at[k], sems.at[3 + k]) for k in range(out.shape[0])]
+    for x in copies:
+        x.start()
+    for x in copies:
+        x.wait()
 
 
 def match_kernel(heads, scale2, group, place, own_b, other_b, q, c, c_cols, log_decay, weighted, own_grad, other_grad, loss,
@@ -64,14 +65,14 @@
     upto = jnp.where(u <= v, 1.0, 0.0).astype(jnp.bfloat16)
     lower = jnp.where(u >= v, 1.0, 0.0).astype(jnp.bfloat16)
     columns = jnp.concatenate([log_decay[...], jnp.zeros((128 - heads, 128), jnp.float32)], axis=0).T
-    log_rows = sum(dot(lower, part) for part in pieces(columns)) * LOG2E
+    log_rows = sum(dot(lower, part) for part in pieces(columns)[:2]) * LOG2E
     for h in range(heads):
         row_log = jnp.broadcast_to(log_rows[:, h : h + 1], (half, 128))
         log_fade[h] = row_log
         fade[h] = jnp.exp2(row_log)
     def sums(ref, matrix):
-        y = dot(ref[:, 256:288].reshape(chips * 32, 128), matrix).reshape(chips, 32, 128)
-        return y[:, 0:8] + y[:, 8:16] + y[:, 16:24]
+        y = dot(ref[:, 256:272].reshape(chips * 16, 128), matrix).reshape(chips, 16, 128)
+        return y[:, 0:8] + y[:, 8:16]
 
     ones = jnp.ones((128, 128), jnp.bfloat16)
     own_tail, other_tail = sums(own_b, after), sums(other_b, after)
@@ -230,7 +231,7 @@
     up = jnp.exp2(13.0 - level)
     for k in range(blocks):
         sent[k, 0:128] = sent[k, 0:128] * up
-        sent[k, 128:144] = jnp.zeros((16, 128), jnp.float32)
+        sent[k, 128:136] = jnp.zeros((8, 128), jnp.float32)
     power[...] = level[0:8]
 
 
@@ -244,7 +245,7 @@
     row = jnp.where(lane == 1, lost_power, row)
     row = jnp.where(lane == 2, coarse, row)
     row = jnp.where(lane == 3, (share - coarse) * 1024.0, row)
-    extra[...] = jnp.concatenate([row, row], axis=0)
+    extra[...] = row
 
 
 def final_kernel(count, back, grad_b, mean):
@@ -287,11 +288,12 @@
     down = log_decay.T
     block = pl.pallas_call(
         block_kernel,
-        out_shape=bf16((chips, 288, 128)),
+        out_shape=hbm_out((chips, 272, 128), jnp.bfloat16),
         in_specs=[hbm] * 3,
-        out_specs=vmem,
+        out_specs=hbm,
         scratch_shapes=[pltpu.VMEM((rows_dev, size), jnp.bfloat16)] * 2
-        + [pltpu.VMEM((heads, rows_dev), jnp.float32), pltpu.SemaphoreType.DMA((3,))],
+        + [pltpu.VMEM((heads, rows_dev), jnp.float32), pltpu.VMEM((272, 128), jnp.bfloat16)]
+        + [pltpu.SemaphoreType.DMA((3 + chips,))],
         compiler_params=pltpu.CompilerParams(vmem_limit_bytes=SMALL),
         name="block",
     )(*(pltpu.with_memory_space_constraint(x, hbm_out) for x in (keys[:, 0], b_proj[:, 0], down)))
@@ -329,7 +331,7 @@
     other_sum = lax.ppermute(other_sum, "context", swap)
     sent, power = pl.pallas_call(
         scale_kernel,
-        out_shape=(f32((chips, 144, 128)), f32((8, 128))),
+        out_shape=(f32((chips, 136, 128)), f32((8, 128))),
         in_specs=[vmem] * 2,
         out_specs=(vmem,) * 2,
         compiler_params=pltpu.CompilerParams(vmem_limit_bytes=SMALL),
@@ -339,14 +341,14 @@
 
     extra = pl.pallas_call(
         extra_kernel,
-        out_shape=f32((16, 128)),
+        out_shape=f32((8, 128)),
         in_specs=[vmem] * 2,
         out_specs=vmem,
         compiler_params=pltpu.CompilerParams(vmem_limit_bytes=SMALL),
         name="extra",
     )(lost, power)
 
-    extra = jnp.broadcast_to(extra.astype(jnp.float16), (chips, 16, 128))
+    extra = jnp.broadcast_to(extra.astype(jnp.float16), (chips, 8, 128))
     sent = lax.dynamic_update_slice(sent, extra, (0, 128, 0))
     back = lax.all_to_all(sent, "context", 0, 0, axis_index_groups=plane)
     grad_c = pl.pallas_call(

time: 79.5 us -> 78.4 us (0.986)
  waiting for transfers between devices: 30.5 us -> 29.3 us
where the time goes in v7:
time: 78.4 us; the launch traced here: 77.9 us
  starting transfers between devices  30.5 us (39%)
  waiting for transfers between devices  29.3 us (37%)
  Pallas kernels  12.9 us (16%)
  local copies, waits for them, and re-layouts  3.36 us (4%)
  other arithmetic  1.08 us (1%)
  between operations  0.79 us (1%)
    all_to_all x1, waiting for transfers between devices, shards(): own_b = lax.all_to_all(block, 'context', 0, 0, axis_index_groups=plane)  16.2 us
    all_to_all x1, starting transfers between devices, shards(): back = lax.all_to_all(sent, 'context', 0, 0, axis_index_groups=plane)  11 us
    all_to_all x1, starting transfers between devices, shards(): lax.all_to_all(lost, ('context', 'head'), 0, 0, axis_index_groups=columns)  8.63 us
    all_to_all x1, starting transfers between devices, shards(): own_b = lax.all_to_all(block, 'context', 0, 0, axis_index_groups=plane)  7.73 us
    all_to_all x1, waiting for transfers between devices, shards(): back = lax.all_to_all(sent, 'context', 0, 0, axis_index_groups=plane)  6.54 us
    pallas_call x1, Pallas kernels, shards(): pl.pallas_call(functools.partial(match_kernel, heads, scale2, group), out...  6.45 us
    all_to_all x1, waiting for transfers between devices, shards(): lax.all_to_all(lost, ('context', 'head'), 0, 0, axis_index_groups=columns)  4.25 us
    pallas_call x1, Pallas kernels, shards(): pl.pallas_call(functools.partial(grad_kernel, group), out_shape=f32((size...  3 us
  transfers between devices with their start and end apart: 5, of which 4 were waited for; matrix products, arithmetic and copies ran while one was open for 3% of the time, Pallas kernels for 4%

profile of v7, /device:TPU:1, one launch (start us, length us, event | category | flops | bytes accessed | tf_op | source)
XLA Modules:
  0.0 77.9 jit_solution(176357373211116168)
XLA Ops:
  0.6 2.0 %block.1 = bf16[16,272,128]{2,1,0:T(8,128)(2,1)} custom-call(bf16[128,128]{1,0:T(8,128)(2,1)} %bitcast.29, bf16[128,128]{1,0:T(8,128)(2,1)} %bitcast.30, f32[8,128]{1,0:T(8,128)} %bitcast.23), custom_call_target="tpu_custom_call" | custom-call | tf_op jit(solution)/shard_map/block/pallas_call | solution.py:289
  2.6 0.0 copy-start.2
  2.7 0.0 copy-start.3
  2.7 7.7 %all-to-all-start = ((bf16[16,272,128]{2,1,0:T(8,128)(2,1)}), bf16[16,272,128]{2,1,0:T(8,128)(2,1)S(1)}, u32[]{:S(2)}, u32[]{:S(2)}) async-start(bf16[16,272,128]{2,1,0:T(8,128)(2,1)} %block.1), calls=%async_computation | async-start | bytes 2228224 | tf_op jit(solution)/shard_map/all_to_all | solution.py:300
  10.4 0.0 copy-start.1
  10.4 0.0 copy-done.2
  10.4 0.2 copy.10
  10.8 0.1 pad_add_fusion.place
  10.8 0.0 copy-done.3
  10.8 0.1 copy_bitcast_fusion.1
  10.9 16.2 %all-to-all-done.own_b = bf16[16,272,128]{2,1,0:T(8,128)(2,1)S(1)} async-done(((bf16[16,272,128]{2,1,0:T(8,128)(2,1)}), bf16[16,272,128]{2,1,0:T(8,128)(2,1)S(1)}, u32[]{:S(2)}, u32[]{:S(2)}) %all-to-all-start) | async-done | bytes 1114144 | tf_op jit(solution)/shard_map/all_to_all | solution.py:300
  27.1 2.7 %collective-permute-start = (bf16[16,272,128]{2,1,0:T(8,128)(2,1)S(1)}, bf16[16,272,128]{2,1,0:T(8,128)(2,1)S(1)}, u32[]{:S(2)}, u32[]{:S(2)}) collective-permute-start(bf16[16,272,128]{2,1,0:T(8,128)(2,1)S(1)} %all-to-all-done.own_b), channel_id=1, source_target_pairs={{0,8},{8,0},{16,24},{24,16},{32,40},{40,32},{48,56},{56,48},{64,72... | collective-permute-start | bytes 3342344 | tf_op jit(solution)/shard_map/ppermute | solution.py:304
  29.8 2.4 %collective-permute-done.other_b = bf16[16,272,128]{2,1,0:T(8,128)(2,1)S(1)} collective-permute-done((bf16[16,272,128]{2,1,0:T(8,128)(2,1)S(1)}, bf16[16,272,128]{2,1,0:T(8,128)(2,1)S(1)}, u32[]{:S(2)}, u32[]{:S(2)}) %collective-permute-start) | collective-permute-done | bytes 1114144 | tf_op jit(solution)/shard_map/ppermute | solution.py:304
  32.2 0.0 copy-done.1
  32.2 6.5 %match.1 = (bf16[4,1024,1024]{2,1,0:T(8,128)(2,1)}, f32[16,128,128]{2,1,0:T(8,128)}, f32[16,128,128]{2,1,0:T(8,128)}, f32[16,1,128]{2,1,0:T(1,128)}) custom-call(s32[2]{0:T(128)S(1)} %pad_add_fusion.place, bf16[16,272,128]{2,1,0:T(8,128)(2,1)S(1)} %all-to-all-done.own_b, bf16[16,272,128]{2,1,0:T(8,128)(2,1)S(1)} %collective-permute-done.other_b, ...), custom_call_target="tpu_custom_call" | custom-call | flops 3221225472 | bytes 12582912 | tf_op jit(solution)/shard_map/match/pallas_call | solution.py:306
  38.6 0.5 collective-permute-start.1
  39.1 8.6 %all-to-all-start.1 = ((f32[16,1,128]{2,1,0:T(1,128)}), f32[16,1,128]{2,1,0:T(1,128)S(1)}, u32[]{:S(2)}, u32[]{:S(2)}) async-start(f32[16,1,128]{2,1,0:T(1,128)} %get-tuple-element.26), calls=%async_computation.1 | async-start | bytes 16384 | tf_op jit(solution)/shard_map/all_to_all | solution.py:329
  47.7 0.0 collective-permute-done.1.other
  47.7 0.0 copy-start
  47.8 1.2 %copy-done = f32[16,128,128]{2,1,0:T(8,128)S(1)} copy-done((f32[16,128,128]{2,1,0:T(8,128)S(1)}, f32[16,128,128]{2,1,0:T(8,128)}, u32[]{:S(2)}) %copy-start) | copy-done | bytes 1048600
  49.0 0.5 scale.1
  49.5 0.9 %convert_element_type.9 = f16[16,136,128]{2,1,0:T(8,128)(2,1)} convert(f32[16,136,128]{2,1,0:T(8,128)S(1)} %get-tuple-element.25) | non-fusion elementwise | flops 278528 | bytes 1671168 | tf_op jit(solution)/shard_map/convert_element_type | solution.py:340
  50.4 4.3 %all-to-all-done.1.lost = f32[16,1,128]{2,1,0:T(1,128)S(1)} async-done(((f32[16,1,128]{2,1,0:T(1,128)}), f32[16,1,128]{2,1,0:T(1,128)S(1)}, u32[]{:S(2)}, u32[]{:S(2)}) %all-to-all-start.1) | async-done | bytes 8224 | tf_op jit(solution)/shard_map/all_to_all | solution.py:329
  54.7 0.6 broadcast_dynamic-update-slice_fusion
  55.3 11.0 %all-to-all-start.2 = ((f16[16,136,128]{2,1,0:T(8,128)(2,1)}), f16[16,136,128]{2,1,0:T(8,128)(2,1)S(1)}, u32[]{:S(2)}, u32[]{:S(2)}) async-start(f16[16,136,128]{2,1,0:T(8,128)(2,1)} %broadcast_dynamic-update-slice_fusion), calls=%async_computation.2 | async-start | bytes 1114112 | tf_op jit(solution)/shard_map/all_to_all | solution.py:353
  66.3 3.0 %grads.1 = f32[128,1024]{1,0:T(8,128)S(1)} custom-call(s32[2]{0:T(128)S(1)} %pad_add_fusion.place, bf16[16,272,128]{2,1,0:T(8,128)(2,1)S(1)} %all-to-all-done.own_b, bf16[16,272,128]{2,1,0:T(8,128)(2,1)S(1)} %collective-permute-done.other_b, bf16[4,1024,1024]{2,1,0:T(8,128)(2,1)} %get-tuple-element.31.weighted), custom_call_target="tpu_custom_call" | custom-call | flops 1073741824 | bytes 10485760 | tf_op jit(solution)/shard_map/grads/pallas_call | solution.py:354
  69.3 0.1 copy.14
  69.4 1.0 %copy.11 = f32[128,8,128]{0,1,2:T(8,128)} copy(f32[128,8,128]{2,1,0:T(8,128)S(1)} %bitcast.25) | data formatting | bytes 1048576 | tf_op jit(solution)/shard_map/reshape | solution.py:364
  70.4 6.5 %all-to-all-done.2 = f16[16,136,128]{2,1,0:T(8,128)(2,1)S(1)} async-done(((f16[16,136,128]{2,1,0:T(8,128)(2,1)}), f16[16,136,128]{2,1,0:T(8,128)(2,1)S(1)}, u32[]{:S(2)}, u32[]{:S(2)}) %all-to-all-start.2) | async-done | bytes 557088 | tf_op jit(solution)/shard_map/all_to_all | solution.py:353
  76.9 0.1 convert_element_type.11.back
  77.0 0.9 %final.1 = (f32[128,128]{1,0:T(8,128)}, f32[1,1]{1,0:T(1,128)}) custom-call(f32[16,136,128]{2,1,0:T(8,128)S(1)} %convert_element_type.11.back), custom_call_target="tpu_custom_call" | custom-call | tf_op jit(solution)/shard_map/final/pallas_call | solution.py:365
  (3 shorter events, 0.1 us)
Async XLA Ops:
  2.6 7.8 %copy-start.2 = (bf16[128,8,128]{2,1,0:T(8,128)(2,1)S(1)}, bf16[128,8,128]{2,1,0:T(8,128)(2,1)}, u32[]{:S(2)}) copy-start(bf16[128,8,128]{2,1,0:T(8,128)(2,1)} %param.7) | copy-start | bytes 786436
  2.7 8.2 %copy-start.3 = (bf16[128,8,128]{2,1,0:T(8,128)(2,1)S(1)}, bf16[128,8,128]{2,1,0:T(8,128)(2,1)}, u32[]{:S(2)}) copy-start(bf16[128,8,128]{2,1,0:T(8,128)(2,1)} %param.5) | copy-start | bytes 786436
  2.7 24.4 %all-to-all-start = ((bf16[16,272,128]{2,1,0:T(8,128)(2,1)}), bf16[16,272,128]{2,1,0:T(8,128)(2,1)S(1)}, u32[]{:S(2)}, u32[]{:S(2)}) async-start(bf16[16,272,128]{2,1,0:T(8,128)(2,1)} %block.1), calls=%async_computation | async-start | bytes 2228224 | tf_op jit(solution)/shard_map/all_to_all | solution.py:300
  10.4 21.8 %copy-start.1 = (f32[128,8]{0,1:T(8,128)S(1)}, f32[128,8]{0,1:T(8,128)}, u32[]{:S(2)}) copy-start(f32[128,8]{0,1:T(8,128)} %param.9) | copy-start | bytes 12292
  27.1 5.1 %collective-permute-start = (bf16[16,272,128]{2,1,0:T(8,128)(2,1)S(1)}, bf16[16,272,128]{2,1,0:T(8,128)(2,1)S(1)}, u32[]{:S(2)}, u32[]{:S(2)}) collective-permute-start(bf16[16,272,128]{2,1,0:T(8,128)(2,1)S(1)} %all-to-all-done.own_b), channel_id=1, source_target_pairs={{0,8},{8,0},{16,24},{24,16},{32,40},{40,32},{48,56},{56,48},{64,72... | collective-permute-start | bytes 3342344 | tf_op jit(solution)/shard_map/ppermute | solution.py:304
  38.6 9.1 %collective-permute-start.1 = (f32[16,128,128]{2,1,0:T(8,128)}, f32[16,128,128]{2,1,0:T(8,128)S(1)}, u32[]{:S(2)}, u32[]{:S(2)}) collective-permute-start(f32[16,128,128]{2,1,0:T(8,128)} %get-tuple-element.24), channel_id=1, source_target_pairs={{0,8},{8,0},{16,24},{24,16},{32,40},{40,32},{48,56},{56,48},{64,72... | collective-permute-start | bytes 3145736 | tf_op jit(solution)/shard_map/ppermute | solution.py:331
  39.1 15.5 %all-to-all-start.1 = ((f32[16,1,128]{2,1,0:T(1,128)}), f32[16,1,128]{2,1,0:T(1,128)S(1)}, u32[]{:S(2)}, u32[]{:S(2)}) async-start(f32[16,1,128]{2,1,0:T(1,128)} %get-tuple-element.26), calls=%async_computation.1 | async-start | bytes 16384 | tf_op jit(solution)/shard_map/all_to_all | solution.py:329
  47.7 1.2 %copy-start = (f32[16,128,128]{2,1,0:T(8,128)S(1)}, f32[16,128,128]{2,1,0:T(8,128)}, u32[]{:S(2)}) copy-start(f32[16,128,128]{2,1,0:T(8,128)} %get-tuple-element.23.own) | copy-start | bytes 3145732
  55.3 21.6 %all-to-all-start.2 = ((f16[16,136,128]{2,1,0:T(8,128)(2,1)}), f16[16,136,128]{2,1,0:T(8,128)(2,1)S(1)}, u32[]{:S(2)}, u32[]{:S(2)}) async-start(f16[16,136,128]{2,1,0:T(8,128)(2,1)} %broadcast_dynamic-update-slice_fusion), calls=%async_computation.2 | async-start | bytes 1114112 | tf_op jit(solution)/shard_map/all_to_all | solution.py:353

commit v8 on v7

--- a/solution.py
+++ b/solution.py
@@ -52,12 +52,18 @@
         x.wait()
 
 
-def match_kernel(heads, scale2, group, place, own_b, other_b, q, c, c_cols, log_decay, weighted, own_grad, other_grad, loss,
-                 scores, tops, peak, total, fade, log_fade, key_fade, key_log, held, own_held, other_held, lost, sems):
+def match_kernel(heads, scale2, group, place, own_b, other_b, q_from, c_from, cols_from, log_decay,
+                 weighted, own_grad, other_grad, loss, q, c, c_cols,
+                 scores, tops, peak, total, fade, log_fade, key_fade, key_log, held, lost, sems, load_sems):
     chip, core = place[0], place[1]
     chips, half = own_b.shape[0], q.shape[1]
     rows = heads * half
     full = chip // group
+    loads = [
+        pltpu.make_async_copy(x, y, load_sems.at[i]) for i, (x, y) in enumerate(((q_from, q), (c_from, c), (cols_from, c_cols)))
+    ]
+    for x in loads:
+        x.start()
 
     u = lax.broadcasted_iota(jnp.int32, (128, 128), 0)
     v = lax.broadcasted_iota(jnp.int32, (128, 128), 1)
@@ -123,6 +129,8 @@
             peak[h] = top
             tops[p, h] = top
 
+    loads[0].wait()
+
     @pl.loop(0, full)
     def _(p):
         score(p, False)
@@ -135,13 +143,6 @@
         peak[h] = jnp.broadcast_to(top + jnp.log2(summed), (half, 128))
     lost[...] = jnp.zeros_like(lost)
 
-    def copies(p):
-        part = pl.ds(p * group, group)
-        return (
-            pltpu.make_async_copy(own_held.at[part], own_grad.at[part], sems.at[heads, p]),
-            pltpu.make_async_copy(other_held.at[part], other_grad.at[part], sems.at[heads + 1, p]),
-        )
-
     def copy(p, h):
         at = pl.ds(h * half, half)
         return pltpu.make_async_copy(held.at[p, at], weighted.at[p, at], sems.at[h, p])
@@ -149,10 +150,8 @@
     @pl.loop(full + 1, chips // group)
     def _(p):
         for i in range(group):
-            own_held[group * p + i] = jnp.zeros((128, 128), jnp.float32)
-            other_held[group * p + i] = jnp.zeros((128, 128), jnp.float32)
-        for x in copies(p):
-            x.start()
+            own_grad[group * p + i] = jnp.zeros((128, 128), jnp.float32)
+            other_grad[group * p + i] = jnp.zeros((128, 128), jnp.float32)
 
     def step(p, masked):
         kept = [2 * group * p + i for i in range(2 * group)]
@@ -176,10 +175,11 @@
         lost[...] += squares
         parts = dot(c_cols[...], held[p])
         for i in range(group):
-            own_held[group * p + i] = parts[:, 256 * i : 256 * i + 128]
-            other_held[group * p + i] = parts[:, 256 * i + 128 : 256 * i + 256]
-        for x in copies(p):
-            x.start()
+            own_grad[group * p + i] = parts[:, 256 * i : 256 * i + 128]
+            other_grad[group * p + i] = parts[:, 256 * i + 128 : 256 * i + 256]
+
+    loads[1].wait()
+    loads[2].wait()
 
     @pl.loop(0, full)
     def _(p):
@@ -192,11 +192,6 @@
     def _(p):
         for h in range(heads):
             copy(p, h).wait()
-
-    @pl.loop(0, chips // group)
-    def _(p):
-        for x in copies(p):
-            x.wait()
 
 
 def grad_kernel(group, place, own_b, other_b, weighted, grad_c, held, sems):
@@ -307,23 +302,23 @@
         functools.partial(match_kernel, heads, scale2, group),
         out_shape=(
             hbm_out((steps, rows, width), jnp.bfloat16),
-            hbm_out((chips, size, 128), jnp.float32),
-            hbm_out((chips, size, 128), jnp.float32),
+            f32((chips, size, 128)),
+            f32((chips, size, 128)),
             hbm_out((2 * z_size, 1, 128), jnp.float32),
         ),
-        in_specs=[smem] + [vmem] * 6,
-        out_specs=(hbm, hbm, hbm, pl.BlockSpec((2 * z_size, 1, 128), lambda: (0, 0, 0))),
-        scratch_shapes=[pltpu.VMEM((steps, rows, width), jnp.float32)]
+        in_specs=[smem, vmem, vmem, hbm, hbm, hbm, vmem],
+        out_specs=(hbm, vmem, vmem, pl.BlockSpec((2 * z_size, 1, 128), lambda: (0, 0, 0))),
+        scratch_shapes=[pltpu.VMEM((heads, rows_dev, size), jnp.bfloat16)] * 2
+        + [pltpu.VMEM((size, rows), jnp.bfloat16), pltpu.VMEM((steps, rows, width), jnp.float32)]
         + [pltpu.VMEM((steps, heads, rows_dev, 128), jnp.float32)]
         + [tile] * 4
         + [pltpu.VMEM((peers, 8, 128), jnp.float32)] * 2
         + [pltpu.VMEM((steps, rows, width), jnp.bfloat16)]
-        + [pltpu.VMEM((chips, size, 128), jnp.float32)] * 2
-        + [pltpu.VMEM((8, 128), jnp.float32), pltpu.SemaphoreType.DMA((heads + 2, steps))],
+        + [pltpu.VMEM((8, 128), jnp.float32), pltpu.SemaphoreType.DMA((heads, steps)), pltpu.SemaphoreType.DMA((3,))],
         compiler_params=pltpu.CompilerParams(vmem_limit_bytes=MATCH),
         cost_estimate=pl.CostEstimate(flops=6 * work * size, bytes_accessed=12 << 20, transcendentals=3 * work),
         name="match",
-    )(place, own_b, other_b, q, c, c_cols, down)
+    )(place, own_b, other_b, *(pltpu.with_memory_space_constraint(x, hbm_out) for x in (q, c, c_cols)), down)
 
     columns = [[(2 * k + c) * z_size + z for c in range(2) for z in range(z_size)] for k in range(chips)]
     lost = lax.all_to_all(lost, ("context", "head"), 0, 0, axis_index_groups=columns)

time: 78.4 us -> 79.2 us (1.010)
  Pallas kernels: 12.9 us -> 14.9 us
  waiting for transfers between devices: 29.3 us -> 27.9 us
    all_to_all x1, waiting for transfers between devices: 16.2 us -> 14.7 us  [shards(): own_b = lax.all_to_all(block, 'context', 0, 0, axis_index_groups=plane)]
    pallas_call x1, Pallas kernels: 0.47 us -> 1.71 us  [shards(): pl.pallas_call(scale_kernel, out_shape=(f32((chips, 136, 128)), f32((8, 1...]
    transpose x1, local copies, waits for them, and re-layouts: 0.09 us -> 0.89 us  [shards(): q, c = (queries.transpose(1, 0, 2), c_proj.transpose(1, 0, 2))]
  transfers between devices with their start and end apart: 5 -> 5, of which waited for: 4 -> 4; matrix products, arithmetic and copies ran while one was open for 3% -> 5% of each run, Pallas kernels for 4% -> 6%
where the time goes in v8:
time: 79.2 us; the launch traced here: 78.7 us
  starting transfers between devices  30.5 us (39%)
  waiting for transfers between devices  27.9 us (35%)
  Pallas kernels  14.9 us (19%)
  local copies, waits for them, and re-layouts  3.66 us (5%)
  other arithmetic  1.07 us (1%)
    all_to_all x1, waiting for transfers between devices, shards(): own_b = lax.all_to_all(block, 'context', 0, 0, axis_index_groups=plane)  14.7 us
    all_to_all x1, starting transfers between devices, shards(): back = lax.all_to_all(sent, 'context', 0, 0, axis_index_groups=plane)  10.9 us
    all_to_all x1, starting transfers between devices, shards(): lax.all_to_all(lost, ('context', 'head'), 0, 0, axis_index_groups=columns)  8.65 us
    all_to_all x1, starting transfers between devices, shards(): own_b = lax.all_to_all(block, 'context', 0, 0, axis_index_groups=plane)  7.73 us
    pallas_call x1, Pallas kernels, shards(): pl.pallas_call(functools.partial(match_kernel, heads, scale2, group), out...  7.21 us
    all_to_all x1, waiting for transfers between devices, shards(): back = lax.all_to_all(sent, 'context', 0, 0, axis_index_groups=plane)  6.54 us
    all_to_all x1, waiting for transfers between devices, shards(): lax.all_to_all(lost, ('context', 'head'), 0, 0, axis_index_groups=columns)  4.26 us
    pallas_call x1, Pallas kernels, shards(): pl.pallas_call(functools.partial(grad_kernel, group), out_shape=f32((size...  3 us
  transfers between devices with their start and end apart: 5, of which 4 were waited for; matrix products, arithmetic and copies ran while one was open for 5% of the time, Pallas kernels for 6%

profile of v8, /device:TPU:1, one launch (start us, length us, event | category | flops | bytes accessed | tf_op | source)
XLA Modules:
  0.0 78.7 jit_solution(3750645325699340264)
XLA Ops:
  0.6 2.0 %block.1 = bf16[16,272,128]{2,1,0:T(8,128)(2,1)} custom-call(bf16[128,128]{1,0:T(8,128)(2,1)} %bitcast.29, bf16[128,128]{1,0:T(8,128)(2,1)} %bitcast.30, f32[8,128]{1,0:T(8,128)} %bitcast.22), custom_call_target="tpu_custom_call" | custom-call | tf_op jit(solution)/shard_map/block/pallas_call | solution.py:284
  2.7 0.0 copy-start.1
  2.7 0.0 copy-start.2
  2.7 7.7 %all-to-all-start = ((bf16[16,272,128]{2,1,0:T(8,128)(2,1)}), bf16[16,272,128]{2,1,0:T(8,128)(2,1)S(1)}, u32[]{:S(2)}, u32[]{:S(2)}) async-start(bf16[16,272,128]{2,1,0:T(8,128)(2,1)} %block.1), calls=%async_computation | async-start | bytes 2228224 | tf_op jit(solution)/shard_map/all_to_all | solution.py:295
  10.4 0.0 copy-start
  10.4 0.0 copy-done.1
  10.5 0.2 copy.10
  10.7 0.8 copy.18
  11.4 0.1 pad_add_fusion.place
  11.5 0.0 copy-done.2
  11.5 0.9 %copy_bitcast_fusion.1 = (bf16[8,128,128]{2,1,0:T(8,128)(2,1)}, bf16[8,128,128]{2,1,0:T(8,128)(2,1)}) fusion(bf16[128,8,128]{2,1,0:T(8,128)(2,1)S(1)} %copy-done.1, bf16[128,8,128]{2,1,0:T(8,128)(2,1)S(1)} %copy-done.2), kind=kLoop, calls=%fused_computation.1 | loop fusion | bytes 1048576 | tf_op jit(solution)/shard_map/transpose | solution.py:296
  12.4 14.7 %all-to-all-done.own_b = bf16[16,272,128]{2,1,0:T(8,128)(2,1)S(1)} async-done(((bf16[16,272,128]{2,1,0:T(8,128)(2,1)}), bf16[16,272,128]{2,1,0:T(8,128)(2,1)S(1)}, u32[]{:S(2)}, u32[]{:S(2)}) %all-to-all-start) | async-done | bytes 1114144 | tf_op jit(solution)/shard_map/all_to_all | solution.py:295
  27.1 2.7 %collective-permute-start = (bf16[16,272,128]{2,1,0:T(8,128)(2,1)S(1)}, bf16[16,272,128]{2,1,0:T(8,128)(2,1)S(1)}, u32[]{:S(2)}, u32[]{:S(2)}) collective-permute-start(bf16[16,272,128]{2,1,0:T(8,128)(2,1)S(1)} %all-to-all-done.own_b), channel_id=1, source_target_pairs={{0,8},{8,0},{16,24},{24,16},{32,40},{40,32},{48,56},{56,48},{64,72... | collective-permute-start | bytes 3342344 | tf_op jit(solution)/shard_map/ppermute | solution.py:299
  29.8 2.4 %collective-permute-done.other_b = bf16[16,272,128]{2,1,0:T(8,128)(2,1)S(1)} collective-permute-done((bf16[16,272,128]{2,1,0:T(8,128)(2,1)S(1)}, bf16[16,272,128]{2,1,0:T(8,128)(2,1)S(1)}, u32[]{:S(2)}, u32[]{:S(2)}) %collective-permute-start) | collective-permute-done | bytes 1114144 | tf_op jit(solution)/shard_map/ppermute | solution.py:299
  32.2 0.0 copy-done
  32.2 7.2 %match.1 = (bf16[4,1024,1024]{2,1,0:T(8,128)(2,1)}, f32[16,128,128]{2,1,0:T(8,128)S(1)}, f32[16,128,128]{2,1,0:T(8,128)}, f32[16,1,128]{2,1,0:T(1,128)}) custom-call(s32[2]{0:T(128)S(1)} %pad_add_fusion.place, bf16[16,272,128]{2,1,0:T(8,128)(2,1)S(1)} %all-to-all-done.own_b, bf16[16,272,128]{2,1,0:T(8,128)(2,1)S(1)} %collective-permute-done.other_b, ...), custom_call_target="tpu_custom_call" | custom-call | flops 3221225472 | bytes 12582912 | tf_op jit(solution)/shard_map/match/pallas_call | solution.py:301
  39.4 0.4 collective-permute-start.1
  39.8 8.7 %all-to-all-start.1 = ((f32[16,1,128]{2,1,0:T(1,128)}), f32[16,1,128]{2,1,0:T(1,128)S(1)}, u32[]{:S(2)}, u32[]{:S(2)}) async-start(f32[16,1,128]{2,1,0:T(1,128)} %get-tuple-element.26), calls=%async_computation.1 | async-start | bytes 16384 | tf_op jit(solution)/shard_map/all_to_all | solution.py:324
  48.5 0.0 collective-permute-done.1.other
  48.5 1.7 %scale.1 = (f32[16,136,128]{2,1,0:T(8,128)S(1)}, f32[8,128]{1,0:T(8,128)S(1)}) custom-call(f32[16,128,128]{2,1,0:T(8,128)S(1)} %get-tuple-element.23.own, f32[16,128,128]{2,1,0:T(8,128)} %collective-permute-done.1.other), custom_call_target="tpu_custom_call" | custom-call | tf_op jit(solution)/shard_map/scale/pallas_call | solution.py:327
  50.2 0.9 %convert_element_type.9 = f16[16,136,128]{2,1,0:T(8,128)(2,1)} convert(f32[16,136,128]{2,1,0:T(8,128)S(1)} %get-tuple-element.25) | non-fusion elementwise | flops 278528 | bytes 1671168 | tf_op jit(solution)/shard_map/convert_element_type | solution.py:335
  51.1 4.3 %all-to-all-done.1.lost = f32[16,1,128]{2,1,0:T(1,128)S(1)} async-done(((f32[16,1,128]{2,1,0:T(1,128)}), f32[16,1,128]{2,1,0:T(1,128)S(1)}, u32[]{:S(2)}, u32[]{:S(2)}) %all-to-all-start.1) | async-done | bytes 8224 | tf_op jit(solution)/shard_map/all_to_all | solution.py:324
  55.4 0.6 broadcast_dynamic-update-slice_fusion
  56.1 10.9 %all-to-all-start.2 = ((f16[16,136,128]{2,1,0:T(8,128)(2,1)}), f16[16,136,128]{2,1,0:T(8,128)(2,1)S(1)}, u32[]{:S(2)}, u32[]{:S(2)}) async-start(f16[16,136,128]{2,1,0:T(8,128)(2,1)} %broadcast_dynamic-update-slice_fusion), calls=%async_computation.2 | async-start | bytes 1114112 | tf_op jit(solution)/shard_map/all_to_all | solution.py:348
  67.0 3.0 %grads.1 = f32[128,1024]{1,0:T(8,128)S(1)} custom-call(s32[2]{0:T(128)S(1)} %pad_add_fusion.place, bf16[16,272,128]{2,1,0:T(8,128)(2,1)S(1)} %all-to-all-done.own_b, bf16[16,272,128]{2,1,0:T(8,128)(2,1)S(1)} %collective-permute-done.other_b, bf16[4,1024,1024]{2,1,0:T(8,128)(2,1)} %get-tuple-element.31.weighted), custom_call_target="tpu_custom_call" | custom-call | flops 1073741824 | bytes 10485760 | tf_op jit(solution)/shard_map/grads/pallas_call | solution.py:349
  70.0 0.1 copy.14
  70.1 1.0 %copy.11 = f32[128,8,128]{0,1,2:T(8,128)} copy(f32[128,8,128]{2,1,0:T(8,128)S(1)} %bitcast.24) | data formatting | bytes 1048576 | tf_op jit(solution)/shard_map/reshape | solution.py:359
  71.2 6.5 %all-to-all-done.2 = f16[16,136,128]{2,1,0:T(8,128)(2,1)S(1)} async-done(((f16[16,136,128]{2,1,0:T(8,128)(2,1)}), f16[16,136,128]{2,1,0:T(8,128)(2,1)S(1)}, u32[]{:S(2)}, u32[]{:S(2)}) %all-to-all-start.2) | async-done | bytes 557088 | tf_op jit(solution)/shard_map/all_to_all | solution.py:348
  77.7 0.1 convert_element_type.11.back
  77.8 0.9 %final.1 = (f32[128,128]{1,0:T(8,128)}, f32[1,1]{1,0:T(1,128)}) custom-call(f32[16,136,128]{2,1,0:T(8,128)S(1)} %convert_element_type.11.back), custom_call_target="tpu_custom_call" | custom-call | tf_op jit(solution)/shard_map/final/pallas_call | solution.py:360
  (2 shorter events, 0.0 us)
Async XLA Ops:
  2.7 7.8 %copy-start.1 = (bf16[128,8,128]{2,1,0:T(8,128)(2,1)S(1)}, bf16[128,8,128]{2,1,0:T(8,128)(2,1)}, u32[]{:S(2)}) copy-start(bf16[128,8,128]{2,1,0:T(8,128)(2,1)} %param.7) | copy-start | bytes 786436
  2.7 8.9 %copy-start.2 = (bf16[128,8,128]{2,1,0:T(8,128)(2,1)S(1)}, bf16[128,8,128]{2,1,0:T(8,128)(2,1)}, u32[]{:S(2)}) copy-start(bf16[128,8,128]{2,1,0:T(8,128)(2,1)} %param.5) | copy-start | bytes 786436
  2.7 24.4 %all-to-all-start = ((bf16[16,272,128]{2,1,0:T(8,128)(2,1)}), bf16[16,272,128]{2,1,0:T(8,128)(2,1)S(1)}, u32[]{:S(2)}, u32[]{:S(2)}) async-start(bf16[16,272,128]{2,1,0:T(8,128)(2,1)} %block.1), calls=%async_computation | async-start | bytes 2228224 | tf_op jit(solution)/shard_map/all_to_all | solution.py:295
  10.4 21.8 %copy-start = (f32[128,8]{0,1:T(8,128)S(1)}, f32[128,8]{0,1:T(8,128)}, u32[]{:S(2)}) copy-start(f32[128,8]{0,1:T(8,128)} %param.9) | copy-start | bytes 12292
  27.1 5.1 %collective-permute-start = (bf16[16,272,128]{2,1,0:T(8,128)(2,1)S(1)}, bf16[16,272,128]{2,1,0:T(8,128)(2,1)S(1)}, u32[]{:S(2)}, u32[]{:S(2)}) collective-permute-start(bf16[16,272,128]{2,1,0:T(8,128)(2,1)S(1)} %all-to-all-done.own_b), channel_id=1, source_target_pairs={{0,8},{8,0},{16,24},{24,16},{32,40},{40,32},{48,56},{56,48},{64,72... | collective-permute-start | bytes 3342344 | tf_op jit(solution)/shard_map/ppermute | solution.py:299
  39.4 9.1 %collective-permute-start.1 = (f32[16,128,128]{2,1,0:T(8,128)}, f32[16,128,128]{2,1,0:T(8,128)}, u32[]{:S(2)}, u32[]{:S(2)}) collective-permute-start(f32[16,128,128]{2,1,0:T(8,128)} %get-tuple-element.24), channel_id=1, source_target_pairs={{0,8},{8,0},{16,24},{24,16},{32,40},{40,32},{48,56},{56,48},{64,72... | collective-permute-start | bytes 3145736 | tf_op jit(solution)/shard_map/ppermute | solution.py:326
  39.8 15.5 %all-to-all-start.1 = ((f32[16,1,128]{2,1,0:T(1,128)}), f32[16,1,128]{2,1,0:T(1,128)S(1)}, u32[]{:S(2)}, u32[]{:S(2)}) async-start(f32[16,1,128]{2,1,0:T(1,128)} %get-tuple-element.26), calls=%async_computation.1 | async-start | bytes 16384 | tf_op jit(solution)/shard_map/all_to_all | solution.py:324
  56.1 21.6 %all-to-all-start.2 = ((f16[16,136,128]{2,1,0:T(8,128)(2,1)}), f16[16,136,128]{2,1,0:T(8,128)(2,1)S(1)}, u32[]{:S(2)}, u32[]{:S(2)}) async-start(f16[16,136,128]{2,1,0:T(8,128)(2,1)} %broadcast_dynamic-update-slice_fusion), calls=%async_computation.2 | async-start | bytes 1114112 | tf_op jit(solution)/shard_map/all_to_all | solution.py:348

commit v9 on v7

--- a/solution.py
+++ b/solution.py
@@ -181,11 +181,19 @@
         for x in copies(p):
             x.start()
 
-    @pl.loop(0, full)
-    def _(p):
-        step(p, False)
-
-    step(full, True)
+    @pl.when(full == chips // group - 1)
+    def _():
+        for p in range(chips // group - 1):
+            step(p, False)
+        step(chips // group - 1, True)
+
+    @pl.when(full < chips // group - 1)
+    def _():
+        @pl.loop(0, full)
+        def _(p):
+            step(p, False)
+
+        step(full, True)
     loss[...] = jnp.broadcast_to(jnp.sum(lost[...], keepdims=True)[None], loss.shape)
 
     @pl.loop(0, full + 1)
@@ -250,16 +258,14 @@
 
 def final_kernel(count, back, grad_b, mean):
     blocks = back.shape[0]
+    extra = jnp.concatenate([back[k, 128:129] for k in range(blocks)], axis=0)
+    scale = jnp.broadcast_to(jnp.exp2(extra[:, 0:1] - 13.0), (blocks, 128))
     total = jnp.zeros((128, 128), jnp.float32)
-    loss = jnp.zeros((1, 128), jnp.float32)
     for k in range(blocks):
-        extra = back[k, 128:129]
-        power = jnp.broadcast_to(extra[:, 0:1], (1, 128))
-        total = total + back[k, 0:128] * jnp.exp2(power - 13.0)
-        share = extra[:, 2:3] + extra[:, 3:4] * (1.0 / 1024.0)
-        loss = loss + jnp.broadcast_to(share * jnp.exp2(extra[:, 1:2]), (1, 128))
+        total = total + back[k, 0:128] * scale[k : k + 1]
     grad_b[...] = 2.0 * total.T
-    mean[0, 0] = jnp.max(loss) * (1.0 / count)
+    share = extra[:, 2:3] + extra[:, 3:4] * (1.0 / 1024.0)
+    mean[0, 0] = jnp.sum(share * jnp.exp2(extra[:, 1:2])) * (1.0 / count)
 
 
 def shards(queries, keys, c_proj, b_proj, log_decay):

time: 78.4 us -> 78.1 us (level)
  no operation moved by 1% of the time
where the time goes in v9:
time: 78.1 us; the launch traced here: 77.7 us
  starting transfers between devices  29.9 us (38%)
  waiting for transfers between devices  29.3 us (38%)
  Pallas kernels  13 us (17%)
  local copies, waits for them, and re-layouts  3.36 us (4%)
  other arithmetic  1.08 us (1%)
  between operations  0.97 us (1%)
    all_to_all x1, waiting for transfers between devices, shards(): own_b = lax.all_to_all(block, 'context', 0, 0, axis_index_groups=plane)  16.2 us
    all_to_all x1, starting transfers between devices, shards(): back = lax.all_to_all(sent, 'context', 0, 0, axis_index_groups=plane)  10.4 us
    all_to_all x1, starting transfers between devices, shards(): lax.all_to_all(lost, ('context', 'head'), 0, 0, axis_index_groups=columns)  8.63 us
    all_to_all x1, starting transfers between devices, shards(): own_b = lax.all_to_all(block, 'context', 0, 0, axis_index_groups=plane)  7.73 us
    pallas_call x1, Pallas kernels, shards(): pl.pallas_call(functools.partial(match_kernel, heads, scale2, group), out...  6.62 us
    all_to_all x1, waiting for transfers between devices, shards(): back = lax.all_to_all(sent, 'context', 0, 0, axis_index_groups=plane)  6.54 us
    all_to_all x1, waiting for transfers between devices, shards(): lax.all_to_all(lost, ('context', 'head'), 0, 0, axis_index_groups=columns)  4.25 us
    pallas_call x1, Pallas kernels, shards(): pl.pallas_call(functools.partial(grad_kernel, group), out_shape=f32((size...  3 us
  transfers between devices with their start and end apart: 5, of which 4 were waited for; matrix products, arithmetic and copies ran while one was open for 3% of the time, Pallas kernels for 4%

profile of v9, /device:TPU:1, one launch (start us, length us, event | category | flops | bytes accessed | tf_op | source)
XLA Modules:
  0.0 77.7 jit_solution(4578569196835644776)
XLA Ops:
  0.6 2.0 %block.1 = bf16[16,272,128]{2,1,0:T(8,128)(2,1)} custom-call(bf16[128,128]{1,0:T(8,128)(2,1)} %bitcast.29, bf16[128,128]{1,0:T(8,128)(2,1)} %bitcast.30, f32[8,128]{1,0:T(8,128)} %bitcast.23), custom_call_target="tpu_custom_call" | custom-call | tf_op jit(solution)/shard_map/block/pallas_call | solution.py:295
  2.6 0.0 copy-start.2
  2.7 0.0 copy-start.3
  2.7 7.7 %all-to-all-start = ((bf16[16,272,128]{2,1,0:T(8,128)(2,1)}), bf16[16,272,128]{2,1,0:T(8,128)(2,1)S(1)}, u32[]{:S(2)}, u32[]{:S(2)}) async-start(bf16[16,272,128]{2,1,0:T(8,128)(2,1)} %block.1), calls=%async_computation | async-start | bytes 2228224 | tf_op jit(solution)/shard_map/all_to_all | solution.py:306
  10.4 0.0 copy-start.1
  10.4 0.0 copy-done.2
  10.4 0.2 copy.10
  10.8 0.1 pad_add_fusion.place
  10.8 0.0 copy-done.3
  10.8 0.1 copy_bitcast_fusion.1
  10.9 16.2 %all-to-all-done.own_b = bf16[16,272,128]{2,1,0:T(8,128)(2,1)S(1)} async-done(((bf16[16,272,128]{2,1,0:T(8,128)(2,1)}), bf16[16,272,128]{2,1,0:T(8,128)(2,1)S(1)}, u32[]{:S(2)}, u32[]{:S(2)}) %all-to-all-start) | async-done | bytes 1114144 | tf_op jit(solution)/shard_map/all_to_all | solution.py:306
  27.1 2.7 %collective-permute-start = (bf16[16,272,128]{2,1,0:T(8,128)(2,1)S(1)}, bf16[16,272,128]{2,1,0:T(8,128)(2,1)S(1)}, u32[]{:S(2)}, u32[]{:S(2)}) collective-permute-start(bf16[16,272,128]{2,1,0:T(8,128)(2,1)S(1)} %all-to-all-done.own_b), channel_id=1, source_target_pairs={{0,8},{8,0},{16,24},{24,16},{32,40},{40,32},{48,56},{56,48},{64,72... | collective-permute-start | bytes 3342344 | tf_op jit(solution)/shard_map/ppermute | solution.py:310
  29.8 2.4 %collective-permute-done.other_b = bf16[16,272,128]{2,1,0:T(8,128)(2,1)S(1)} collective-permute-done((bf16[16,272,128]{2,1,0:T(8,128)(2,1)S(1)}, bf16[16,272,128]{2,1,0:T(8,128)(2,1)S(1)}, u32[]{:S(2)}, u32[]{:S(2)}) %collective-permute-start) | collective-permute-done | bytes 1114144 | tf_op jit(solution)/shard_map/ppermute | solution.py:310
  32.2 0.0 copy-done.1
  32.2 6.6 %match.1 = (bf16[4,1024,1024]{2,1,0:T(8,128)(2,1)}, f32[16,128,128]{2,1,0:T(8,128)}, f32[16,128,128]{2,1,0:T(8,128)}, f32[16,1,128]{2,1,0:T(1,128)}) custom-call(s32[2]{0:T(128)S(1)} %pad_add_fusion.place, bf16[16,272,128]{2,1,0:T(8,128)(2,1)S(1)} %all-to-all-done.own_b, bf16[16,272,128]{2,1,0:T(8,128)(2,1)S(1)} %collective-permute-done.other_b, ...), custom_call_target="tpu_custom_call" | custom-call | flops 3221225472 | bytes 12582912 | tf_op jit(solution)/shard_map/match/pallas_call | solution.py:312
  38.8 0.5 collective-permute-start.1
  39.3 8.6 %all-to-all-start.1 = ((f32[16,1,128]{2,1,0:T(1,128)}), f32[16,1,128]{2,1,0:T(1,128)S(1)}, u32[]{:S(2)}, u32[]{:S(2)}) async-start(f32[16,1,128]{2,1,0:T(1,128)} %get-tuple-element.26), calls=%async_computation.1 | async-start | bytes 16384 | tf_op jit(solution)/shard_map/all_to_all | solution.py:335
  47.9 0.0 collective-permute-done.1.other
  47.9 0.0 copy-start
  47.9 1.2 %copy-done = f32[16,128,128]{2,1,0:T(8,128)S(1)} copy-done((f32[16,128,128]{2,1,0:T(8,128)S(1)}, f32[16,128,128]{2,1,0:T(8,128)}, u32[]{:S(2)}) %copy-start) | copy-done | bytes 1048600
  49.1 0.5 scale.1
  49.6 0.9 %convert_element_type.9 = f16[16,136,128]{2,1,0:T(8,128)(2,1)} convert(f32[16,136,128]{2,1,0:T(8,128)S(1)} %get-tuple-element.25) | non-fusion elementwise | flops 278528 | bytes 1671168 | tf_op jit(solution)/shard_map/convert_element_type | solution.py:346
  50.5 4.3 %all-to-all-done.1.lost = f32[16,1,128]{2,1,0:T(1,128)S(1)} async-done(((f32[16,1,128]{2,1,0:T(1,128)}), f32[16,1,128]{2,1,0:T(1,128)S(1)}, u32[]{:S(2)}, u32[]{:S(2)}) %all-to-all-start.1) | async-done | bytes 8224 | tf_op jit(solution)/shard_map/all_to_all | solution.py:335
  54.8 0.6 broadcast_dynamic-update-slice_fusion
  55.5 10.4 %all-to-all-start.2 = ((f16[16,136,128]{2,1,0:T(8,128)(2,1)}), f16[16,136,128]{2,1,0:T(8,128)(2,1)S(1)}, u32[]{:S(2)}, u32[]{:S(2)}) async-start(f16[16,136,128]{2,1,0:T(8,128)(2,1)} %broadcast_dynamic-update-slice_fusion), calls=%async_computation.2 | async-start | bytes 1114112 | tf_op jit(solution)/shard_map/all_to_all | solution.py:359
  65.9 3.0 %grads.1 = f32[128,1024]{1,0:T(8,128)S(1)} custom-call(s32[2]{0:T(128)S(1)} %pad_add_fusion.place, bf16[16,272,128]{2,1,0:T(8,128)(2,1)S(1)} %all-to-all-done.own_b, bf16[16,272,128]{2,1,0:T(8,128)(2,1)S(1)} %collective-permute-done.other_b, bf16[4,1024,1024]{2,1,0:T(8,128)(2,1)} %get-tuple-element.31.weighted), custom_call_target="tpu_custom_call" | custom-call | flops 1073741824 | bytes 10485760 | tf_op jit(solution)/shard_map/grads/pallas_call | solution.py:360
  68.9 0.1 copy.14
  69.0 1.0 %copy.11 = f32[128,8,128]{0,1,2:T(8,128)} copy(f32[128,8,128]{2,1,0:T(8,128)S(1)} %bitcast.25) | data formatting | bytes 1048576 | tf_op jit(solution)/shard_map/reshape | solution.py:370
  70.0 6.5 %all-to-all-done.2 = f16[16,136,128]{2,1,0:T(8,128)(2,1)S(1)} async-done(((f16[16,136,128]{2,1,0:T(8,128)(2,1)}), f16[16,136,128]{2,1,0:T(8,128)(2,1)S(1)}, u32[]{:S(2)}, u32[]{:S(2)}) %all-to-all-start.2) | async-done | bytes 557088 | tf_op jit(solution)/shard_map/all_to_all | solution.py:359
  76.6 0.1 convert_element_type.11.back
  76.6 0.8 %final.1 = (f32[128,128]{1,0:T(8,128)}, f32[1,1]{1,0:T(1,128)}) custom-call(f32[16,136,128]{2,1,0:T(8,128)S(1)} %convert_element_type.11.back), custom_call_target="tpu_custom_call" | custom-call | tf_op jit(solution)/shard_map/final/pallas_call | solution.py:371
  (3 shorter events, 0.1 us)
Async XLA Ops:
  2.6 7.8 %copy-start.2 = (bf16[128,8,128]{2,1,0:T(8,128)(2,1)S(1)}, bf16[128,8,128]{2,1,0:T(8,128)(2,1)}, u32[]{:S(2)}) copy-start(bf16[128,8,128]{2,1,0:T(8,128)(2,1)} %param.7) | copy-start | bytes 786436
  2.7 8.2 %copy-start.3 = (bf16[128,8,128]{2,1,0:T(8,128)(2,1)S(1)}, bf16[128,8,128]{2,1,0:T(8,128)(2,1)}, u32[]{:S(2)}) copy-start(bf16[128,8,128]{2,1,0:T(8,128)(2,1)} %param.5) | copy-start | bytes 786436
  2.7 24.4 %all-to-all-start = ((bf16[16,272,128]{2,1,0:T(8,128)(2,1)}), bf16[16,272,128]{2,1,0:T(8,128)(2,1)S(1)}, u32[]{:S(2)}, u32[]{:S(2)}) async-start(bf16[16,272,128]{2,1,0:T(8,128)(2,1)} %block.1), calls=%async_computation | async-start | bytes 2228224 | tf_op jit(solution)/shard_map/all_to_all | solution.py:306
  10.4 21.8 %copy-start.1 = (f32[128,8]{0,1:T(8,128)S(1)}, f32[128,8]{0,1:T(8,128)}, u32[]{:S(2)}) copy-start(f32[128,8]{0,1:T(8,128)} %param.9) | copy-start | bytes 12292
  27.1 5.1 %collective-permute-start = (bf16[16,272,128]{2,1,0:T(8,128)(2,1)S(1)}, bf16[16,272,128]{2,1,0:T(8,128)(2,1)S(1)}, u32[]{:S(2)}, u32[]{:S(2)}) collective-permute-start(bf16[16,272,128]{2,1,0:T(8,128)(2,1)S(1)} %all-to-all-done.own_b), channel_id=1, source_target_pairs={{0,8},{8,0},{16,24},{24,16},{32,40},{40,32},{48,56},{56,48},{64,72... | collective-permute-start | bytes 3342344 | tf_op jit(solution)/shard_map/ppermute | solution.py:310
  38.8 9.1 %collective-permute-start.1 = (f32[16,128,128]{2,1,0:T(8,128)}, f32[16,128,128]{2,1,0:T(8,128)S(1)}, u32[]{:S(2)}, u32[]{:S(2)}) collective-permute-start(f32[16,128,128]{2,1,0:T(8,128)} %get-tuple-element.24), channel_id=1, source_target_pairs={{0,8},{8,0},{16,24},{24,16},{32,40},{40,32},{48,56},{56,48},{64,72... | collective-permute-start | bytes 3145736 | tf_op jit(solution)/shard_map/ppermute | solution.py:337
  39.3 15.5 %all-to-all-start.1 = ((f32[16,1,128]{2,1,0:T(1,128)}), f32[16,1,128]{2,1,0:T(1,128)S(1)}, u32[]{:S(2)}, u32[]{:S(2)}) async-start(f32[16,1,128]{2,1,0:T(1,128)} %get-tuple-element.26), calls=%async_computation.1 | async-start | bytes 16384 | tf_op jit(solution)/shard_map/all_to_all | solution.py:335
  47.9 1.2 %copy-start = (f32[16,128,128]{2,1,0:T(8,128)S(1)}, f32[16,128,128]{2,1,0:T(8,128)}, u32[]{:S(2)}) copy-start(f32[16,128,128]{2,1,0:T(8,128)} %get-tuple-element.23.own) | copy-start | bytes 3145732
  55.5 21.1 %all-to-all-start.2 = ((f16[16,136,128]{2,1,0:T(8,128)(2,1)}), f16[16,136,128]{2,1,0:T(8,128)(2,1)S(1)}, u32[]{:S(2)}, u32[]{:S(2)}) async-start(f16[16,136,128]{2,1,0:T(8,128)(2,1)} %broadcast_dynamic-update-slice_fusion), calls=%async_computation.2 | async-start | bytes 1114112 | tf_op jit(solution)/shard_map/all_to_all | solution.py:359
